TPU v7x, 256 devices: a whole 4x4x8 slice. The times are simulated.
256 devices in a mesh: seq: 64 (over y, z, core), head: 4 (over x).
Axes of the slice: x: 4, y: 4, z: 8, core: 2. Of those that a mesh axis runs over, the one named last changes fastest.
Arguments:
- queries: bfloat16 [32768, 4096], P('seq', 'head'), may hold values from -6 to 6
- keys: bfloat16 [32768, 4096], P('seq', 'head'), may hold values from -0.5 to 0.5
- values: bfloat16 [32768, 4096], P('seq', 'head'), may hold values from -18 to 18
- gate: bfloat16 [32768, 4096], P('seq', 'head'), may hold values from -6 to 6
- gain: float32 [4096], P('head'), may hold values from 0.5 to 2
- dout: bfloat16 [32768, 4096], P('seq', 'head'), may hold values from -6 to 6
Outputs:
- output: bfloat16 [32768, 4096], P('seq', 'head')
- dqueries: bfloat16 [32768, 4096], P('seq', 'head')
- dkeys: bfloat16 [32768, 4096], P('seq', 'head')
- dvalues: bfloat16 [32768, 4096], P('seq', 'head')
- dgate: bfloat16 [32768, 4096], P('seq', 'head')
- dgain: float32 [4096], P('head')
All inputs are finite; a program needn't handle non-finite values.
Results may differ from a plain program's by a relative error of at most 0.005.
Values sent between devices are 32-bit elements; how exact they have to be, the bound alone decides.
No kernel may reach another device: no remote copies, remote signals or barrier semaphores. Data moves between devices by JAX's collectives and lax.ppermute only.
A program may use at most 128 MiB of HBM per device.

v0:
```python
import jax
import jax.numpy as jnp
from jax import lax
from jax.sharding import PartitionSpec as P

DH = 128
BLOCK = 512


epsilon = 1e-06


def entering(part, axis, combine, identity, reverse):
    count = lax.axis_size(axis)
    place = lax.axis_index(axis)
    ahead = count - 1 - place if reverse else place
    gathered = lax.all_gather(part, axis)
    state = jnp.zeros_like(part) + jnp.asarray(identity, part.dtype)

    def one(turn, state):
        source = count - 1 - turn if reverse else turn
        return combine(state, lax.dynamic_index_in_dim(gathered, source, 0, False))

    return lax.fori_loop(0, ahead, one, state)


def add_states(earlier, later):
    return earlier + later


def body(queries, keys, values, gate, gain, dout):
    highest = lax.Precision.HIGHEST
    tokens_here, width_here = queries.shape
    heads_here = width_here // DH
    count = tokens_here // BLOCK
    shape_blk = (count, BLOCK, heads_here, DH)
    causal = jnp.tril(jnp.ones((BLOCK, BLOCK), dtype=bool))
    query_blk = queries.reshape(shape_blk)
    key_blk = keys.reshape(shape_blk)
    value_blk = values.reshape(shape_blk)
    scores = jnp.einsum("bshd,bthd->bhst", query_blk, key_blk, preferred_element_type=jnp.float32)
    attend = jnp.where(causal, scores, 0.0).astype(jnp.bfloat16)
    key_value = jnp.einsum(
        "bthd,bthe->bhde", key_blk, value_blk, preferred_element_type=jnp.float32
    )
    local_total = jnp.sum(key_value, axis=0)
    earlier_dev = entering(local_total, "seq", add_states, jnp.zeros_like(local_total), False)
    before = earlier_dev[None] + jnp.cumsum(key_value, axis=0) - key_value
    intra = jnp.einsum("bhst,bthe->bshe", attend, value_blk, preferred_element_type=jnp.float32)
    inter = jnp.einsum("bshd,bhde->bshe", query_blk.astype(jnp.float32), before, precision=highest)
    attn_out = (intra + inter).reshape(tokens_here, heads_here, DH)
    gain_hd = gain.reshape(heads_here, DH)
    sig_gate = jax.nn.sigmoid(gate.astype(jnp.float32).reshape(tokens_here, heads_here, DH))
    grad_out = dout.astype(jnp.float32).reshape(tokens_here, heads_here, DH)
    grad_normed = grad_out * sig_gate
    grad_scaled = grad_normed * gain_hd
    square_sum, product_sum = lax.psum(
        (jnp.sum(attn_out * attn_out, axis=(1, 2)), jnp.sum(grad_scaled * attn_out, axis=(1, 2))),
        "head",
    )
    features = heads_here * DH * lax.axis_size("head")
    scale_tok = lax.rsqrt(square_sum / features + epsilon)[:, None, None]
    mean_prod = (product_sum / features)[:, None, None]
    normed = attn_out * scale_tok * gain_hd
    output = (normed * sig_gate).astype(jnp.bfloat16)
    dgate = (grad_out * normed * sig_gate * (1.0 - sig_gate)).astype(jnp.bfloat16)
    gain_part = jnp.sum(grad_normed * attn_out * scale_tok, axis=0)
    grad_attn = (scale_tok * grad_scaled - attn_out * scale_tok**3 * mean_prod).astype(jnp.bfloat16)
    grad_blk = grad_attn.reshape(shape_blk)
    grad_state = jnp.einsum(
        "bshd,bshe->bhde", query_blk, grad_blk, preferred_element_type=jnp.float32
    )
    own_total = jnp.sum(grad_state, axis=0)
    later_dev = entering(own_total, "seq", add_states, jnp.zeros_like(own_total), True)
    dgain_hd = lax.psum(gain_part, "seq")
    after = later_dev[None] + own_total[None] - jnp.cumsum(grad_state, axis=0)
    back_scores = jnp.einsum(
        "bshe,bthe->bhst", grad_blk, value_blk, preferred_element_type=jnp.float32
    )
    back_attend = jnp.where(causal, back_scores, 0.0).astype(jnp.bfloat16)
    grad_query = jnp.einsum(
        "bhst,bthd->bshd", back_attend, key_blk, preferred_element_type=jnp.float32
    )
    grad_query = grad_query + jnp.einsum(
        "bshe,bhde->bshd", grad_blk.astype(jnp.float32), before, precision=highest
    )
    grad_key = jnp.einsum(
        "bhst,bshd->bthd", back_attend, query_blk, preferred_element_type=jnp.float32
    )
    grad_key = grad_key + jnp.einsum(
        "bthe,bhde->bthd", value_blk.astype(jnp.float32), after, precision=highest
    )
    grad_value = jnp.einsum("bhst,bshe->bthe", attend, grad_blk, preferred_element_type=jnp.float32)
    grad_value = grad_value + jnp.einsum(
        "bthd,bhde->bthe", key_blk.astype(jnp.float32), after, precision=highest
    )
    flat = (tokens_here, width_here)
    return (
        output.reshape(flat),
        grad_query.reshape(flat).astype(jnp.bfloat16),
        grad_key.reshape(flat).astype(jnp.bfloat16),
        grad_value.reshape(flat).astype(jnp.bfloat16),
        dgate.reshape(flat),
        dgain_hd.reshape(width_here),
    )


def solution(mesh):
    in_specs = (
        P("seq", "head"),
        P("seq", "head"),
        P("seq", "head"),
        P("seq", "head"),
        P("head"),
        P("seq", "head"),
    )
    out_specs = (
        P("seq", "head"),
        P("seq", "head"),
        P("seq", "head"),
        P("seq", "head"),
        P("seq", "head"),
        P("head"),
    )
    return jax.shard_map(body, mesh=mesh, in_specs=in_specs, out_specs=out_specs, check_vma=False)
```

profile of v0, /device:TPU:1, one launch (start us, length us, event | category | flops | bytes accessed | tf_op | source)
XLA Modules:
  0.0 506.6 jit_solution(4298086648799629868)
XLA Ops:
  7.2 2.6 copy.67
  9.8 1.6 copy.39
  11.5 1.3 fusion.22
  12.9 2.5 select_convert_fusion.1
  15.5 1.9 copy-done.3
  17.4 2.9 fusion.17
  20.3 139.4 %all-gather.5.cloned.1.call-done = f32[512,128,128]{2,1,0:T(8,128)} async-done(((f32[8,128,128]{2,1,0:T(8,128)}), f32[512,128,128]{2,1,0:T(8,128)}) %all-gather.5.cloned.1.call-update) | async-done | bytes 33554448 | tf_op jit(solution)/shard_map/all_gather | solution.py:17
  159.7 1.2 while.22
  159.7 1.2 bitcast_add_fusion.7
  161.7 3.1 fusion.5
  164.8 8.4 %psum.21 = f32[512]{0:T(512)S(1)} all-reduce(f32[512]{0:T(512)S(1)} %get-tuple-element.126), channel_id=1, replica_groups=mesh['seq'=64,'head'=4] {'head'}, use_global_device_ids=true, to_apply=%region_3.4 | all-reduce | flops 512 | bytes 4096 | tf_op jit(solution)/shard_map/psum | solution.py:57
  173.2 1.9 copy.43
  175.1 5.0 fusion.2
  180.1 2.9 copy.44
  183.0 2.8 fusion.11
  185.8 6.2 %psum.22 = f32[512]{0:T(512)S(1)} all-reduce(f32[512]{0:T(512)S(1)} %get-tuple-element.104), channel_id=1, replica_groups=mesh['seq'=64,'head'=4] {'head'}, use_global_device_ids=true, to_apply=%region_5.6 | all-reduce | flops 512 | bytes 4096 | tf_op jit(solution)/shard_map/psum | solution.py:57
  192.0 3.1 convolution_bitcast_fusion
  195.1 2.0 copy.52
  197.1 2.1 fusion.15
  199.3 1.5 select_convert_fusion
  200.9 1.5 fusion.44
  204.1 1.3 copy.57
  205.4 199.6 %psum.23 = f32[1024]{0:T(1024)} all-reduce(f32[1024]{0:T(1024)S(1)} %bitcast.162), channel_id=1, replica_groups=mesh['seq'=64,'head'=4] {'seq'}, use_global_device_ids=true, to_apply=%region_9.10 | all-reduce | flops 1024 | bytes 8192 | tf_op jit(solution)/shard_map/psum | solution.py:75
  405.0 4.4 fusion.45
  410.5 74.0 %while.23 = (s32[]{:T(128)}, f32[8,128,128]{2,1,0:T(8,128)S(1)}, s32[]{:T(128)}, f32[64,8,128,128]{3,2,1,0:T(8,128)}, s32[]{:T(128)}, /*index=5*/s32[]{:T(128)}, s32[]{:T(128)}, s32[]{:T(128)}) while((s32[]{:T(128)}, f32[8,128,128]{2,1,0:T(8,128)S(1)}, s32[]{:T(128)}, f32[64,8,128,128]{3,2,1,0:T(8,128)}, s32[]{:T(128)}, /*index=5*/s32[]{:T(128)}, ...), condition=%wide.region_7.8_spmd, body=%wide.region_6.7_spmd.sunk | while | flops 131078 | bytes 1573007 | solution.py:24
  410.5 1.3 bitcast_add_fusion.8
  423.7 1.2 bitcast_add_fusion.8
  424.9 1.2 bitcast_add_fusion.8
  426.1 1.2 bitcast_add_fusion.8
  427.3 1.2 bitcast_add_fusion.8
  428.5 1.2 bitcast_add_fusion.8
  429.7 1.2 bitcast_add_fusion.8
  430.9 1.2 bitcast_add_fusion.8
  446.3 1.2 bitcast_add_fusion.8
  447.5 1.2 bitcast_add_fusion.8
  448.7 1.2 bitcast_add_fusion.8
  449.9 1.2 bitcast_add_fusion.8
  451.1 1.2 bitcast_add_fusion.8
  452.3 1.2 bitcast_add_fusion.8
  453.5 1.2 bitcast_add_fusion.8
  469.0 1.2 bitcast_add_fusion.8
  470.2 1.2 bitcast_add_fusion.8
  471.4 1.2 bitcast_add_fusion.8
  485.5 3.5 fusion.19
  489.0 2.1 add_convert_fusion
  491.2 2.4 copy.59
  493.6 4.0 fusion.3
  497.5 2.3 copy.58
  (93 shorter events, 56.4 us)
Async XLA Ops:
  7.2 5.8 %copy-start = (bf16[512,1024]{1,0:T(8,128)(2,1)S(1)}, bf16[512,1024]{1,0:T(8,128)(2,1)}, u32[]{:S(2)}) copy-start(bf16[512,1024]{1,0:T(8,128)(2,1)} %param.10) | copy-start | bytes 3145732
  7.2 152.5 %all-gather.5.cloned.1.call-start = ((), (), s32[]{:S(2)}) async-start(), calls=%async_computation | async-start | bytes 34078720 | tf_op jit(solution)/shard_map/all_gather | solution.py:17
  7.2 4.3 copy-start.9
  11.5 4.0 copy-start.7
  12.8 397.6 %all-gather.7.cloned.1.call-start = ((), (), s32[]{:S(2)}) async-start(), calls=%async_computation.1 | async-start | bytes 34078720 | tf_op jit(solution)/shard_map/all_gather | solution.py:17
  15.5 2.0 copy-start.3
  160.9 0.8 copy-start.1
  173.2 1.9 copy-start.18
  197.1 2.1 copy-start.10
  199.2 3.1 copy-start.5
  199.2 1.6 copy-start.8
  200.9 2.1 copy-start.4
  200.9 2.1 copy-start.2
  200.9 2.1 copy-start.12
  204.1 201.0 %copy-start.6 = (bf16[512,8,128]{0,2,1:T(8,128)(2,1)S(1)}, bf16[512,8,128]{0,2,1:T(8,128)(2,1)}, u32[]{:S(2)}) copy-start(bf16[512,8,128]{0,2,1:T(8,128)(2,1)} %copy-done.5) | copy-start | bytes 3145732
  410.4 75.0 %copy-start.11 = (bf16[512,1024]{1,0:T(8,128)(2,1)S(1)}, bf16[512,1024]{1,0:T(8,128)(2,1)}, u32[]{:S(2)}) copy-start(bf16[512,1024]{1,0:T(8,128)(2,1)} %param.12) | copy-start | bytes 3145732
  410.5 75.0 %copy-start.15 = (f32[8,128,128]{1,2,0:T(8,128)S(1)}, f32[8,128,128]{1,2,0:T(8,128)}, u32[]{:S(2)}) copy-start(f32[8,128,128]{1,2,0:T(8,128)} %convolution_bitcast_fusion) | copy-start | bytes 1572868
  485.5 3.6 copy-start.13
  485.5 3.6 copy-start.16
  485.5 3.6 copy-start.17
  491.2 2.4 copy-start.14
Sparse Core Ops, SparseCore 0:
  12.9 146.7 all-gather.4
  197.2 213.1 all-gather.6
where the time goes:
time: 512 us; the launch traced here: 507 us
  blocking collectives  214 us (42%)
  waiting for transfers between devices  140 us (27%)
  other arithmetic  83.7 us (16%)
  matrix products  30.9 us (6%)
  local copies, waits for them, and re-layouts  21.6 us (4%)
  between operations  14.3 us (3%)
    psum x1, blocking collectives, body(): dgain_hd = lax.psum(gain_part, 'seq')  200 us
    all_gather x2, waiting for transfers between devices, entering(): gathered = lax.all_gather(part, axis)  140 us
    add x63, other arithmetic, add_states(): return earlier + later  73.8 us
    psum x2, blocking collectives, body(): lax.psum((jnp.sum(attn_out * attn_out, axis=(1, 2)), jnp.sum(grad_scaled...  14.6 us
    unnamed x42, local copies, waits for them, and re-layouts  12.1 us
  transfers between devices with their start and end apart: 2, of which 2 were waited for; matrix products, arithmetic and copies ran while one was open for 3% of the time, Pallas kernels for 0%

commit v1 on v0

v1 whole, which is shorter than its diff:
```python
import functools
import jax
import jax.numpy as jnp
from jax import lax
from jax.experimental import pallas as pl
from jax.experimental.pallas import tpu as pltpu
from jax.sharding import PartitionSpec as P

DH = 128
BLOCK = 512
HALF = BLOCK // 2
HEADS_HERE = 8
OWNED = HEADS_HERE // 2
FEATURES = 4096
CHIPS = 32
PIECE = OWNED * DH // CHIPS
EXTRA = 8
EPSILON = 1e-06

F32 = jnp.float32
BF16 = jnp.bfloat16
VMEM_LIMIT = 24 * 1024 * 1024


def dot_nn(a, b):
    return lax.dot_general(a, b, (((1,), (0,)), ((), ())), preferred_element_type=F32)


def dot_nt(a, b):
    return lax.dot_general(a, b, (((1,), (1,)), ((), ())), preferred_element_type=F32)


def dot_tn(a, b):
    return lax.dot_general(a, b, (((0,), (0,)), ((), ())), preferred_element_type=F32)


def split_state(state):
    high = state.astype(BF16)
    return high, (state - high.astype(F32)).astype(BF16)


def times_state(a, state):
    high, low = split_state(state)
    return dot_nn(jnp.concatenate([a, a], axis=1), jnp.concatenate([high, low], axis=0))


def times_state_t(a, state):
    high, low = split_state(state)
    return dot_nt(jnp.concatenate([a, a], axis=1), jnp.concatenate([high, low], axis=1))


def masked(scores, lower):
    row = lax.broadcasted_iota(jnp.int32, scores.shape, 0)
    column = lax.broadcasted_iota(jnp.int32, scores.shape, 1)
    keep = (row >= column) if lower else (row <= column)
    return jnp.where(keep, scores, 0.0).astype(BF16)


def causal_product(a, b, values):
    top = masked(dot_nt(a[:HALF], b[:HALF]), True)
    left = dot_nt(a[HALF:], b[:HALF]).astype(BF16)
    right = masked(dot_nt(a[HALF:], b[HALF:]), True)
    first = dot_nn(top, values[:HALF])
    second = dot_nn(jnp.concatenate([left, right], axis=1), values)
    return first, second


def anticausal_product(a, b, values):
    left = masked(dot_nt(a[:HALF], b[:HALF]), False)
    right = dot_nt(a[:HALF], b[HALF:]).astype(BF16)
    bottom = masked(dot_nt(a[HALF:], b[HALF:]), False)
    first = dot_nn(jnp.concatenate([left, right], axis=1), values)
    second = dot_nn(bottom, values[HALF:])
    return first, second


def params():
    return pltpu.CompilerParams(vmem_limit_bytes=VMEM_LIMIT)


def shape(dims, dtype=F32):
    return jax.ShapeDtypeStruct(dims, dtype)


def head_of(step, core):
    return jnp.where(step < OWNED, OWNED * (1 - core[0]) + step, OWNED * core[0] + step - OWNED)


def column_spec():
    return pl.BlockSpec((BLOCK, DH), lambda i, core: (0, head_of(i, core)))


def theirs_spec(rows):
    return pl.BlockSpec((1, rows, DH), lambda i, core: (jnp.minimum(i, OWNED - 1), 0, 0))


def mine_spec(rows):
    return pl.BlockSpec((1, rows, DH), lambda i, core: (jnp.maximum(i - OWNED, 0), 0, 0))


def state_kernel(core, key, value, theirs, mine):
    step = pl.program_id(0)
    state = dot_tn(key[...], value[...])

    @pl.when(step < OWNED)
    def _():
        theirs[0] = state

    @pl.when(step >= OWNED)
    def _():
        mine[0] = state


def own_states(core, keys, values):
    return pl.pallas_call(
        state_kernel,
        grid_spec=pltpu.PrefetchScalarGridSpec(
            num_scalar_prefetch=1,
            grid=(HEADS_HERE,),
            in_specs=[column_spec(), column_spec()],
            out_specs=[theirs_spec(DH), mine_spec(DH)],
        ),
        out_shape=[shape((OWNED, DH, DH))] * 2,
        compiler_params=params(),
        name="own_states",
    )(core, keys, values)


def intra_kernel(query, key, value, gate, dout, intra, grad_normed):
    first, second = causal_product(query[...], key[...], value[...])
    intra[:HALF] = first
    intra[HALF:] = second
    grad_normed[...] = dout[...].astype(F32) * jax.nn.sigmoid(gate[...].astype(F32))


def plain_column():
    return pl.BlockSpec((BLOCK, DH), lambda i: (0, i))


def intra_part(queries, keys, values, gate, dout):
    wide = (BLOCK, HEADS_HERE * DH)
    return pl.pallas_call(
        intra_kernel,
        grid=(HEADS_HERE,),
        in_specs=[plain_column()] * 5,
        out_specs=[plain_column()] * 2,
        out_shape=[shape(wide), shape(wide)],
        compiler_params=params(),
        name="intra",
    )(queries, keys, values, gate, dout)


def select_state(core, step, own, other):
    return jnp.where(step // OWNED == core[0], own[0, :DH], other[0, :DH])


def attend_kernel(core, query, intra, grad_normed, gain, own, other, attn_out, sums, squares, products):
    step = pl.program_id(0)
    state = select_state(core, step, own, other)
    out = intra[...] + times_state(query[...], state)
    attn_out[...] = out
    square = out * out
    product = out * (grad_normed[...] * gain[...])

    @pl.when(step == 0)
    def _():
        squares[...] = square
        products[...] = product

    @pl.when(step > 0)
    def _():
        squares[...] += square
        products[...] += product

    @pl.when(step == HEADS_HERE - 1)
    def _():
        for which, acc in enumerate((squares, products)):
            for part in range(BLOCK // DH):
                turned = acc[part * DH:(part + 1) * DH, :].T
                place = which * (BLOCK // DH) + part
                sums[place:place + 1, :] = jnp.sum(turned, axis=0, keepdims=True)


def core_column():
    return pl.BlockSpec((BLOCK, DH), lambda i, core: (0, i))


def core_state(rows):
    return pl.BlockSpec((1, rows, DH), lambda i, core: (lax.rem(i, OWNED), 0, 0))


def gain_spec():
    return pl.BlockSpec((1, DH), lambda i, core: (0, i))


def attend(core, queries, intra, grad_normed, gain, own, other):
    return pl.pallas_call(
        attend_kernel,
        grid_spec=pltpu.PrefetchScalarGridSpec(
            num_scalar_prefetch=1,
            grid=(HEADS_HERE,),
            in_specs=[core_column()] * 3 + [gain_spec()] + [core_state(DH)] * 2,
            out_specs=[core_column(), pl.BlockSpec((8, DH), lambda i, core: (0, 0))],
            scratch_shapes=[pltpu.VMEM((BLOCK, DH), F32)] * 2,
        ),
        out_shape=[shape((BLOCK, HEADS_HERE * DH)), shape((8, DH))],
        compiler_params=params(),
        name="attend",
    )(core, queries, intra, grad_normed, gain, own, other)


def grad_kernel(core, sums, query, attn_out, grad_normed, gain, grad, scale, theirs, mine, cubes):
    step = pl.program_id(0)

    @pl.when(step == 0)
    def _():
        for part in range(BLOCK // DH):
            rows = slice(part * DH, (part + 1) * DH)
            mean_square = sums[part:part + 1, :] / FEATURES
            mean_prod = sums[part + 4:part + 5, :] / FEATURES
            one = lax.rsqrt(mean_square + EPSILON)
            scale[rows, :] = jnp.broadcast_to(one, (DH, DH)).T
            cubes[rows, :] = jnp.broadcast_to(one * one * one * mean_prod, (DH, DH)).T

    out = attn_out[...]
    rate = scale[...]
    normed = grad_normed[...]
    here = (rate * (normed * gain[...]) - out * cubes[...]).astype(BF16)
    grad[...] = here
    state = dot_tn(query[...], here)
    gain_row = jnp.sum(normed * out * rate, axis=0, keepdims=True)
    extra = jnp.broadcast_to(gain_row, (EXTRA, DH))

    @pl.when(step < OWNED)
    def _():
        theirs[0, :DH] = state
        theirs[0, DH:] = extra

    @pl.when(step >= OWNED)
    def _():
        mine[0, :DH] = state
        mine[0, DH:] = extra


def token_grads(core, sums, queries, attn_out, grad_normed, gain):
    whole = pl.BlockSpec((8, DH), lambda i, core: (0, 0))
    gain_col = pl.BlockSpec((1, DH), lambda i, core: (0, head_of(i, core)))
    return pl.pallas_call(
        grad_kernel,
        grid_spec=pltpu.PrefetchScalarGridSpec(
            num_scalar_prefetch=1,
            grid=(HEADS_HERE,),
            in_specs=[whole] + [column_spec()] * 3 + [gain_col],
            out_specs=[
                column_spec(),
                pl.BlockSpec((BLOCK, DH), lambda i, core: (0, 0)),
                theirs_spec(DH + EXTRA),
                mine_spec(DH + EXTRA),
            ],
            scratch_shapes=[pltpu.VMEM((BLOCK, DH), F32)],
        ),
        out_shape=[
            shape((BLOCK, HEADS_HERE * DH), BF16),
            shape((BLOCK, DH)),
            shape((OWNED, DH + EXTRA, DH)),
            shape((OWNED, DH + EXTRA, DH)),
        ],
        compiler_params=params(),
        name="token_grads",
    )(core, sums, queries, attn_out, grad_normed, gain)


def local_kernel(core, query, key, value, gate, dout, attn_out, scale, gain, grad, own, other,
                 output, dgate, grad_query, grad_key, grad_value):
    step = pl.program_id(0)
    state = select_state(core, step, own, other)
    sig = jax.nn.sigmoid(gate[...].astype(F32))
    normed = attn_out[...] * scale[...] * gain[...]
    result = normed * sig
    output[...] = result.astype(BF16)
    dgate[...] = (dout[...].astype(F32) * result * (1.0 - sig)).astype(BF16)
    query_here, key_here, value_here, grad_here = query[...], key[...], value[...], grad[...]
    inter = times_state_t(grad_here, state)
    first, second = causal_product(grad_here, value_here, key_here)
    grad_query[:HALF] = (first + inter[:HALF]).astype(BF16)
    grad_query[HALF:] = (second + inter[HALF:]).astype(BF16)
    first, second = anticausal_product(value_here, grad_here, query_here)
    grad_key[:HALF] = first
    grad_key[HALF:] = second
    first, second = anticausal_product(key_here, query_here, grad_here)
    grad_value[:HALF] = first
    grad_value[HALF:] = second


def local_grads(core, queries, keys, values, gate, dout, attn_out, scale, gain, grad, own, other):
    wide = (BLOCK, HEADS_HERE * DH)
    return pl.pallas_call(
        local_kernel,
        grid_spec=pltpu.PrefetchScalarGridSpec(
            num_scalar_prefetch=1,
            grid=(HEADS_HERE,),
            in_specs=[core_column()] * 6
            + [pl.BlockSpec((BLOCK, DH), lambda i, core: (0, 0)), gain_spec(), core_column()]
            + [core_state(DH)] * 2,
            out_specs=[core_column()] * 5,
        ),
        out_shape=[shape(wide, BF16)] * 3 + [shape(wide)] * 2,
        compiler_params=params(),
        name="local_grads",
    )(core, queries, keys, values, gate, dout, attn_out, scale, gain, grad, own, other)


def last_kernel(core, key, value, part_key, part_value, own, other, grad_key, grad_value, dgain):
    step = pl.program_id(0)
    here = step // OWNED == core[0]
    state = jnp.where(here, own[0, :DH], other[0, :DH])
    dgain[pl.ds(step, 1), :] = jnp.where(here, own[0, DH:DH + 1], other[0, DH:DH + 1])
    grad_key[...] = (part_key[...] + times_state_t(value[...], state)).astype(BF16)
    grad_value[...] = (part_value[...] + times_state(key[...], state)).astype(BF16)


def last_grads(core, keys, values, part_key, part_value, own, other):
    wide = (BLOCK, HEADS_HERE * DH)
    return pl.pallas_call(
        last_kernel,
        grid_spec=pltpu.PrefetchScalarGridSpec(
            num_scalar_prefetch=1,
            grid=(HEADS_HERE,),
            in_specs=[core_column()] * 4 + [core_state(DH + EXTRA)] * 2,
            out_specs=[core_column()] * 2
            + [pl.BlockSpec((HEADS_HERE, DH), lambda i, core: (0, 0))],
        ),
        out_shape=[shape(wide, BF16)] * 2 + [shape((HEADS_HERE, DH))],
        compiler_params=params(),
        name="last_grads",
    )(core, keys, values, part_key, part_value, own, other)


def pack_kernel(mine, received, pieces):
    extra = pieces.shape[1] - PIECE
    for head in range(OWNED):
        for part in range(DH // PIECE):
            rows = slice(part * PIECE, (part + 1) * PIECE)
            place = head * (DH // PIECE) + part
            pieces[place, :PIECE] = mine[head, rows] + received[head, rows]
            if extra:
                pieces[place, PIECE:] = mine[head, DH:] + received[head, DH:]


def prefix_kernel(reverse, pieces, sums):
    extra = pieces.shape[1] - PIECE
    total = jnp.zeros((PIECE, DH), F32)
    order = range(CHIPS - 1, -1, -1) if reverse else range(CHIPS)
    for chip in order:
        sums[chip, :PIECE] = total
        total = total + pieces[chip, :PIECE]
    if extra:
        whole = pieces[0, PIECE:]
        for chip in range(1, CHIPS):
            whole = whole + pieces[chip, PIECE:]
        for chip in range(CHIPS):
            sums[chip, PIECE:] = whole


def unpack_kernel(reverse, core, back, mine, received, own, send):
    extra = back.shape[1] - PIECE
    ahead = core[0] == (1 if reverse else 0)
    for head in range(OWNED):
        for part in range(DH // PIECE):
            rows = slice(part * PIECE, (part + 1) * PIECE)
            state = back[head * (DH // PIECE) + part, :PIECE]
            own[head, rows] = state + jnp.where(ahead, 0.0, received[head, rows])
            send[head, rows] = state + jnp.where(ahead, mine[head, rows], 0.0)
        if extra:
            whole = back[head * (DH // PIECE), PIECE:]
            own[head, DH:] = whole
            send[head, DH:] = whole


def vmem():
    return pl.BlockSpec(memory_space=pltpu.VMEM)


def sums_beyond(core, mine, theirs, seq_size, reverse):
    cores = [(i, i ^ 1) for i in range(seq_size)]
    groups = [[2 * i + one for i in range(seq_size // 2)] for one in range(2)]
    extra = mine.shape[1] - DH
    piece = (CHIPS, PIECE + extra, DH)
    received = lax.ppermute(theirs, "seq", cores)
    if extra:
        pieces = pl.pallas_call(
            pack_kernel,
            in_specs=[vmem()] * 2,
            out_specs=vmem(),
            out_shape=shape(piece),
            compiler_params=params(),
            name="pack",
        )(mine, received)
    else:
        pieces = (mine + received).reshape(piece)
    gathered = lax.all_to_all(pieces, "seq", 0, 0, axis_index_groups=groups)
    sums = pl.pallas_call(
        functools.partial(prefix_kernel, reverse),
        in_specs=[vmem()],
        out_specs=vmem(),
        out_shape=shape(piece),
        compiler_params=params(),
        name="prefix",
    )(gathered)
    back = lax.all_to_all(sums, "seq", 0, 0, axis_index_groups=groups)
    own, send = pl.pallas_call(
        functools.partial(unpack_kernel, reverse),
        in_specs=[pl.BlockSpec(memory_space=pltpu.SMEM)] + [vmem()] * 3,
        out_specs=[vmem()] * 2,
        out_shape=[shape(mine.shape)] * 2,
        compiler_params=params(),
        name="unpack",
    )(core, back, mine, received)
    return own, lax.ppermute(send, "seq", cores)


def body(queries, keys, values, gate, gain, dout):
    seq_size = lax.axis_size("seq")
    core = lax.rem(lax.axis_index("seq"), 2).astype(jnp.int32).reshape(1)
    gain_row = gain.reshape(1, HEADS_HERE * DH)
    theirs, mine = own_states(core, keys, values)
    own, other = sums_beyond(core, mine, theirs, seq_size, False)
    intra, grad_normed = intra_part(queries, keys, values, gate, dout)
    attn_out, sums = attend(core, queries, intra, grad_normed, gain_row, own, other)
    sums = lax.psum(sums, "head")
    grad, scale, theirs, mine = token_grads(core, sums, queries, attn_out, grad_normed, gain_row)
    output, dgate, grad_query, part_key, part_value = local_grads(
        core, queries, keys, values, gate, dout, attn_out, scale, gain_row, grad, own, other
    )
    own, other = sums_beyond(core, mine, theirs, seq_size, True)
    grad_key, grad_value, dgain = last_grads(core, keys, values, part_key, part_value, own, other)
    return output, grad_query, grad_key, grad_value, dgate, dgain.reshape(HEADS_HERE * DH)


def solution(mesh):
    wide = P("seq", "head")
    return jax.shard_map(
        body,
        mesh=mesh,
        in_specs=(wide, wide, wide, wide, P("head"), wide),
        out_specs=(wide, wide, wide, wide, wide, P("head")),
        check_vma=False,
    )
```

time: 512 us -> 135 us (0.26)
  waiting for transfers between devices: 140 us -> 2.35 us
  blocking collectives: 214 us -> 77.8 us
  other arithmetic: 83.7 us -> 0.03 us
  Pallas kernels: 0 us -> 32.5 us
  matrix products: 30.9 us -> 0 us
  local copies, waits for them, and re-layouts: 21.6 us -> 7.01 us
  starting transfers between devices: 0.08 us -> 13.9 us
  between operations: 14.3 us -> 0.81 us
    psum x3 -> x1, blocking collectives: 214 us -> 8.42 us  [body(): sums = lax.psum(sums, 'head')]
    all_gather x2 -> x0, waiting for transfers between devices: 140 us -> none  [entering(): gathered = lax.all_gather(part, axis)]
    add x63 -> x1, other arithmetic: 73.8 us -> 0.03 us  [sums_beyond(): pieces = (mine + received).reshape(piece)]
    all_to_all x0 -> x4, blocking collectives: none -> 69.4 us  [the longest x2 35.1 us: sums_beyond(): gathered = lax.all_to_all(pieces, 'seq', 0, 0, axis_index_groups=groups)]
    pallas_call x0 -> x11, Pallas kernels: none -> 32.5 us  [the longest x1 11.8 us: local_grads(): pl.pallas_call(local_kernel, grid_spec=pltpu.PrefetchScalarGridSpec(num_s...]
    dot_general x12 -> x0, matrix products: 30.9 us -> none  [the longest x1 4.37 us: body(): jnp.einsum('bhst,bshe->bthe', attend, grad_blk, preferred_element_type=jn...]
    ppermute x0 -> x4, starting transfers between devices: none -> 13.9 us  [the longest x2 8.39 us: sums_beyond(): return (own, lax.ppermute(send, 'seq', cores))]
    unnamed x42 -> x34, local copies, waits for them, and re-layouts: 12.1 us -> 7.01 us
  transfers between devices with their start and end apart: 2 -> 4, of which waited for: 2 -> 2; matrix products, arithmetic and copies ran while one was open for 3% -> 0% of each run, Pallas kernels for 0% -> 13%
where the time goes in v1:
time: 135 us; the launch traced here: 134 us
  blocking collectives  77.8 us (58%)
  Pallas kernels  32.5 us (24%)
  starting transfers between devices  13.9 us (10%)
  local copies, waits for them, and re-layouts  7.01 us (5%)
  waiting for transfers between devices  2.35 us (2%)
    all_to_all x2, blocking collectives, sums_beyond(): gathered = lax.all_to_all(pieces, 'seq', 0, 0, axis_index_groups=groups)  35.1 us
    all_to_all x2, blocking collectives, sums_beyond(): back = lax.all_to_all(sums, 'seq', 0, 0, axis_index_groups=groups)  34.3 us
    pallas_call x1, Pallas kernels, local_grads(): pl.pallas_call(local_kernel, grid_spec=pltpu.PrefetchScalarGridSpec(num_s...  11.8 us
    psum x1, blocking collectives, body(): sums = lax.psum(sums, 'head')  8.42 us
    ppermute x2, starting transfers between devices, sums_beyond(): return (own, lax.ppermute(send, 'seq', cores))  8.39 us
    unnamed x34, local copies, waits for them, and re-layouts  7.01 us
    ppermute x2, starting transfers between devices, sums_beyond(): received = lax.ppermute(theirs, 'seq', cores)  5.48 us
    pallas_call x1, Pallas kernels, intra_part(): pl.pallas_call(intra_kernel, grid=(HEADS_HERE,), in_specs=[plain_column()...  5.24 us
  transfers between devices with their start and end apart: 4, of which 2 were waited for; matrix products, arithmetic and copies ran while one was open for 0% of the time, Pallas kernels for 13%

profile of v1, /device:TPU:1, one launch (start us, length us, event | category | flops | bytes accessed | tf_op | source)
XLA Modules:
  0.0 134.4 jit_solution(6561233426199382815)
XLA Ops:
  0.6 0.0 copy-start
  0.6 1.2 copy-done
  1.9 0.0 copy-start.2
  1.9 1.2 copy-done.2
  3.1 0.0 copy-start.10
  3.1 2.6 %own_states.1 = (f32[4,128,128]{2,1,0:T(8,128)S(1)}, f32[4,128,128]{2,1,0:T(8,128)S(1)}) custom-call(s32[1]{0:T(128)} %bitcast.core, bf16[512,1024]{1,0:T(8,128)(2,1)S(1)} %copy-done, bf16[512,1024]{1,0:T(8,128)(2,1)S(1)} %copy-done.2), custom_call_target="tpu_custom_call" | custom-call | tf_op jit(solution)/shard_map/own_states/pallas_call | solution.py:115
  5.8 0.0 copy-start.1
  5.8 0.0 copy-start.3
  5.8 0.0 copy-start.4
  5.8 3.3 %collective-permute-start = (f32[4,128,128]{2,1,0:T(8,128)S(1)}, f32[4,128,128]{2,1,0:T(8,128)S(1)}, u32[]{:S(2)}, u32[]{:S(2)}) collective-permute-start(f32[4,128,128]{2,1,0:T(8,128)S(1)} %get-tuple-element.31), channel_id=1, source_target_pairs={{0,4},{4,0},{8,12},{12,8},{16,20},{20,16},{24,28},{28,24},{32,36},... | collective-permute-start | bytes 786440 | tf_op jit(solution)/shard_map/ppermute | solution.py:389
  9.1 1.2 collective-permute-done.received
  10.3 18.9 %all_to_all.20.pieces = f32[32,16,128]{2,1,0:T(8,128)S(1)} all-to-all(f32[32,16,128]{2,1,0:T(8,128)S(1)} %bitcast.7), channel_id=1, replica_groups={{0,8,16,24,32,40,48,56,64,72,80,88,96,104,112,120,128,136,144,152,160,1..., dimensions={0} | all-to-all | bytes 524288 | tf_op jit(solution)/shard_map/all_to_all | solution.py:401
  29.3 16.2 %all_to_all.21.back = f32[32,16,128]{2,1,0:T(8,128)S(1)} all-to-all(f32[32,16,128]{2,1,0:T(8,128)S(1)} %prefix.2), channel_id=1, replica_groups={{0,8,16,24,32,40,48,56,64,72,80,88,96,104,112,120,128,136,144,152,160,1..., dimensions={0} | all-to-all | bytes 524288 | tf_op jit(solution)/shard_map/all_to_all | solution.py:410
  45.5 0.1 unpack.2
  45.5 0.0 copy-start.16
  45.5 3.7 %collective-permute-start.1 = (f32[4,128,128]{2,1,0:T(8,128)S(1)}, f32[4,128,128]{2,1,0:T(8,128)S(1)}, u32[]{:S(2)}, u32[]{:S(2)}) collective-permute-start(f32[4,128,128]{2,1,0:T(8,128)S(1)} %get-tuple-element.33), channel_id=1, source_target_pairs={{0,4},{4,0},{8,12},{12,8},{16,20},{20,16},{24,28},{28,24},{32,36},... | collective-permute-start | bytes 786440 | tf_op jit(solution)/shard_map/ppermute | solution.py:419
  49.2 0.0 copy-done.10
  49.2 0.0 copy-done.12
  49.2 0.0 copy-done.1
  49.2 0.0 copy-done.3
  49.2 0.0 copy-done.4
  49.2 5.2 %intra.1 = (f32[512,1024]{1,0:T(8,128)S(1)}, f32[512,1024]{1,0:T(8,128)S(1)}) custom-call(bf16[512,1024]{1,0:T(8,128)(2,1)S(1)} %copy-done.4, bf16[512,1024]{1,0:T(8,128)(2,1)S(1)} %copy-done.1, bf16[512,1024]{1,0:T(8,128)(2,1)S(1)} %copy-done.3, bf16[512,1024]{1,0:T(8,128)(2,1)S(1)} %copy-done.10, bf16[512,1024]{1,0:T(8,128)(2,1)S(1)} %copy-done.12), custom_call_target="tpu_custom_call" | custom-call | tf_op jit(solution)/shard_map/intra/pallas_call | solution.py:142
  54.5 0.0 copy-start.8
  54.5 0.0 collective-permute-done.1.other
  54.5 0.0 copy-start.14
  54.5 0.0 copy-done.16
  54.5 3.7 %attend.1 = (f32[512,1024]{1,0:T(8,128)S(1)}, f32[8,128]{1,0:T(8,128)S(1)}) custom-call(s32[1]{0:T(128)} %bitcast.core, bf16[512,1024]{1,0:T(8,128)(2,1)S(1)} %copy-done.4, f32[512,1024]{1,0:T(8,128)S(1)} %get-tuple-element.28.intra, f32[512,1024]{1,0:T(8,128)S(1)} %get-tuple-element.29.grad_normed, f32[1,1024]{1,0:T(1,128)S(1)} %bitcast.4, ...), custom_call_target="tpu_custom_call" | custom-call | tf_op jit(solution)/shard_map/attend/pallas_call | solution.py:197
  58.2 0.0 copy-done.8
  58.2 0.0 copy-done.14
  58.3 0.0 copy-start.5
  58.3 1.3 copy-done.5
  59.6 8.4 %psum.7.sums = f32[8,128]{1,0:T(8,128)S(1)} all-reduce(f32[8,128]{1,0:T(8,128)S(1)} %get-tuple-element.35), channel_id=1, replica_groups=mesh['seq'=64,'head'=4] {'head'}, use_global_device_ids=true, to_apply=%region_0.0 | all-reduce | flops 1024 | bytes 8192 | tf_op jit(solution)/shard_map/psum | solution.py:430
  68.0 1.6 %copy-done.6 = f32[512,1024]{1,0:T(8,128)S(1)} copy-done((f32[512,1024]{1,0:T(8,128)S(1)}, f32[512,1024]{1,0:T(8,128)}, u32[]{:S(2)}) %copy-start.6) | copy-done | bytes 2097176
  69.6 1.6 %copy-done.9 = f32[512,1024]{1,0:T(8,128)S(1)} copy-done((f32[512,1024]{1,0:T(8,128)S(1)}, f32[512,1024]{1,0:T(8,128)}, u32[]{:S(2)}) %copy-start.9) | copy-done | bytes 2097176
  71.2 3.7 %token_grads.1 = (bf16[512,1024]{1,0:T(8,128)(2,1)S(1)}, f32[512,128]{1,0:T(8,128)S(1)}, f32[4,136,128]{2,1,0:T(8,128)S(1)}, f32[4,136,128]{2,1,0:T(8,128)S(1)}) custom-call(s32[1]{0:T(128)} %bitcast.core, f32[8,128]{1,0:T(8,128)S(1)} %psum.7.sums, bf16[512,1024]{1,0:T(8,128)(2,1)S(1)} %copy-done.4, f32[512,1024]{1,0:T(8,128)S(1)} %copy-done.6, ...), custom_call_target="tpu_custom_call" | custom-call | tf_op jit(solution)/shard_map/token_grads/pallas_call | solution.py:248
  74.9 2.2 %collective-permute-start.2 = (f32[4,136,128]{2,1,0:T(8,128)S(1)}, f32[4,136,128]{2,1,0:T(8,128)S(1)}, u32[]{:S(2)}, u32[]{:S(2)}) collective-permute-start(f32[4,136,128]{2,1,0:T(8,128)S(1)} %get-tuple-element.43), channel_id=1, source_target_pairs={{0,4},{4,0},{8,12},{12,8},{16,20},{20,16},{24,28},{28,24},{32,36},... | collective-permute-start | bytes 835592 | tf_op jit(solution)/shard_map/ppermute | solution.py:389
  77.0 1.2 collective-permute-done.2.received
  78.3 16.1 %all_to_all.22.pieces = f32[32,24,128]{2,1,0:T(8,128)S(1)} all-to-all(f32[32,24,128]{2,1,0:T(8,128)S(1)} %pack.1), channel_id=1, replica_groups={{0,8,16,24,32,40,48,56,64,72,80,88,96,104,112,120,128,136,144,152,160,1..., dimensions={0} | all-to-all | bytes 786432 | tf_op jit(solution)/shard_map/all_to_all | solution.py:401
  94.4 18.2 %all_to_all.23.back = f32[32,24,128]{2,1,0:T(8,128)S(1)} all-to-all(f32[32,24,128]{2,1,0:T(8,128)S(1)} %prefix.3), channel_id=1, replica_groups={{0,8,16,24,32,40,48,56,64,72,80,88,96,104,112,120,128,136,144,152,160,1..., dimensions={0} | all-to-all | bytes 786432 | tf_op jit(solution)/shard_map/all_to_all | solution.py:410
  112.6 0.1 unpack.3
  112.7 4.7 %collective-permute-start.3 = (f32[4,136,128]{2,1,0:T(8,128)S(1)}, f32[4,136,128]{2,1,0:T(8,128)S(1)}, u32[]{:S(2)}, u32[]{:S(2)}) collective-permute-start(f32[4,136,128]{2,1,0:T(8,128)S(1)} %get-tuple-element.45), channel_id=1, source_target_pairs={{0,4},{4,0},{8,12},{12,8},{16,20},{20,16},{24,28},{28,24},{32,36},... | collective-permute-start | bytes 835592 | tf_op jit(solution)/shard_map/ppermute | solution.py:419
  117.4 0.0 copy-done.15
  117.4 0.0 copy-done.7
  117.4 0.0 copy-done.11
  117.4 0.0 copy-done.13
  117.4 11.8 %local_grads.1 = (bf16[512,1024]{1,0:T(8,128)(2,1)}, bf16[512,1024]{1,0:T(8,128)(2,1)}, bf16[512,1024]{1,0:T(8,128)(2,1)}, f32[512,1024]{1,0:T(8,128)S(1)}, f32[512,1024]{1,0:T(8,128)S(1)}) custom-call(s32[1]{0:T(128)} %bitcast.core, bf16[512,1024]{1,0:T(8,128)(2,1)S(1)} %copy-done.4, bf16[512,1024]{1,0:T(8,128)(2,1)S(1)} %copy-done.1, ...), custom_call_target="tpu_custom_call" | custom-call | tf_op jit(solution)/shard_map/local_grads/pallas_call | solution.py:297
  129.2 0.0 collective-permute-done.3.other
  129.3 5.1 %last_grads.1 = (bf16[512,1024]{1,0:T(8,128)(2,1)}, bf16[512,1024]{1,0:T(8,128)(2,1)}, f32[8,128]{1,0:T(8,128)}) custom-call(s32[1]{0:T(128)} %bitcast.core, bf16[512,1024]{1,0:T(8,128)(2,1)S(1)} %copy-done.1, bf16[512,1024]{1,0:T(8,128)(2,1)S(1)} %copy-done.3, f32[512,1024]{1,0:T(8,128)S(1)} %get-tuple-element.40.part_key, ...), custom_call_target="tpu_custom_call" | custom-call | tf_op jit(solution)/shard_map/last_grads/pallas_call | solution.py:324
  (11 shorter events, 0.2 us)
Async XLA Ops:
  0.6 1.2 copy-start
  1.9 1.2 copy-start.2
  3.1 46.1 %copy-start.10 = (bf16[512,1024]{1,0:T(8,128)(2,1)S(1)}, bf16[512,1024]{1,0:T(8,128)(2,1)}, u32[]{:S(2)}) copy-start(bf16[512,1024]{1,0:T(8,128)(2,1)} %gate.3) | copy-start | bytes 3145732
  3.1 46.1 %copy-start.12 = (bf16[512,1024]{1,0:T(8,128)(2,1)S(1)}, bf16[512,1024]{1,0:T(8,128)(2,1)}, u32[]{:S(2)}) copy-start(bf16[512,1024]{1,0:T(8,128)(2,1)} %dout.3) | copy-start | bytes 3145732
  5.8 43.5 %copy-start.1 = (bf16[512,1024]{1,0:T(8,128)(2,1)S(1)}, bf16[512,1024]{1,0:T(8,128)(2,1)}, u32[]{:S(2)}) copy-start(bf16[512,1024]{1,0:T(8,128)(2,1)} %key.7) | copy-start | bytes 3145732
  5.8 43.5 %copy-start.3 = (bf16[512,1024]{1,0:T(8,128)(2,1)S(1)}, bf16[512,1024]{1,0:T(8,128)(2,1)}, u32[]{:S(2)}) copy-start(bf16[512,1024]{1,0:T(8,128)(2,1)} %value.7) | copy-start | bytes 3145732
  5.8 43.5 %copy-start.4 = (bf16[512,1024]{1,0:T(8,128)(2,1)S(1)}, bf16[512,1024]{1,0:T(8,128)(2,1)}, u32[]{:S(2)}) copy-start(bf16[512,1024]{1,0:T(8,128)(2,1)} %query.7) | copy-start | bytes 3145732
  5.8 4.5 %collective-permute-start = (f32[4,128,128]{2,1,0:T(8,128)S(1)}, f32[4,128,128]{2,1,0:T(8,128)S(1)}, u32[]{:S(2)}, u32[]{:S(2)}) collective-permute-start(f32[4,128,128]{2,1,0:T(8,128)S(1)} %get-tuple-element.31), channel_id=1, source_target_pairs={{0,4},{4,0},{8,12},{12,8},{16,20},{20,16},{24,28},{28,24},{32,36},... | collective-permute-start | bytes 786440 | tf_op jit(solution)/shard_map/ppermute | solution.py:389
  45.5 9.0 %copy-start.16 = (f32[1024]{0:T(1024)S(1)}, f32[1024]{0:T(1024)}, u32[]{:S(2)}) copy-start(f32[1024]{0:T(1024)} %param.10) | copy-start | bytes 12292
  45.5 9.0 %collective-permute-start.1 = (f32[4,128,128]{2,1,0:T(8,128)S(1)}, f32[4,128,128]{2,1,0:T(8,128)S(1)}, u32[]{:S(2)}, u32[]{:S(2)}) collective-permute-start(f32[4,128,128]{2,1,0:T(8,128)S(1)} %get-tuple-element.33), channel_id=1, source_target_pairs={{0,4},{4,0},{8,12},{12,8},{16,20},{20,16},{24,28},{28,24},{32,36},... | collective-permute-start | bytes 786440 | tf_op jit(solution)/shard_map/ppermute | solution.py:419
  54.5 3.7 %copy-start.8 = (f32[512,1024]{1,0:T(8,128)}, f32[512,1024]{1,0:T(8,128)S(1)}, u32[]{:S(2)}) copy-start(f32[512,1024]{1,0:T(8,128)S(1)} %get-tuple-element.29.grad_normed) | copy-start | bytes 6291460
  54.5 3.7 %copy-start.14 = (f32[4,128,128]{2,1,0:T(8,128)}, f32[4,128,128]{2,1,0:T(8,128)S(1)}, u32[]{:S(2)}) copy-start(f32[4,128,128]{2,1,0:T(8,128)S(1)} %collective-permute-done.1.other) | copy-start | bytes 786436
  58.3 1.3 copy-start.5
  68.0 1.6 %copy-start.6 = (f32[512,1024]{1,0:T(8,128)S(1)}, f32[512,1024]{1,0:T(8,128)}, u32[]{:S(2)}) copy-start(f32[512,1024]{1,0:T(8,128)} %copy-done.5) | copy-start | bytes 6291460
  69.6 1.6 %copy-start.9 = (f32[512,1024]{1,0:T(8,128)S(1)}, f32[512,1024]{1,0:T(8,128)}, u32[]{:S(2)}) copy-start(f32[512,1024]{1,0:T(8,128)} %copy-done.8) | copy-start | bytes 6291460
  71.2 46.2 %copy-start.15 = (f32[4,128,128]{2,1,0:T(8,128)S(1)}, f32[4,128,128]{2,1,0:T(8,128)}, u32[]{:S(2)}) copy-start(f32[4,128,128]{2,1,0:T(8,128)} %copy-done.14) | copy-start | bytes 786436
  74.9 3.3 %collective-permute-start.2 = (f32[4,136,128]{2,1,0:T(8,128)S(1)}, f32[4,136,128]{2,1,0:T(8,128)S(1)}, u32[]{:S(2)}, u32[]{:S(2)}) collective-permute-start(f32[4,136,128]{2,1,0:T(8,128)S(1)} %get-tuple-element.43), channel_id=1, source_target_pairs={{0,4},{4,0},{8,12},{12,8},{16,20},{20,16},{24,28},{28,24},{32,36},... | collective-permute-start | bytes 835592 | tf_op jit(solution)/shard_map/ppermute | solution.py:389
  78.2 39.2 %copy-start.7 = (f32[512,1024]{1,0:T(8,128)S(1)}, f32[512,1024]{1,0:T(8,128)}, u32[]{:S(2)}) copy-start(f32[512,1024]{1,0:T(8,128)} %copy-done.5) | copy-start | bytes 6291460
  78.2 39.2 %copy-start.11 = (bf16[512,1024]{1,0:T(8,128)(2,1)S(1)}, bf16[512,1024]{1,0:T(8,128)(2,1)}, u32[]{:S(2)}) copy-start(bf16[512,1024]{1,0:T(8,128)(2,1)} %gate.3) | copy-start | bytes 3145732
  78.2 39.2 %copy-start.13 = (bf16[512,1024]{1,0:T(8,128)(2,1)S(1)}, bf16[512,1024]{1,0:T(8,128)(2,1)}, u32[]{:S(2)}) copy-start(bf16[512,1024]{1,0:T(8,128)(2,1)} %dout.3) | copy-start | bytes 3145732
  112.7 16.5 %collective-permute-start.3 = (f32[4,136,128]{2,1,0:T(8,128)S(1)}, f32[4,136,128]{2,1,0:T(8,128)S(1)}, u32[]{:S(2)}, u32[]{:S(2)}) collective-permute-start(f32[4,136,128]{2,1,0:T(8,128)S(1)} %get-tuple-element.45), channel_id=1, source_target_pairs={{0,4},{4,0},{8,12},{12,8},{16,20},{20,16},{24,28},{28,24},{32,36},... | collective-permute-start | bytes 835592 | tf_op jit(solution)/shard_map/ppermute | solution.py:419

commit v2 on v0

v2 whole, which is shorter than its diff:
```python
import functools
import jax
import jax.numpy as jnp
from jax import lax
from jax.experimental import pallas as pl
from jax.experimental.pallas import tpu as pltpu
from jax.sharding import PartitionSpec as P

DH = 128
BLOCK = 512
HALF = BLOCK // 2
HEADS_HERE = 8
OWNED = HEADS_HERE // 2
FEATURES = 4096
CHIPS = 32
PIECE = OWNED * DH // CHIPS
EXTRA = 8
EPSILON = 1e-06

F32 = jnp.float32
BF16 = jnp.bfloat16
MIB = 1024 * 1024


def dot_nn(a, b):
    return lax.dot_general(a, b, (((1,), (0,)), ((), ())), preferred_element_type=F32)


def dot_nt(a, b):
    return lax.dot_general(a, b, (((1,), (1,)), ((), ())), preferred_element_type=F32)


def dot_tn(a, b):
    return lax.dot_general(a, b, (((0,), (0,)), ((), ())), preferred_element_type=F32)


def split_state(state):
    high = state.astype(BF16)
    return high, (state - high.astype(F32)).astype(BF16)


def times_state(a, state):
    high, low = split_state(state)
    return dot_nn(jnp.concatenate([a, a], axis=1), jnp.concatenate([high, low], axis=0))


def times_state_t(a, state):
    high, low = split_state(state)
    return dot_nt(jnp.concatenate([a, a], axis=1), jnp.concatenate([high, low], axis=1))


def masked(scores, lower):
    row = lax.broadcasted_iota(jnp.int32, scores.shape, 0)
    column = lax.broadcasted_iota(jnp.int32, scores.shape, 1)
    keep = (row >= column) if lower else (row <= column)
    return jnp.where(keep, scores, 0.0).astype(BF16)


def causal_product(a, b, values):
    top = masked(dot_nt(a[:HALF], b[:HALF]), True)
    left = dot_nt(a[HALF:], b[:HALF]).astype(BF16)
    right = masked(dot_nt(a[HALF:], b[HALF:]), True)
    first = dot_nn(top, values[:HALF])
    second = dot_nn(jnp.concatenate([left, right], axis=1), values)
    return first, second


def anticausal_product(a, b, values):
    left = masked(dot_nt(a[:HALF], b[:HALF]), False)
    right = dot_nt(a[:HALF], b[HALF:]).astype(BF16)
    bottom = masked(dot_nt(a[HALF:], b[HALF:]), False)
    first = dot_nn(jnp.concatenate([left, right], axis=1), values)
    second = dot_nn(bottom, values[HALF:])
    return first, second


WIDE = HEADS_HERE * DH
HALF_WIDE = OWNED * DH


def shape(dims, dtype=F32):
    return jax.ShapeDtypeStruct(dims, dtype)


def vmem():
    return pl.BlockSpec(memory_space=pltpu.VMEM)


def smem():
    return pl.BlockSpec(memory_space=pltpu.SMEM)


def hbm():
    return pl.BlockSpec(memory_space=pltpu.HBM)


def call(kernel, name, outs, core, *args, ins=None, out_places=None, scratch=(), limit=8):
    ins = [vmem()] * len(args) if ins is None else ins
    out_places = [vmem()] * len(outs) if out_places is None else out_places
    return pl.pallas_call(
        kernel,
        in_specs=[smem()] + ins,
        out_specs=out_places,
        out_shape=outs,
        scratch_shapes=list(scratch),
        compiler_params=pltpu.CompilerParams(vmem_limit_bytes=limit * MIB),
        name=name,
    )(core, *args)


def head_columns(core, owned, index):
    first = OWNED * (core[0] if owned else 1 - core[0])
    return pl.ds(pl.multiple_of((first + index) * DH, DH), DH)


def local_columns(index):
    return slice(index * DH, (index + 1) * DH)


def states_theirs_kernel(core, keys, values, theirs, key_here, value_here, sems):
    copies = []
    for owned in (False, True):
        for index in range(OWNED):
            columns = head_columns(core, owned, index)
            place = len(copies)
            pair = [
                pltpu.make_async_copy(keys.at[:, columns], key_here.at[:, columns], sems.at[0, place]),
                pltpu.make_async_copy(values.at[:, columns], value_here.at[:, columns], sems.at[1, place]),
            ]
            for copy in pair:
                copy.start()
            copies.append(pair)
    for index in range(OWNED):
        for copy in copies[index]:
            copy.wait()
        columns = head_columns(core, False, index)
        theirs[index] = dot_tn(key_here[:, columns], value_here[:, columns])
    for pair in copies[OWNED:]:
        for copy in pair:
            copy.wait()


def states_mine_kernel(core, keys, values, mine):
    for index in range(OWNED):
        columns = head_columns(core, True, index)
        mine[index] = dot_tn(keys[:, columns], values[:, columns])


def intra_kernel(core, queries, keys, values, gate, dout, intra_own, intra_other, normed_own, normed_other):
    for owned, intra, normed in ((True, intra_own, normed_own), (False, intra_other, normed_other)):
        for index in range(OWNED):
            columns, here = head_columns(core, owned, index), local_columns(index)
            first, second = causal_product(queries[:, columns], keys[:, columns], values[:, columns])
            intra[:HALF, here] = first
            intra[HALF:, here] = second
            sig = jax.nn.sigmoid(gate[:, columns].astype(F32))
            normed[:, here] = dout[:, columns].astype(F32) * sig


def intra_part(core, queries, keys, values, gate, dout):
    half = shape((BLOCK, HALF_WIDE))
    return call(intra_kernel, "intra", [half] * 4, core, queries, keys, values, gate, dout)


def attend_half(core, owned, queries, intra, normed, gain, state, attn_out):
    squares = products = None
    for index in range(OWNED):
        columns, here = head_columns(core, owned, index), local_columns(index)
        out = intra[:, here] + times_state(queries[:, columns], state[index, :DH])
        attn_out[:, here] = out
        square = out * out
        product = out * (normed[:, here] * gain[:, columns])
        squares = square if squares is None else squares + square
        products = product if products is None else products + product
    return squares, products


def attend_own_kernel(core, queries, intra, normed, gain, state, attn_out, squares, products):
    squares[...], products[...] = attend_half(core, True, queries, intra, normed, gain, state, attn_out)


def attend_other_kernel(core, queries, intra, normed, gain, state, squares, products, attn_out, sums):
    found = attend_half(core, False, queries, intra, normed, gain, state, attn_out)
    for which, (acc, more) in enumerate(zip((squares, products), found)):
        total = acc[...] + more
        for part in range(BLOCK // DH):
            turned = total[part * DH:(part + 1) * DH, :].T
            place = which * (BLOCK // DH) + part
            sums[place:place + 1, :] = jnp.sum(turned, axis=0, keepdims=True)


def grads_half(core, owned, queries, attn_out, normed, gain, scale, cubes, grad, states):
    for index in range(OWNED):
        columns, here = head_columns(core, owned, index), local_columns(index)
        out, rate, one = attn_out[:, here], scale[...], normed[:, here]
        part = (rate * (one * gain[:, columns]) - out * cubes[...]).astype(BF16)
        grad[:, here] = part
        states[index, :DH] = dot_tn(queries[:, columns], part)
        row = jnp.sum(one * out * rate, axis=0, keepdims=True)
        states[index, DH:] = jnp.broadcast_to(row, (EXTRA, DH))


def grads_theirs_kernel(core, sums, sums_1, sums_2, sums_3, queries, attn_out, normed, gain,
                        grad, scale, cubes, theirs):
    whole = (sums[...] + sums_1[...]) + (sums_2[...] + sums_3[...])
    for part in range(BLOCK // DH):
        rows = slice(part * DH, (part + 1) * DH)
        mean_square = whole[part:part + 1, :] / FEATURES
        mean_prod = whole[part + 4:part + 5, :] / FEATURES
        one = lax.rsqrt(mean_square + EPSILON)
        scale[rows, :] = jnp.broadcast_to(one, (DH, DH)).T
        cubes[rows, :] = jnp.broadcast_to(one * one * one * mean_prod, (DH, DH)).T
    grads_half(core, False, queries, attn_out, normed, gain, scale, cubes, grad, theirs)


def grads_mine_kernel(core, scale, cubes, queries, attn_out, normed, gain, grad, mine):
    grads_half(core, True, queries, attn_out, normed, gain, scale, cubes, grad, mine)


def local_kernel(core, queries, keys, values, gate, out_own, out_other, normed_own, normed_other,
                 scale, gain, grad_own, grad_other, own, other,
                 output, dgate, grad_query, key_own, key_other, value_own, value_other,
                 output_buf, dgate_buf, query_buf, sems):
    halves = (
        (True, out_own, normed_own, grad_own, own, key_own, value_own),
        (False, out_other, normed_other, grad_other, other, key_other, value_other),
    )
    copies = []
    for owned, attn_out, normed, grads, states, part_key, part_value in halves:
        for index in range(OWNED):
            columns, here = head_columns(core, owned, index), local_columns(index)
            place = index if owned else OWNED + index
            sig = jax.nn.sigmoid(gate[:, columns].astype(F32))
            scaled = attn_out[:, here] * scale[...] * gain[:, columns]
            output_buf[place] = (scaled * sig).astype(BF16)
            dgate_buf[place] = (normed[:, here] * scaled * (1.0 - sig)).astype(BF16)
            query, key, value, grad = queries[:, columns], keys[:, columns], values[:, columns], grads[:, here]
            inter = times_state_t(grad, states[index, :DH])
            first, second = causal_product(grad, value, key)
            query_buf[place, :HALF] = (first + inter[:HALF]).astype(BF16)
            query_buf[place, HALF:] = (second + inter[HALF:]).astype(BF16)
            first, second = anticausal_product(value, grad, query)
            part_key[:HALF, here] = first
            part_key[HALF:, here] = second
            first, second = anticausal_product(key, query, grad)
            part_value[:HALF, here] = first
            part_value[HALF:, here] = second
            targets = ((output_buf, output), (dgate_buf, dgate), (query_buf, grad_query))
            for which, (buffer, target) in enumerate(targets):
                copy = pltpu.make_async_copy(buffer.at[place], target.at[:, columns], sems.at[which, place])
                copy.start()
                copies.append(copy)
    for copy in copies:
        copy.wait()


def last_kernel(core, keys, values, key_own, key_other, value_own, value_other, own, other,
                grad_key, grad_value, dgain, key_buf, value_buf, sems):
    copies = []
    halves = ((True, key_own, value_own, own), (False, key_other, value_other, other))
    for owned, part_key, part_value, states in halves:
        for index in range(OWNED):
            columns, here = head_columns(core, owned, index), local_columns(index)
            place = index if owned else OWNED + index
            state = states[index, :DH]
            key_buf[place] = (part_key[:, here] + times_state_t(values[:, columns], state)).astype(BF16)
            value_buf[place] = (part_value[:, here] + times_state(keys[:, columns], state)).astype(BF16)
            pair = [
                pltpu.make_async_copy(key_buf.at[place], grad_key.at[:, columns], sems.at[0, place]),
                pltpu.make_async_copy(value_buf.at[place], grad_value.at[:, columns], sems.at[1, place]),
            ]
            for copy in pair:
                copy.start()
            copies += pair
            row = OWNED * (core[0] if owned else 1 - core[0]) + index
            dgain[pl.ds(row, 1), :] = states[index, DH:DH + 1]
    for copy in copies:
        copy.wait()


def piece_rows(place, rows):
    return slice(place * rows, place * rows + PIECE)


def pack_kernel(rows, core, mine, received, pieces):
    for head in range(OWNED):
        for part in range(DH // PIECE):
            source = slice(part * PIECE, (part + 1) * PIECE)
            place = head * (DH // PIECE) + part
            pieces[piece_rows(place, rows)] = mine[head, source] + received[head, source]
            if rows > PIECE:
                last = place * rows + PIECE
                pieces[last:last + 1] = mine[head, DH:DH + 1] + received[head, DH:DH + 1]


def prefix_kernel(rows, reverse, core, pieces, sums):
    total = jnp.zeros((PIECE, DH), F32)
    order = range(CHIPS - 1, -1, -1) if reverse else range(CHIPS)
    for chip in order:
        sums[piece_rows(chip, rows)] = total
        total = total + pieces[piece_rows(chip, rows)]
    if rows > PIECE:
        places = [slice(chip * rows + PIECE, (chip + 1) * rows) for chip in range(CHIPS)]
        whole = pieces[places[0]]
        for place in places[1:]:
            whole = whole + pieces[place]
        for place in places:
            sums[place] = whole


def unpack_kernel(rows, reverse, core, back, mine, received, own, send):
    ahead = core[0] == (1 if reverse else 0)
    for head in range(OWNED):
        for part in range(DH // PIECE):
            target = slice(part * PIECE, (part + 1) * PIECE)
            state = back[piece_rows(head * (DH // PIECE) + part, rows)]
            own[head, target] = state + jnp.where(ahead, 0.0, received[head, target])
            send[head, target] = state + jnp.where(ahead, mine[head, target], 0.0)
        if rows > PIECE:
            last = head * (DH // PIECE) * rows + PIECE
            whole = jnp.broadcast_to(back[last:last + 1], (EXTRA, DH))
            own[head, DH:] = whole
            send[head, DH:] = whole


def sums_beyond(core, mine, theirs, seq_size, reverse):
    cores = [(i, i ^ 1) for i in range(seq_size)]
    groups = [[2 * i + one for i in range(seq_size // 2)] for one in range(2)]
    rows = PIECE + (1 if mine.shape[1] > DH else 0)
    flat = (CHIPS * rows, DH)

    def exchange(pieces):
        pieces = pieces.reshape(CHIPS, 1, rows * DH)
        return lax.all_to_all(pieces, "seq", 0, 0, axis_index_groups=groups).reshape(flat)

    received = lax.ppermute(theirs, "seq", cores)
    (pieces,) = call(functools.partial(pack_kernel, rows), "pack", [shape(flat)], core, mine, received)
    (sums,) = call(
        functools.partial(prefix_kernel, rows, reverse), "prefix", [shape(flat)], core, exchange(pieces)
    )
    own, send = call(
        functools.partial(unpack_kernel, rows, reverse), "unpack", [shape(mine.shape)] * 2,
        core, exchange(sums), mine, received,
    )
    return own, lax.ppermute(send, "seq", cores)


def body(queries, keys, values, gate, gain, dout):
    seq_size = lax.axis_size("seq")
    core = lax.rem(lax.axis_index("seq"), 2).astype(jnp.int32).reshape(1)
    gain_row = gain.reshape(1, WIDE)
    half = shape((BLOCK, HALF_WIDE))
    half_low = shape((BLOCK, HALF_WIDE), BF16)
    wide = shape((BLOCK, WIDE), BF16)
    tokens = shape((BLOCK, DH))
    with_gain = shape((OWNED, DH + EXTRA, DH))

    state = shape((OWNED, DH, DH))
    theirs, keys, values = call(
        states_theirs_kernel, "states_theirs", [state, wide, wide], core, keys, values,
        ins=[hbm()] * 2, scratch=[pltpu.SemaphoreType.DMA((2, HEADS_HERE))], limit=8,
    )
    (mine,) = call(states_mine_kernel, "states_mine", [state], core, keys, values)
    own, other = sums_beyond(core, mine, theirs, seq_size, False)
    intra_own, intra_other, normed_own, normed_other = intra_part(core, queries, keys, values, gate, dout)
    out_own, squares, products = call(
        attend_own_kernel, "attend_own", [half, tokens, tokens],
        core, queries, intra_own, normed_own, gain_row, own,
    )
    out_other, sums = call(
        attend_other_kernel, "attend_other", [half, shape((8, DH))],
        core, queries, intra_other, normed_other, gain_row, other, squares, products,
    )
    ring = lax.axis_size("head")
    all_sums = [sums] + [
        lax.ppermute(sums, "head", [(i, (i + step) % ring) for i in range(ring)]) for step in (2, 1, 3)
    ]
    grad_other, scale, cubes, theirs = call(
        grads_theirs_kernel, "grads_theirs", [half_low, tokens, tokens, with_gain],
        core, *all_sums, queries, out_other, normed_other, gain_row,
    )
    grad_own, mine = call(
        grads_mine_kernel, "grads_mine", [half_low, with_gain],
        core, scale, cubes, queries, out_own, normed_own, gain_row,
    )
    buffer = pltpu.VMEM((HEADS_HERE, BLOCK, DH), BF16)
    output, dgate, grad_query, key_own, key_other, value_own, value_other = call(
        local_kernel, "local_grads", [wide, wide, wide, half, half, half, half],
        core, queries, keys, values, gate, out_own, out_other, normed_own, normed_other,
        scale, gain_row, grad_own, grad_other, own, other,
        out_places=[hbm()] * 3 + [vmem()] * 4,
        scratch=[buffer] * 3 + [pltpu.SemaphoreType.DMA((3, HEADS_HERE))],
    )
    own, other = sums_beyond(core, mine, theirs, seq_size, True)
    grad_key, grad_value, dgain = call(
        last_kernel, "last_grads", [wide, wide, shape((HEADS_HERE, DH))],
        core, keys, values, key_own, key_other, value_own, value_other, own, other,
        out_places=[hbm(), hbm(), vmem()],
        scratch=[buffer, buffer, pltpu.SemaphoreType.DMA((2, HEADS_HERE))],
    )
    return output, grad_query, grad_key, grad_value, dgate, dgain.reshape(WIDE)


def solution(mesh):
    wide = P("seq", "head")
    return jax.shard_map(
        body,
        mesh=mesh,
        in_specs=(wide, wide, wide, wide, P("head"), wide),
        out_specs=(wide, wide, wide, wide, wide, P("head")),
        check_vma=False,
    )
```

time: 512 us -> 109 us (0.21)
  blocking collectives: 214 us -> 65.9 us
  waiting for transfers between devices: 140 us -> 3.34 us
  other arithmetic: 83.7 us -> 0 us
  matrix products: 30.9 us -> 0 us
  Pallas kernels: 0 us -> 18.7 us
  local copies, waits for them, and re-layouts: 21.6 us -> 3.14 us
  starting transfers between devices: 0.08 us -> 16.8 us
  between operations: 14.3 us -> 0.91 us
    psum x3 -> x0, blocking collectives: 214 us -> none  [the longest x1 200 us: body(): dgain_hd = lax.psum(gain_part, 'seq')]
    all_gather x2 -> x0, waiting for transfers between devices: 140 us -> none  [entering(): gathered = lax.all_gather(part, axis)]
    add x63 -> x0, other arithmetic: 73.8 us -> none  [add_states(): return earlier + later]
    all_to_all x0 -> x4, blocking collectives: none -> 65.9 us  [exchange(): lax.all_to_all(pieces, 'seq', 0, 0, axis_index_groups=groups).reshape(flat)]
    dot_general x12 -> x0, matrix products: 30.9 us -> none  [the longest x1 4.37 us: body(): jnp.einsum('bhst,bshe->bthe', attend, grad_blk, preferred_element_type=jn...]
    pallas_call x0 -> x15, Pallas kernels: none -> 18.7 us  [call(): pl.pallas_call(kernel, in_specs=[smem()] + ins, out_specs=out_places, out...]
    ppermute x0 -> x7, starting transfers between devices: none -> 16.8 us  [the longest x2 7.64 us: sums_beyond(): return (own, lax.ppermute(send, 'seq', cores))]
    unnamed x42 -> x12, local copies, waits for them, and re-layouts: 12.1 us -> 3.14 us
  transfers between devices with their start and end apart: 2 -> 7, of which waited for: 2 -> 4; matrix products, arithmetic and copies ran while one was open for 3% -> 0% of each run, Pallas kernels for 0% -> 11%
where the time goes in v2:
time: 109 us
  blocking collectives  65.9 us (60%)
  Pallas kernels  18.7 us (17%)
  starting transfers between devices  16.8 us (15%)
  waiting for transfers between devices  3.34 us (3%)
  local copies, waits for them, and re-layouts  3.14 us (3%)
    all_to_all x4, blocking collectives, exchange(): lax.all_to_all(pieces, 'seq', 0, 0, axis_index_groups=groups).reshape(flat)  65.9 us
    pallas_call x15, Pallas kernels, call(): pl.pallas_call(kernel, in_specs=[smem()] + ins, out_specs=out_places, out...  18.7 us
    ppermute x2, starting transfers between devices, sums_beyond(): return (own, lax.ppermute(send, 'seq', cores))  7.64 us
    ppermute x2, starting transfers between devices, sums_beyond(): received = lax.ppermute(theirs, 'seq', cores)  4.86 us
    ppermute x3, starting transfers between devices, body(): lax.ppermute(sums, 'head', [(i, (i + step) % ring) for i in range(ring)])  4.3 us
    unnamed x12, local copies, waits for them, and re-layouts  3.14 us
    ppermute x3, waiting for transfers between devices, body(): lax.ppermute(sums, 'head', [(i, (i + step) % ring) for i in range(ring)])  2.23 us
  transfers between devices with their start and end apart: 7, of which 4 were waited for; matrix products, arithmetic and copies ran while one was open for 0% of the time, Pallas kernels for 11%

profile of v2, /device:TPU:1, one launch (start us, length us, event | category | flops | bytes accessed | tf_op | source)
XLA Modules:
  0.0 108.7 jit_solution(12965605951574893979)
XLA Ops:
  0.6 0.0 copy-start.2
  0.6 1.2 %copy-done.2 = bf16[512,1024]{1,0:T(8,128)(2,1)S(1)} copy-done((bf16[512,1024]{1,0:T(8,128)(2,1)S(1)}, bf16[512,1024]{1,0:T(8,128)(2,1)}, u32[]{:S(2)}) %copy-start.2) | copy-done | bytes 1048600
  1.9 0.0 copy-start.3
  1.9 1.2 %copy-done.3 = bf16[512,1024]{1,0:T(8,128)(2,1)S(1)} copy-done((bf16[512,1024]{1,0:T(8,128)(2,1)S(1)}, bf16[512,1024]{1,0:T(8,128)(2,1)}, u32[]{:S(2)}) %copy-start.3) | copy-done | bytes 1048600
  3.1 1.8 %states_theirs.1 = (f32[4,128,128]{2,1,0:T(8,128)S(1)}, bf16[512,1024]{1,0:T(8,128)(2,1)S(1)}, bf16[512,1024]{1,0:T(8,128)(2,1)S(1)}) custom-call(s32[1]{0:T(128)} %bitcast.core, bf16[512,1024]{1,0:T(8,128)(2,1)S(1)} %copy-done.2, bf16[512,1024]{1,0:T(8,128)(2,1)S(1)} %copy-done.3), custom_call_target="tpu_custom_call" | custom-call | tf_op jit(solution)/shard_map/states_theirs/pallas_call | solution.py:100
  4.9 3.3 %collective-permute-start = (f32[4,128,128]{2,1,0:T(8,128)S(1)}, f32[4,128,128]{2,1,0:T(8,128)S(1)}, u32[]{:S(2)}, u32[]{:S(2)}) collective-permute-start(f32[4,128,128]{2,1,0:T(8,128)S(1)} %get-tuple-element.42), channel_id=1, source_target_pairs={{0,4},{4,0},{8,12},{12,8},{16,20},{20,16},{24,28},{28,24},{32,36},... | collective-permute-start | bytes 786440 | tf_op jit(solution)/shard_map/ppermute | solution.py:336
  8.2 0.5 states_mine.1.mine
  8.7 0.7 collective-permute-done.received
  9.4 0.0 copy-start.4
  9.4 0.0 copy-start.1
  9.4 19.1 %all_to_all.20 = f32[32,1,2048]{2,1,0:T(1,128)S(1)} all-to-all(f32[32,1,2048]{2,1,0:T(1,128)S(1)} %bitcast.18), channel_id=1, replica_groups={{0,8,16,24,32,40,48,56,64,72,80,88,96,104,112,120,128,136,144,152,160,1..., dimensions={0} | all-to-all | bytes 524288 | tf_op jit(solution)/shard_map/all_to_all | solution.py:334
  28.5 0.0 copy-start
  28.5 16.3 %all_to_all.21 = f32[32,1,2048]{2,1,0:T(1,128)S(1)} all-to-all(f32[32,1,2048]{2,1,0:T(1,128)S(1)} %bitcast.16), channel_id=1, replica_groups={{0,8,16,24,32,40,48,56,64,72,80,88,96,104,112,120,128,136,144,152,160,1..., dimensions={0} | all-to-all | bytes 524288 | tf_op jit(solution)/shard_map/all_to_all | solution.py:334
  44.8 0.1 unpack.2
  44.9 3.7 %collective-permute-start.1 = (f32[4,128,128]{2,1,0:T(8,128)S(1)}, f32[4,128,128]{2,1,0:T(8,128)S(1)}, u32[]{:S(2)}, u32[]{:S(2)}) collective-permute-start(f32[4,128,128]{2,1,0:T(8,128)S(1)} %get-tuple-element.47), channel_id=1, source_target_pairs={{0,4},{4,0},{8,12},{12,8},{16,20},{20,16},{24,28},{28,24},{32,36},... | collective-permute-start | bytes 786440 | tf_op jit(solution)/shard_map/ppermute | solution.py:345
  48.6 0.0 copy-done.4
  48.6 0.0 copy-done.1
  48.6 0.0 copy-done
  48.6 2.6 %intra.1 = (f32[512,512]{1,0:T(8,128)S(1)}, f32[512,512]{1,0:T(8,128)S(1)}, f32[512,512]{1,0:T(8,128)S(1)}, f32[512,512]{1,0:T(8,128)S(1)}) custom-call(s32[1]{0:T(128)} %bitcast.core, bf16[512,1024]{1,0:T(8,128)(2,1)S(1)} %copy-done, bf16[512,1024]{1,0:T(8,128)(2,1)S(1)} %get-tuple-element.38.keys, bf16[512,1024]{1,0:T(8,128)(2,1)S(1)} %get-tuple-element.39.values, ...), custom_call_target="tpu_custom_call" | custom-call | tf_op jit(solution)/shard_map/intra/pallas_call | solution.py:100
  51.2 0.0 copy-start.5
  51.2 0.7 copy-done.5
  51.9 0.5 attend_own.1
  52.4 0.0 collective-permute-done.1.state.other
  52.4 0.6 attend_other.1
  53.0 2.6 %collective-permute-start.4 = (f32[8,128]{1,0:T(8,128)S(1)}, f32[8,128]{1,0:T(8,128)S(1)}, u32[]{:S(2)}, u32[]{:S(2)}) collective-permute-start(f32[8,128]{1,0:T(8,128)S(1)} %get-tuple-element.51.sums), channel_id=1, source_target_pairs={{0,3},{1,0},{2,1},{3,2},{4,7},{5,4},{6,5},{7,6},{8,11},{9,8},{10,9... | collective-permute-start | bytes 12296 | tf_op jit(solution)/shard_map/ppermute | solution.py:376
  55.6 0.0 collective-permute-start.3
  55.6 1.7 %collective-permute-start.2 = (f32[8,128]{1,0:T(8,128)S(1)}, f32[8,128]{1,0:T(8,128)S(1)}, u32[]{:S(2)}, u32[]{:S(2)}) collective-permute-start(f32[8,128]{1,0:T(8,128)S(1)} %get-tuple-element.51.sums), channel_id=1, source_target_pairs={{0,2},{1,3},{2,0},{3,1},{4,6},{5,7},{6,4},{7,5},{8,10},{9,11},{10,... | collective-permute-start | bytes 12296 | tf_op jit(solution)/shard_map/ppermute | solution.py:376
  57.3 0.0 collective-permute-done.4.sums_3
  57.3 1.9 %collective-permute-done.3.sums_2 = f32[8,128]{1,0:T(8,128)S(1)} collective-permute-done((f32[8,128]{1,0:T(8,128)S(1)}, f32[8,128]{1,0:T(8,128)S(1)}, u32[]{:S(2)}, u32[]{:S(2)}) %collective-permute-start.3) | collective-permute-done | bytes 4128 | tf_op jit(solution)/shard_map/ppermute | solution.py:376
  59.3 0.3 collective-permute-done.2.sums_1
  59.6 0.9 grads_theirs.1
  60.4 1.5 %collective-permute-start.5 = (f32[4,136,128]{2,1,0:T(8,128)S(1)}, f32[4,136,128]{2,1,0:T(8,128)S(1)}, u32[]{:S(2)}, u32[]{:S(2)}) collective-permute-start(f32[4,136,128]{2,1,0:T(8,128)S(1)} %get-tuple-element.63), channel_id=1, source_target_pairs={{0,4},{4,0},{8,12},{12,8},{16,20},{20,16},{24,28},{28,24},{32,36},... | collective-permute-start | bytes 835592 | tf_op jit(solution)/shard_map/ppermute | solution.py:336
  62.0 0.7 grads_mine.1
  62.7 0.4 collective-permute-done.5.received
  63.1 0.1 pack.3
  63.2 13.8 %all_to_all.22 = f32[32,1,2176]{2,1,0:T(1,128)S(1)} all-to-all(f32[32,1,2176]{2,1,0:T(1,128)S(1)} %bitcast.14), channel_id=1, replica_groups={{0,8,16,24,32,40,48,56,64,72,80,88,96,104,112,120,128,136,144,152,160,1..., dimensions={0} | all-to-all | bytes 557056 | tf_op jit(solution)/shard_map/all_to_all | solution.py:334
  77.1 16.7 %all_to_all.23 = f32[32,1,2176]{2,1,0:T(1,128)S(1)} all-to-all(f32[32,1,2176]{2,1,0:T(1,128)S(1)} %bitcast.12), channel_id=1, replica_groups={{0,8,16,24,32,40,48,56,64,72,80,88,96,104,112,120,128,136,144,152,160,1..., dimensions={0} | all-to-all | bytes 557056 | tf_op jit(solution)/shard_map/all_to_all | solution.py:334
  93.8 0.1 unpack.3
  93.8 3.9 %collective-permute-start.6 = (f32[4,136,128]{2,1,0:T(8,128)S(1)}, f32[4,136,128]{2,1,0:T(8,128)S(1)}, u32[]{:S(2)}, u32[]{:S(2)}) collective-permute-start(f32[4,136,128]{2,1,0:T(8,128)S(1)} %get-tuple-element.65), channel_id=1, source_target_pairs={{0,4},{4,0},{8,12},{12,8},{16,20},{20,16},{24,28},{28,24},{32,36},... | collective-permute-start | bytes 835592 | tf_op jit(solution)/shard_map/ppermute | solution.py:345
  97.8 8.0 %local_grads.1 = (bf16[512,1024]{1,0:T(8,128)(2,1)}, bf16[512,1024]{1,0:T(8,128)(2,1)}, bf16[512,1024]{1,0:T(8,128)(2,1)}, f32[512,512]{1,0:T(8,128)S(1)}, f32[5...) custom-call(s32[1]{0:T(128)} %bitcast.core, bf16[512,1024]{1,0:T(8,128)(2,1)S(1)} %copy-done, ...), custom_call_target="tpu_custom_call" | custom-call | tf_op jit(solution)/shard_map/local_grads/pallas_call | solution.py:100
  105.8 0.0 collective-permute-done.6.other
  105.8 2.7 %last_grads.1 = (bf16[512,1024]{1,0:T(8,128)(2,1)}, bf16[512,1024]{1,0:T(8,128)(2,1)}, f32[8,128]{1,0:T(8,128)}) custom-call(s32[1]{0:T(128)} %bitcast.core, bf16[512,1024]{1,0:T(8,128)(2,1)S(1)} %get-tuple-element.38.keys, bf16[512,1024]{1,0:T(8,128)(2,1)S(1)} %get-tuple-element.39.values, f32[512,512]{1,0:T(8,128)S(1)} %get-tuple-element.58.key_own, ...), custom_call_target="tpu_custom_call" | custom-call | tf_op jit(solution)/shard_map/last_grads/pallas_call | solution.py:100
  (3 shorter events, 0.1 us)
Async XLA Ops:
  0.6 1.2 %copy-start.2 = (bf16[512,1024]{1,0:T(8,128)(2,1)S(1)}, bf16[512,1024]{1,0:T(8,128)(2,1)}, u32[]{:S(2)}) copy-start(bf16[512,1024]{1,0:T(8,128)(2,1)} %keys.1) | copy-start | bytes 3145732
  1.9 1.2 %copy-start.3 = (bf16[512,1024]{1,0:T(8,128)(2,1)S(1)}, bf16[512,1024]{1,0:T(8,128)(2,1)}, u32[]{:S(2)}) copy-start(bf16[512,1024]{1,0:T(8,128)(2,1)} %values.1) | copy-start | bytes 3145732
  4.9 4.5 %collective-permute-start = (f32[4,128,128]{2,1,0:T(8,128)S(1)}, f32[4,128,128]{2,1,0:T(8,128)S(1)}, u32[]{:S(2)}, u32[]{:S(2)}) collective-permute-start(f32[4,128,128]{2,1,0:T(8,128)S(1)} %get-tuple-element.42), channel_id=1, source_target_pairs={{0,4},{4,0},{8,12},{12,8},{16,20},{20,16},{24,28},{28,24},{32,36},... | collective-permute-start | bytes 786440 | tf_op jit(solution)/shard_map/ppermute | solution.py:336
  9.4 39.2 %copy-start.4 = (bf16[512,1024]{1,0:T(8,128)(2,1)S(1)}, bf16[512,1024]{1,0:T(8,128)(2,1)}, u32[]{:S(2)}) copy-start(bf16[512,1024]{1,0:T(8,128)(2,1)} %dout.1) | copy-start | bytes 3145732
  9.4 39.2 %copy-start.1 = (bf16[512,1024]{1,0:T(8,128)(2,1)S(1)}, bf16[512,1024]{1,0:T(8,128)(2,1)}, u32[]{:S(2)}) copy-start(bf16[512,1024]{1,0:T(8,128)(2,1)} %gate.3) | copy-start | bytes 3145732
  28.5 20.1 %copy-start = (bf16[512,1024]{1,0:T(8,128)(2,1)S(1)}, bf16[512,1024]{1,0:T(8,128)(2,1)}, u32[]{:S(2)}) copy-start(bf16[512,1024]{1,0:T(8,128)(2,1)} %queries.11) | copy-start | bytes 3145732
  44.9 7.5 %collective-permute-start.1 = (f32[4,128,128]{2,1,0:T(8,128)S(1)}, f32[4,128,128]{2,1,0:T(8,128)S(1)}, u32[]{:S(2)}, u32[]{:S(2)}) collective-permute-start(f32[4,128,128]{2,1,0:T(8,128)S(1)} %get-tuple-element.47), channel_id=1, source_target_pairs={{0,4},{4,0},{8,12},{12,8},{16,20},{20,16},{24,28},{28,24},{32,36},... | collective-permute-start | bytes 786440 | tf_op jit(solution)/shard_map/ppermute | solution.py:345
  51.2 0.7 copy-start.5
  53.0 4.3 %collective-permute-start.4 = (f32[8,128]{1,0:T(8,128)S(1)}, f32[8,128]{1,0:T(8,128)S(1)}, u32[]{:S(2)}, u32[]{:S(2)}) collective-permute-start(f32[8,128]{1,0:T(8,128)S(1)} %get-tuple-element.51.sums), channel_id=1, source_target_pairs={{0,3},{1,0},{2,1},{3,2},{4,7},{5,4},{6,5},{7,6},{8,11},{9,8},{10,9... | collective-permute-start | bytes 12296 | tf_op jit(solution)/shard_map/ppermute | solution.py:376
  55.6 3.7 %collective-permute-start.3 = (f32[8,128]{1,0:T(8,128)S(1)}, f32[8,128]{1,0:T(8,128)S(1)}, u32[]{:S(2)}, u32[]{:S(2)}) collective-permute-start(f32[8,128]{1,0:T(8,128)S(1)} %get-tuple-element.51.sums), channel_id=1, source_target_pairs={{0,1},{1,2},{2,3},{3,0},{4,5},{5,6},{6,7},{7,4},{8,9},{9,10},{10,1... | collective-permute-start | bytes 12296 | tf_op jit(solution)/shard_map/ppermute | solution.py:376
  55.6 4.0 %collective-permute-start.2 = (f32[8,128]{1,0:T(8,128)S(1)}, f32[8,128]{1,0:T(8,128)S(1)}, u32[]{:S(2)}, u32[]{:S(2)}) collective-permute-start(f32[8,128]{1,0:T(8,128)S(1)} %get-tuple-element.51.sums), channel_id=1, source_target_pairs={{0,2},{1,3},{2,0},{3,1},{4,6},{5,7},{6,4},{7,5},{8,10},{9,11},{10,... | collective-permute-start | bytes 12296 | tf_op jit(solution)/shard_map/ppermute | solution.py:376
  60.4 2.7 %collective-permute-start.5 = (f32[4,136,128]{2,1,0:T(8,128)S(1)}, f32[4,136,128]{2,1,0:T(8,128)S(1)}, u32[]{:S(2)}, u32[]{:S(2)}) collective-permute-start(f32[4,136,128]{2,1,0:T(8,128)S(1)} %get-tuple-element.63), channel_id=1, source_target_pairs={{0,4},{4,0},{8,12},{12,8},{16,20},{20,16},{24,28},{28,24},{32,36},... | collective-permute-start | bytes 835592 | tf_op jit(solution)/shard_map/ppermute | solution.py:336
  93.8 12.0 %collective-permute-start.6 = (f32[4,136,128]{2,1,0:T(8,128)S(1)}, f32[4,136,128]{2,1,0:T(8,128)S(1)}, u32[]{:S(2)}, u32[]{:S(2)}) collective-permute-start(f32[4,136,128]{2,1,0:T(8,128)S(1)} %get-tuple-element.65), channel_id=1, source_target_pairs={{0,4},{4,0},{8,12},{12,8},{16,20},{20,16},{24,28},{28,24},{32,36},... | collective-permute-start | bytes 835592 | tf_op jit(solution)/shard_map/ppermute | solution.py:345

commit v3 on v2

v3 whole, which is shorter than its diff:
```python
import functools
import jax
import jax.numpy as jnp
from jax import lax
from jax.experimental import pallas as pl
from jax.experimental.pallas import tpu as pltpu
from jax.sharding import PartitionSpec as P

DH = 128
BLOCK = 512
HALF = BLOCK // 2
HEADS_HERE = 8
OWNED = HEADS_HERE // 2
FEATURES = 4096
COLUMN = 4
ROW = 8
PIECE = OWNED * DH // ROW
EXTRA = 8
EPSILON = 1e-06

F32 = jnp.float32
BF16 = jnp.bfloat16
MIB = 1024 * 1024
FIRST_LIMIT = 8 * MIB
PARTS = 4


def dot_nn(a, b):
    return lax.dot_general(a, b, (((1,), (0,)), ((), ())), preferred_element_type=F32)


def dot_nt(a, b):
    return lax.dot_general(a, b, (((1,), (1,)), ((), ())), preferred_element_type=F32)


def dot_tn(a, b):
    return lax.dot_general(a, b, (((0,), (0,)), ((), ())), preferred_element_type=F32)


def split_state(state):
    high = state.astype(BF16)
    return high, (state - high.astype(F32)).astype(BF16)


def times_state(a, state):
    high, low = split_state(state)
    return dot_nn(jnp.concatenate([a, a], axis=1), jnp.concatenate([high, low], axis=0))


def times_state_t(a, state):
    high, low = split_state(state)
    return dot_nt(jnp.concatenate([a, a], axis=1), jnp.concatenate([high, low], axis=1))


def masked(scores, lower):
    row = lax.broadcasted_iota(jnp.int32, scores.shape, 0)
    column = lax.broadcasted_iota(jnp.int32, scores.shape, 1)
    keep = (row >= column) if lower else (row <= column)
    return jnp.where(keep, scores, 0.0).astype(BF16)


def causal_product(a, b, values):
    top = masked(dot_nt(a[:HALF], b[:HALF]), True)
    left = dot_nt(a[HALF:], b[:HALF]).astype(BF16)
    right = masked(dot_nt(a[HALF:], b[HALF:]), True)
    first = dot_nn(top, values[:HALF])
    second = dot_nn(jnp.concatenate([left, right], axis=1), values)
    return first, second


def anticausal_product(a, b, values):
    left = masked(dot_nt(a[:HALF], b[:HALF]), False)
    right = dot_nt(a[:HALF], b[HALF:]).astype(BF16)
    bottom = masked(dot_nt(a[HALF:], b[HALF:]), False)
    first = dot_nn(jnp.concatenate([left, right], axis=1), values)
    second = dot_nn(bottom, values[HALF:])
    return first, second


WIDE = HEADS_HERE * DH
HALF_WIDE = OWNED * DH


def shape(dims, dtype=F32):
    return jax.ShapeDtypeStruct(dims, dtype)


def vmem():
    return pl.BlockSpec(memory_space=pltpu.VMEM)


def smem():
    return pl.BlockSpec(memory_space=pltpu.SMEM)


def hbm():
    return pl.BlockSpec(memory_space=pltpu.HBM)


def call(kernel, name, outs, core, *args, ins=None, out_places=None, scratch=(), limit=8 * MIB, aliases={}):
    ins = [vmem()] * len(args) if ins is None else ins
    out_places = [vmem()] * len(outs) if out_places is None else out_places
    return pl.pallas_call(
        kernel,
        in_specs=[smem()] + ins,
        out_specs=out_places,
        out_shape=outs,
        scratch_shapes=list(scratch),
        input_output_aliases=aliases,
        compiler_params=pltpu.CompilerParams(vmem_limit_bytes=limit),
        name=name,
    )(core, *args)


def head_columns(core, owned, index):
    first = OWNED * (core[0] if owned else 1 - core[0])
    return pl.ds(pl.multiple_of((first + index) * DH, DH), DH)


def local_columns(index):
    return slice(index * DH, (index + 1) * DH)


def states_kernel(core, column, keys, values, theirs, mine, key_buf, value_buf, sems):
    copies = []
    for part in range(PARTS):
        rows = slice(part * BLOCK // PARTS, (part + 1) * BLOCK // PARTS)
        pair = [
            pltpu.make_async_copy(keys.at[rows], key_buf.at[rows], sems.at[0, part]),
            pltpu.make_async_copy(values.at[rows], value_buf.at[rows], sems.at[1, part]),
        ]
        for copy in pair:
            copy.start()
        copies.append(pair)
    for part in range(PARTS):
        for copy in copies[part]:
            copy.wait()
        rows = slice(part * BLOCK // PARTS, (part + 1) * BLOCK // PARTS)
        for owned, states in ((False, theirs), (True, mine)):
            for index in range(OWNED):
                columns = head_columns(core, owned, index)
                state = dot_tn(key_buf[rows, columns], value_buf[rows, columns])
                states[index] = state if part == 0 else states[index] + state


def intra_kernel(owned, core, queries, keys, values, intra, done):
    for index in range(OWNED):
        columns, here = head_columns(core, owned, index), local_columns(index)
        first, second = causal_product(queries[:, columns], keys[:, columns], values[:, columns])
        intra[:HALF, here] = first
        intra[HALF:, here] = second
    done[...] = jnp.zeros_like(done)


def gates_kernel(core, gate, dout, gain, normed_own, normed_other, gain_here, done):
    for owned, normed in ((True, normed_own), (False, normed_other)):
        for index in range(OWNED):
            columns, here = head_columns(core, owned, index), local_columns(index)
            normed[:, here] = dout[:, columns].astype(F32) * jax.nn.sigmoid(gate[:, columns].astype(F32))
    gain_here[...] = gain[...]
    done[...] = jnp.zeros_like(done)


def turned_kernel(owned, core, queries, keys, top, bottom, done):
    for index in range(OWNED):
        columns = head_columns(core, owned, index)
        query, key = queries[:, columns], keys[:, columns]
        top[index, :, :HALF] = masked(dot_nt(key[:HALF], query[:HALF]), False)
        top[index, :, HALF:] = dot_nt(key[:HALF], query[HALF:]).astype(BF16)
        bottom[index] = masked(dot_nt(key[HALF:], query[HALF:]), False)
    done[...] = jnp.zeros_like(done)


def attend_half(core, owned, queries, intra, normed, gain, state, attn_out):
    squares = products = None
    for index in range(OWNED):
        columns, here = head_columns(core, owned, index), local_columns(index)
        out = intra[:, here] + times_state(queries[:, columns], state[index, :DH])
        attn_out[:, here] = out
        square = out * out
        product = out * (normed[:, here] * gain[:, columns])
        squares = square if squares is None else squares + square
        products = product if products is None else products + product
    return squares, products


def attend_own_kernel(core, queries, intra, normed, gain, state, attn_out, squares, products):
    squares[...], products[...] = attend_half(core, True, queries, intra, normed, gain, state, attn_out)


def attend_other_kernel(core, queries, intra, normed, gain, state, squares, products, attn_out, sums):
    found = attend_half(core, False, queries, intra, normed, gain, state, attn_out)
    for which, (acc, more) in enumerate(zip((squares, products), found)):
        total = acc[...] + more
        for part in range(BLOCK // DH):
            turned = total[part * DH:(part + 1) * DH, :].T
            place = which * (BLOCK // DH) + part
            sums[place:place + 1, :] = jnp.sum(turned, axis=0, keepdims=True)


def grads_half(core, owned, queries, attn_out, normed, gain, scale, cubes, grad, states):
    for index in range(OWNED):
        columns, here = head_columns(core, owned, index), local_columns(index)
        out, rate, one = attn_out[:, here], scale[...], normed[:, here]
        part = (rate * (one * gain[:, columns]) - out * cubes[...]).astype(BF16)
        grad[:, here] = part
        states[index, :DH] = dot_tn(queries[:, columns], part)
        row = jnp.sum(one * out * rate, axis=0, keepdims=True)
        states[index, DH:] = jnp.broadcast_to(row, (EXTRA, DH))


def add_kernel(core, one, other, *done_and_total):
    done_and_total[-1][...] = one[...] + other[...]


def grads_theirs_kernel(core, pair, other_pair, turned_done, early_done, queries, attn_out, normed, gain,
                        grad, scale, cubes, theirs):
    whole = pair[...] + other_pair[...]
    for part in range(BLOCK // DH):
        rows = slice(part * DH, (part + 1) * DH)
        mean_square = whole[part:part + 1, :] / FEATURES
        mean_prod = whole[part + 4:part + 5, :] / FEATURES
        one = lax.rsqrt(mean_square + EPSILON)
        scale[rows, :] = jnp.broadcast_to(one, (DH, DH)).T
        cubes[rows, :] = jnp.broadcast_to(one * one * one * mean_prod, (DH, DH)).T
    grads_half(core, False, queries, attn_out, normed, gain, scale, cubes, grad, theirs)


def grads_mine_kernel(core, scale, cubes, queries, attn_out, normed, gain, grad, mine):
    grads_half(core, True, queries, attn_out, normed, gain, scale, cubes, grad, mine)


def each_head(core, *halves):
    for owned in (True, False):
        for index in range(OWNED):
            place = index if owned else OWNED + index
            arrays = [pair[0] if owned else pair[1] for pair in halves]
            yield head_columns(core, owned, index), local_columns(index), place, index, arrays


def early_kernel(owned, core, gate, attn_out, normed, gain, output, dgate, done):
    for index in range(OWNED):
        columns, here = head_columns(core, owned, index), local_columns(index)
        sig = jax.nn.sigmoid(gate[:, columns].astype(F32))
        scaled = attn_out[:, here] * gain[:, columns]
        output[:, here] = scaled * sig
        dgate[:, here] = normed[:, here] * scaled * (1.0 - sig)
    done[...] = jnp.zeros_like(done)


def outputs_kernel(core, scale, output_own, output_other, dgate_own, dgate_other, output, dgate, done):
    for columns, here, _, _, (early_output, early_dgate) in each_head(
        core, (output_own, output_other), (dgate_own, dgate_other)
    ):
        rate = scale[...]
        output[:, columns] = (early_output[:, here] * rate).astype(BF16)
        dgate[:, columns] = (early_dgate[:, here] * rate).astype(BF16)
    done[...] = jnp.zeros_like(done)


def copy_out(source, target, sem):
    copy = pltpu.make_async_copy(source, target, sem)
    copy.start()
    return copy


def query_kernel(core, keys, values, grad_own, grad_other, own, other, output_here,
                 grad_query, output, done, sem):
    copy = copy_out(output_here, output, sem)
    for columns, here, _, index, (grads, states) in each_head(core, (grad_own, grad_other), (own, other)):
        grad = grads[:, here]
        inter = times_state_t(grad, states[index, :DH])
        first, second = causal_product(grad, values[:, columns], keys[:, columns])
        grad_query[:HALF, columns] = (first + inter[:HALF]).astype(BF16)
        grad_query[HALF:, columns] = (second + inter[HALF:]).astype(BF16)
    done[...] = jnp.zeros_like(done)
    copy.wait()


def key_kernel(core, queries, values, grad_own, grad_other, dgate_here, key_own, key_other, dgate, done, sem):
    copy = copy_out(dgate_here, dgate, sem)
    for columns, here, _, _, (grads, part) in each_head(core, (grad_own, grad_other), (key_own, key_other)):
        first, second = anticausal_product(values[:, columns], grads[:, here], queries[:, columns])
        part[:HALF, here] = first
        part[HALF:, here] = second
    done[...] = jnp.zeros_like(done)
    copy.wait()


def value_kernel(core, grad_own, grad_other, top_own, top_other, bottom_own, bottom_other, query_here,
                 value_own, value_other, grad_query, sem):
    copy = copy_out(query_here, grad_query, sem)
    for _, here, _, index, (grads, top, bottom, part) in each_head(
        core, (grad_own, grad_other), (top_own, top_other), (bottom_own, bottom_other), (value_own, value_other)
    ):
        part[:HALF, here] = dot_nn(top[index], grads[:, here])
        part[HALF:, here] = dot_nn(bottom[index], grads[HALF:, here])
    copy.wait()


def last_half(owned, core, keys, values, part_key, part_value, states, grad_key, grad_value, key_buf, value_buf, sems):
    copies = []
    for index in range(OWNED):
        columns, here = head_columns(core, owned, index), local_columns(index)
        state = states[index, :DH]
        key_buf[index] = (part_key[:, here] + times_state_t(values[:, columns], state)).astype(BF16)
        value_buf[index] = (part_value[:, here] + times_state(keys[:, columns], state)).astype(BF16)
        for which, (buffer, target) in enumerate(((key_buf, grad_key), (value_buf, grad_value))):
            copy = pltpu.make_async_copy(buffer.at[index], target.at[:, columns], sems.at[which, index])
            copy.start()
            copies.append(copy)
    for copy in copies:
        copy.wait()


def last_own_kernel(core, keys, values, part_key, part_value, states, grad_key, grad_value, *scratch):
    last_half(True, core, keys, values, part_key, part_value, states, grad_key, grad_value, *scratch)


def last_other_kernel(core, keys, values, part_key, part_value, own, other, key_before, value_before,
                      grad_key, grad_value, dgain, dgain_buf, dgain_sem, *scratch):
    for owned, states in ((True, own), (False, other)):
        for index in range(OWNED):
            row = OWNED * (core[0] if owned else 1 - core[0]) + index
            dgain_buf[pl.ds(row, 1), :] = states[index, DH:DH + 1]
    copy = pltpu.make_async_copy(dgain_buf, dgain, dgain_sem)
    copy.start()
    last_half(False, core, keys, values, part_key, part_value, other, grad_key, grad_value, *scratch)
    copy.wait()


def piece_rows(place, rows):
    return slice(place * rows, place * rows + PIECE)


def pack_kernel(rows, reverse, core, mine, received, *done_and_results):
    *_, pieces, kept = done_and_results
    ahead = core[0] == (1 if reverse else 0)
    for head in range(OWNED):
        kept[head] = jnp.where(ahead, mine[head, :DH], received[head, :DH])
    for head in range(OWNED):
        for part in range(DH // PIECE):
            source = slice(part * PIECE, (part + 1) * PIECE)
            place = head * (DH // PIECE) + part
            pieces[piece_rows(place, rows)] = mine[head, source] + received[head, source]
            if rows > PIECE:
                last = place * rows + PIECE
                pieces[last:last + 1] = mine[head, DH:DH + 1] + received[head, DH:DH + 1]


def row_total_kernel(rows, core, pieces, total):
    whole = pieces[:rows]
    for chip in range(1, ROW):
        whole = whole + pieces[chip * rows:(chip + 1) * rows]
    total[...] = whole


def prefix_kernel(rows, reverse, column, pieces, neighbour, pair, other_pair, *done_and_sums):
    sums = done_and_sums[-1]
    odd, high = lax.rem(column[0], 2) == 1, column[0] >= 2
    take_one = jnp.logical_not(odd) if reverse else odd
    take_pair = jnp.logical_not(high) if reverse else high
    total = jnp.where(take_one, neighbour[:PIECE], 0.0) + jnp.where(take_pair, other_pair[:PIECE], 0.0)
    order = range(ROW - 1, -1, -1) if reverse else range(ROW)
    for chip in order:
        sums[piece_rows(chip, rows)] = total
        total = total + pieces[piece_rows(chip, rows)]
    if rows > PIECE:
        whole = pair[PIECE:] + other_pair[PIECE:]
        for chip in range(ROW):
            sums[chip * rows + PIECE:(chip + 1) * rows] = whole


def unpack_kernel(rows, reverse, core, back, kept, own, send):
    ahead = core[0] == (1 if reverse else 0)
    for head in range(OWNED):
        for part in range(DH // PIECE):
            target = slice(part * PIECE, (part + 1) * PIECE)
            state = back[piece_rows(head * (DH // PIECE) + part, rows)]
            both = state + kept[head, target]
            own[head, target] = jnp.where(ahead, state, both)
            send[head, target] = jnp.where(ahead, both, state)
        if rows > PIECE:
            last = head * (DH // PIECE) * rows + PIECE
            whole = jnp.broadcast_to(back[last:last + 1], (EXTRA, DH))
            own[head, DH:] = whole
            send[head, DH:] = whole


def device(column, row, core):
    return (column * ROW + row) * 2 + core


def moved(to_column):
    return [
        (device(y, z, c), device(to_column(y), z, c))
        for y in range(COLUMN) for z in range(ROW) for c in range(2)
    ]


CORES = [(i, i ^ 1) for i in range(2 * COLUMN * ROW)]
ROWS = [[device(y, z, c) for z in range(ROW)] for y in range(COLUMN) for c in range(2)]


def sums_beyond(core, column, mine, theirs, reverse, beside_first, beside_second, before=()):
    rows = PIECE + (1 if mine.shape[1] > DH else 0)
    flat = (ROW * rows, DH)

    def exchange(pieces):
        pieces = pieces.reshape(ROW, 1, rows * DH)
        return lax.all_to_all(pieces, "seq", 0, 0, axis_index_groups=ROWS).reshape(flat)

    received = lax.ppermute(theirs, "seq", CORES)
    pieces, kept = call(
        functools.partial(pack_kernel, rows, reverse), "pack", [shape(flat), shape((OWNED, DH, DH))],
        core, mine, received, *before,
    )
    pieces = exchange(pieces)
    (total,) = call(functools.partial(row_total_kernel, rows), "row_total", [shape((rows, DH))], core, pieces)
    neighbour = lax.ppermute(total, "seq", moved(lambda y: y ^ 1))
    first = beside_first()
    (pair,) = call(add_kernel, "pair_total", [shape((rows, DH))], core, total, neighbour, first)
    other_pair = lax.ppermute(pair, "seq", moved(lambda y: COLUMN - 1 - y))
    second = beside_second()
    (sums,) = call(
        functools.partial(prefix_kernel, rows, reverse), "prefix", [shape(flat)],
        column, pieces, neighbour, pair, other_pair, *second,
    )
    own, send = call(
        functools.partial(unpack_kernel, rows, reverse), "unpack", [shape(mine.shape)] * 2,
        core, exchange(sums), kept,
    )
    return own, lax.ppermute(send, "seq", CORES)


def body(queries, keys, values, gate, gain, dout):
    index = lax.axis_index("seq").astype(jnp.int32)
    core = lax.rem(index, 2).reshape(1)
    column = lax.div(index, 2 * ROW).reshape(1)
    gain_row = gain.reshape(1, WIDE)
    half = shape((BLOCK, HALF_WIDE))
    half_low = shape((BLOCK, HALF_WIDE), BF16)
    wide = shape((BLOCK, WIDE), BF16)
    tokens = shape((BLOCK, DH))
    with_gain = shape((OWNED, DH + EXTRA, DH))
    done = shape((8, DH))

    state = shape((OWNED, DH, DH))
    whole = pltpu.VMEM((BLOCK, WIDE), BF16)
    theirs, mine = call(
        states_kernel, "states", [state, state], core, column, keys, values,
        ins=[smem()] + [hbm()] * 2,
        scratch=[whole, whole, pltpu.SemaphoreType.DMA((2, PARTS))],
        limit=FIRST_LIMIT,
    )

    intra = {}

    def intra_part(owned):
        name = "intra_own" if owned else "intra_other"
        intra[owned], ended = call(
            functools.partial(intra_kernel, owned), name, [half, done], core, queries, keys, values,
        )
        return ended

    normed_own, normed_other, gain_row, gates_done = call(
        gates_kernel, "gates", [half, half, shape((1, WIDE)), done], core, gate, dout, gain_row,
    )
    own, other = sums_beyond(
        core, column, mine, theirs, False,
        lambda: intra_part(True), lambda: (intra_part(False), gates_done),
    )
    intra_own, intra_other = intra[True], intra[False]
    out_own, squares, products = call(
        attend_own_kernel, "attend_own", [half, tokens, tokens],
        core, queries, intra_own, normed_own, gain_row, own,
    )
    out_other, sums = call(
        attend_other_kernel, "attend_other", [half, done],
        core, queries, intra_other, normed_other, gain_row, other, squares, products,
    )

    turned = {}

    def turned_part(owned):
        name = "turned_own" if owned else "turned_other"
        *turned[owned], ended = call(
            functools.partial(turned_kernel, owned), name,
            [shape((OWNED, HALF, BLOCK), BF16), shape((OWNED, HALF, HALF), BF16), done],
            core, queries, keys,
        )
        return ended

    early = {}

    def early_part(owned, attn_out, normed):
        name = "early_own" if owned else "early_other"
        *early[owned], ended = call(
            functools.partial(early_kernel, owned), name, [half, half, done],
            core, gate, attn_out, normed, gain_row,
        )
        return ended

    ring = lax.axis_size("head")
    neighbour = lax.ppermute(sums, "head", [(i, i ^ 1) for i in range(ring)])
    (pair,) = call(
        add_kernel, "pair_sums", [done],
        core, sums, neighbour, turned_part(True), early_part(True, out_own, normed_own),
    )
    other_pair = lax.ppermute(pair, "head", [(i, ring - 1 - i) for i in range(ring)])
    grad_other, scale, cubes, theirs = call(
        grads_theirs_kernel, "grads_theirs", [half_low, tokens, tokens, with_gain],
        core, pair, other_pair, turned_part(False), early_part(False, out_other, normed_other),
        queries, out_other, normed_other, gain_row,
    )
    grad_own, mine = call(
        grads_mine_kernel, "grads_mine", [half_low, with_gain],
        core, scale, cubes, queries, out_own, normed_own, gain_row,
    )
    output, dgate, outputs_done = call(
        outputs_kernel, "outputs", [wide, wide, done],
        core, scale, early[True][0], early[False][0], early[True][1], early[False][1],
    )

    results = {}

    one_copy = [pltpu.SemaphoreType.DMA]

    def query_part():
        *results["query"], ended = call(
            query_kernel, "grad_query", [wide, wide, done],
            core, keys, values, grad_own, grad_other, own, other, output,
            out_places=[vmem(), hbm(), vmem()],
            scratch=one_copy,
        )
        return ended

    def key_part():
        *results["key"], ended = call(
            key_kernel, "grad_key", [half, half, wide, done],
            core, queries, values, grad_own, grad_other, dgate,
            out_places=[vmem(), vmem(), hbm(), vmem()],
            scratch=one_copy,
        )
        return (ended,)

    later_own, later_other = sums_beyond(
        core, column, mine, theirs, True, query_part, key_part, (outputs_done,)
    )
    grad_query, output = results["query"]
    key_own, key_other, dgate = results["key"]
    value_own, value_other, grad_query = call(
        value_kernel, "grad_value", [half, half, wide],
        core, grad_own, grad_other, turned[True][0], turned[False][0], turned[True][1], turned[False][1],
        grad_query,
        out_places=[vmem(), vmem(), hbm()],
        scratch=one_copy,
    )
    buffer = pltpu.VMEM((OWNED, BLOCK, DH), BF16)
    scratch = [buffer, buffer, pltpu.SemaphoreType.DMA((2, OWNED))]
    grad_key, grad_value = call(
        last_own_kernel, "last_own", [wide, wide], core, keys, values, key_own, value_own, later_own,
        out_places=[hbm(), hbm()],
        scratch=scratch,
    )
    grad_key, grad_value, dgain = call(
        last_other_kernel, "last_other", [wide, wide, shape((HEADS_HERE, DH))],
        core, keys, values, key_other, value_other, later_own, later_other, grad_key, grad_value,
        ins=[vmem()] * 6 + [hbm()] * 2,
        out_places=[hbm()] * 3,
        scratch=[pltpu.VMEM((HEADS_HERE, DH), F32), pltpu.SemaphoreType.DMA] + scratch,
        aliases={7: 0, 8: 1},
    )
    return output, grad_query, grad_key, grad_value, dgate, dgain.reshape(WIDE)


def solution(mesh):
    wide = P("seq", "head")
    return jax.shard_map(
        body,
        mesh=mesh,
        in_specs=(wide, wide, wide, wide, P("head"), wide),
        out_specs=(wide, wide, wide, wide, wide, P("head")),
        check_vma=False,
    )
```

time: 109 us -> 106 us (0.972)
  blocking collectives: 65.9 us -> 56.2 us
  starting transfers between devices: 16.8 us -> 25.3 us
    all_to_all x4, blocking collectives: 65.9 us -> 56.2 us  [exchange(): lax.all_to_all(pieces, 'seq', 0, 0, axis_index_groups=ROWS).reshape(flat)]
    ppermute x7 -> x10, starting transfers between devices: 16.8 us -> 25.3 us  [the longest x2 8.09 us: sums_beyond(): return (own, lax.ppermute(send, 'seq', CORES))]
    ppermute x7 -> x10, waiting for transfers between devices: 3.34 us -> 2.51 us  [the longest x2 1.16 us: sums_beyond(): received = lax.ppermute(theirs, 'seq', CORES)]
    unnamed x12 -> x16, local copies, waits for them, and re-layouts: 3.14 us -> 2.47 us
    pallas_call x15 -> x29, Pallas kernels: 18.7 us -> 18.5 us  [call(): pl.pallas_call(kernel, in_specs=[smem()] + ins, out_specs=out_places, out...]
  transfers between devices with their start and end apart: 7 -> 10, of which waited for: 4 -> 5; matrix products, arithmetic and copies ran while one was open for 0% -> 0% of each run, Pallas kernels for 11% -> 13%
where the time goes in v3:
time: 106 us
  blocking collectives  56.2 us (53%)
  starting transfers between devices  25.3 us (24%)
  Pallas kernels  18.5 us (17%)
  waiting for transfers between devices  2.51 us (2%)
  local copies, waits for them, and re-layouts  2.47 us (2%)
  between operations  1.07 us (1%)
    all_to_all x4, blocking collectives, exchange(): lax.all_to_all(pieces, 'seq', 0, 0, axis_index_groups=ROWS).reshape(flat)  56.2 us
    pallas_call x29, Pallas kernels, call(): pl.pallas_call(kernel, in_specs=[smem()] + ins, out_specs=out_places, out...  18.5 us
    ppermute x2, starting transfers between devices, sums_beyond(): return (own, lax.ppermute(send, 'seq', CORES))  8.09 us
    ppermute x2, starting transfers between devices, sums_beyond(): received = lax.ppermute(theirs, 'seq', CORES)  6.25 us
    ppermute x2, starting transfers between devices, sums_beyond(): other_pair = lax.ppermute(pair, 'seq', moved(lambda y: COLUMN - 1 - y))  5.59 us
    ppermute x1, starting transfers between devices, body(): lax.ppermute(pair, 'head', [(i, ring - 1 - i) for i in range(ring)])  2.48 us
    unnamed x16, local copies, waits for them, and re-layouts  2.47 us
  transfers between devices with their start and end apart: 10, of which 5 were waited for; matrix products, arithmetic and copies ran while one was open for 0% of the time, Pallas kernels for 13%

profile of v3, /device:TPU:1, one launch (start us, length us, event | category | flops | bytes accessed | tf_op | source)
XLA Modules:
  0.0 106.0 jit_solution(13132245115200908500)
XLA Ops:
  0.6 1.2 %copy-done.1 = bf16[512,1024]{1,0:T(8,128)(2,1)S(1)} copy-done((bf16[512,1024]{1,0:T(8,128)(2,1)S(1)}, bf16[512,1024]{1,0:T(8,128)(2,1)}, u32[]{:S(2)}) %copy-start.1) | copy-done | bytes 1048600
  1.9 1.2 %copy-done.3 = bf16[512,1024]{1,0:T(8,128)(2,1)S(1)} copy-done((bf16[512,1024]{1,0:T(8,128)(2,1)S(1)}, bf16[512,1024]{1,0:T(8,128)(2,1)}, u32[]{:S(2)}) %copy-start.3) | copy-done | bytes 1048600
  3.1 1.0 states.1
  4.1 0.0 copy-start
  4.2 3.3 %collective-permute-start = (f32[4,128,128]{2,1,0:T(8,128)S(1)}, f32[4,128,128]{2,1,0:T(8,128)S(1)}, u32[]{:S(2)}, u32[]{:S(2)}) collective-permute-start(f32[4,128,128]{2,1,0:T(8,128)S(1)} %get-tuple-element.69), channel_id=1, source_target_pairs={{0,4},{4,0},{8,12},{12,8},{16,20},{20,16},{24,28},{28,24},{32,36},... | collective-permute-start | bytes 786440 | tf_op jit(solution)/shard_map/ppermute | solution.py:413
  7.5 1.2 %collective-permute-done.received = f32[4,128,128]{2,1,0:T(8,128)S(1)} collective-permute-done((f32[4,128,128]{2,1,0:T(8,128)S(1)}, f32[4,128,128]{2,1,0:T(8,128)S(1)}, u32[]{:S(2)}, u32[]{:S(2)}) %collective-permute-start) | collective-permute-done | bytes 262176 | tf_op jit(solution)/shard_map/ppermute | solution.py:413
  8.7 17.3 %all_to_all.20 = f32[8,1,8192]{2,1,0:T(1,128)S(1)} all-to-all(f32[8,1,8192]{2,1,0:T(1,128)S(1)} %bitcast.21), channel_id=1, replica_groups={{0,8,16,24,32,40,48,56},{4,12,20,28,36,44,52,60},{64,72,80,88,96,104,11..., dimensions={0} | all-to-all | bytes 524288 | tf_op jit(solution)/shard_map/all_to_all | solution.py:411
  26.0 1.4 %collective-permute-start.1 = (f32[64,128]{1,0:T(8,128)S(1)}, f32[64,128]{1,0:T(8,128)S(1)}, u32[]{:S(2)}, u32[]{:S(2)}) collective-permute-start(f32[64,128]{1,0:T(8,128)S(1)} %row_total.2.one), channel_id=1, source_target_pairs={{0,64},{4,68},{8,72},{12,76},{16,80},{20,84},{24,88},{28,92},{32,9... | collective-permute-start | bytes 98312 | tf_op jit(solution)/shard_map/ppermute | solution.py:420
  27.4 1.1 %intra_own.1 = (f32[512,512]{1,0:T(8,128)S(1)}, f32[8,128]{1,0:T(8,128)S(1)}) custom-call(s32[1]{0:T(128)} %bitcast.core, bf16[512,1024]{1,0:T(8,128)(2,1)S(1)} %copy-done, bf16[512,1024]{1,0:T(8,128)(2,1)S(1)} %copy-done.2, bf16[512,1024]{1,0:T(8,128)(2,1)S(1)} %copy-done.3), custom_call_target="tpu_custom_call" | custom-call | tf_op jit(solution)/shard_map/intra_own/pallas_call | solution.py:103
  28.5 0.4 collective-permute-done.1.other.neighbour
  28.9 0.0 copy-start.6
  28.9 2.8 %collective-permute-start.2 = (f32[64,128]{1,0:T(8,128)S(1)}, f32[64,128]{1,0:T(8,128)S(1)}, u32[]{:S(2)}, u32[]{:S(2)}) collective-permute-start(f32[64,128]{1,0:T(8,128)S(1)} %pair_total.2.pair), channel_id=1, source_target_pairs={{0,192},{4,196},{8,200},{12,204},{16,208},{20,212},{24,216},{28,22... | collective-permute-start | bytes 98312 | tf_op jit(solution)/shard_map/ppermute | solution.py:423
  31.7 1.1 %intra_other.1 = (f32[512,512]{1,0:T(8,128)S(1)}, f32[8,128]{1,0:T(8,128)S(1)}) custom-call(s32[1]{0:T(128)} %bitcast.core, bf16[512,1024]{1,0:T(8,128)(2,1)S(1)} %copy-done, bf16[512,1024]{1,0:T(8,128)(2,1)S(1)} %copy-done.2, bf16[512,1024]{1,0:T(8,128)(2,1)S(1)} %copy-done.3), custom_call_target="tpu_custom_call" | custom-call | tf_op jit(solution)/shard_map/intra_other/pallas_call | solution.py:103
  32.9 0.6 gates.1
  33.4 0.0 collective-permute-done.2.other_pair
  33.5 11.9 %all_to_all.21 = f32[8,1,8192]{2,1,0:T(1,128)S(1)} all-to-all(f32[8,1,8192]{2,1,0:T(1,128)S(1)} %bitcast.19), channel_id=1, replica_groups={{0,8,16,24,32,40,48,56},{4,12,20,28,36,44,52,60},{64,72,80,88,96,104,11..., dimensions={0} | all-to-all | bytes 524288 | tf_op jit(solution)/shard_map/all_to_all | solution.py:411
  45.4 4.7 %collective-permute-start.3 = (f32[4,128,128]{2,1,0:T(8,128)S(1)}, f32[4,128,128]{2,1,0:T(8,128)S(1)}, u32[]{:S(2)}, u32[]{:S(2)}) collective-permute-start(f32[4,128,128]{2,1,0:T(8,128)S(1)} %get-tuple-element.75), channel_id=1, source_target_pairs={{0,4},{4,0},{8,12},{12,8},{16,20},{20,16},{24,28},{28,24},{32,36},... | collective-permute-start | bytes 786440 | tf_op jit(solution)/shard_map/ppermute | solution.py:433
  50.1 0.5 attend_own.1
  50.6 0.7 collective-permute-done.3.state.other
  51.2 0.6 attend_other.1
  51.8 1.3 %collective-permute-start.4 = (f32[8,128]{1,0:T(8,128)S(1)}, f32[8,128]{1,0:T(8,128)S(1)}, u32[]{:S(2)}, u32[]{:S(2)}) collective-permute-start(f32[8,128]{1,0:T(8,128)S(1)} %get-tuple-element.81.one), channel_id=1, source_target_pairs={{0,1},{1,0},{2,3},{3,2},{4,5},{5,4},{6,7},{7,6},{8,9},{9,8},{10,11... | collective-permute-start | bytes 12296 | tf_op jit(solution)/shard_map/ppermute | solution.py:505
  53.1 0.6 turned_own.1
  53.7 0.5 early_own.1
  54.2 0.2 collective-permute-done.4.other
  54.4 2.5 %collective-permute-start.5 = (f32[8,128]{1,0:T(8,128)S(1)}, f32[8,128]{1,0:T(8,128)S(1)}, u32[]{:S(2)}, u32[]{:S(2)}) collective-permute-start(f32[8,128]{1,0:T(8,128)S(1)} %pair_sums.1.pair), channel_id=1, source_target_pairs={{0,3},{1,2},{2,1},{3,0},{4,7},{5,6},{6,5},{7,4},{8,11},{9,10},{10,... | collective-permute-start | bytes 12296 | tf_op jit(solution)/shard_map/ppermute | solution.py:510
  56.9 0.6 turned_other.1
  57.5 0.5 early_other.1
  57.9 0.1 collective-permute-done.5.other_pair
  58.1 0.8 grads_theirs.1
  58.9 2.9 %collective-permute-start.6 = (f32[4,136,128]{2,1,0:T(8,128)S(1)}, f32[4,136,128]{2,1,0:T(8,128)S(1)}, u32[]{:S(2)}, u32[]{:S(2)}) collective-permute-start(f32[4,136,128]{2,1,0:T(8,128)S(1)} %get-tuple-element.108), channel_id=1, source_target_pairs={{0,4},{4,0},{8,12},{12,8},{16,20},{20,16},{24,28},{28,24},{32,36},... | collective-permute-start | bytes 835592 | tf_op jit(solution)/shard_map/ppermute | solution.py:413
  61.8 0.7 grads_mine.1
  62.6 0.6 outputs.1
  63.2 0.0 copy-start.4
  63.2 0.0 collective-permute-done.6.received
  63.2 0.1 pack.3
  63.3 15.0 %all_to_all.22 = f32[8,1,8320]{2,1,0:T(1,128)S(1)} all-to-all(f32[8,1,8320]{2,1,0:T(1,128)S(1)} %bitcast.20), channel_id=1, replica_groups={{0,8,16,24,32,40,48,56},{4,12,20,28,36,44,52,60},{64,72,80,88,96,104,11..., dimensions={0} | all-to-all | bytes 532480 | tf_op jit(solution)/shard_map/all_to_all | solution.py:411
  78.3 0.2 collective-permute-start.7
  78.5 3.0 %grad_query.1 = (bf16[512,1024]{1,0:T(8,128)(2,1)S(1)}, bf16[512,1024]{1,0:T(8,128)(2,1)}, f32[8,128]{1,0:T(8,128)S(1)}) custom-call(s32[1]{0:T(128)} %bitcast.core, bf16[512,1024]{1,0:T(8,128)(2,1)S(1)} %copy-done.2, bf16[512,1024]{1,0:T(8,128)(2,1)S(1)} %copy-done.4, bf16[512,512]{1,0:T(8,128)(2,1)S(1)} %get-tuple-element.90.grad_own, ...), custom_call_target="tpu_custom_call" | custom-call | tf_op jit(solution)/shard_map/grad_query/pallas_call | solution.py:103
  81.5 0.0 collective-permute-done.7.other.neighbour
  81.5 2.8 %collective-permute-start.8 = (f32[65,128]{1,0:T(8,128)S(1)}, f32[65,128]{1,0:T(8,128)S(1)}, u32[]{:S(2)}, u32[]{:S(2)}) collective-permute-start(f32[65,128]{1,0:T(8,128)S(1)} %pair_total.3.pair), channel_id=1, source_target_pairs={{0,192},{4,196},{8,200},{12,204},{16,208},{20,212},{24,216},{28,22... | collective-permute-start | bytes 99848 | tf_op jit(solution)/shard_map/ppermute | solution.py:423
  84.3 2.0 %grad_key.1 = (f32[512,512]{1,0:T(8,128)S(1)}, f32[512,512]{1,0:T(8,128)S(1)}, bf16[512,1024]{1,0:T(8,128)(2,1)}, f32[8,128]{1,0:T(8,128)S(1)}) custom-call(s32[1]{0:T(128)} %bitcast.core, bf16[512,1024]{1,0:T(8,128)(2,1)S(1)} %copy-done, bf16[512,1024]{1,0:T(8,128)(2,1)S(1)} %copy-done.4, bf16[512,512]{1,0:T(8,128)(2,1)S(1)} %get-tuple-element.90.grad_own, ...), custom_call_target="tpu_custom_call" | custom-call | tf_op jit(solution)/shard_map/grad_key/pallas_call | solution.py:103
  86.2 0.0 collective-permute-done.8.other_pair
  86.3 12.0 %all_to_all.23 = f32[8,1,8320]{2,1,0:T(1,128)S(1)} all-to-all(f32[8,1,8320]{2,1,0:T(1,128)S(1)} %bitcast.16), channel_id=1, replica_groups={{0,8,16,24,32,40,48,56},{4,12,20,28,36,44,52,60},{64,72,80,88,96,104,11..., dimensions={0} | all-to-all | bytes 532480 | tf_op jit(solution)/shard_map/all_to_all | solution.py:411
  98.4 3.4 %collective-permute-start.9 = (f32[4,136,128]{2,1,0:T(8,128)S(1)}, f32[4,136,128]{2,1,0:T(8,128)S(1)}, u32[]{:S(2)}, u32[]{:S(2)}) collective-permute-start(f32[4,136,128]{2,1,0:T(8,128)S(1)} %get-tuple-element.115), channel_id=1, source_target_pairs={{0,4},{4,0},{8,12},{12,8},{16,20},{20,16},{24,28},{28,24},{32,36},... | collective-permute-start | bytes 835592 | tf_op jit(solution)/shard_map/ppermute | solution.py:433
  101.8 1.0 grad_value.1
  102.8 1.5 %last_own.1 = (bf16[512,1024]{1,0:T(8,128)(2,1)}, bf16[512,1024]{1,0:T(8,128)(2,1)}) custom-call(s32[1]{0:T(128)} %bitcast.core, bf16[512,1024]{1,0:T(8,128)(2,1)S(1)} %copy-done.2, bf16[512,1024]{1,0:T(8,128)(2,1)S(1)} %copy-done.4, f32[512,512]{1,0:T(8,128)S(1)} %get-tuple-element.116.part_key, f32[512,512]{1,0:T(8,128)S(1)} %get-tuple-element.117.part_value, ...), custom_call_target="tpu_custom_call" | custom-call | tf_op jit(solution)/shard_map/last_own/pallas_call | solution.py:103
  104.3 0.0 collective-permute-done.9.other
  104.3 1.5 %last_other.1 = (bf16[512,1024]{1,0:T(8,128)(2,1)}, bf16[512,1024]{1,0:T(8,128)(2,1)}, f32[8,128]{1,0:T(8,128)}) custom-call(s32[1]{0:T(128)} %bitcast.core, bf16[512,1024]{1,0:T(8,128)(2,1)S(1)} %copy-done.2, bf16[512,1024]{1,0:T(8,128)(2,1)S(1)} %copy-done.4, ...), custom_call_target="tpu_custom_call", output_to_operand_aliasing={{0}: (7, {}), {1}: (8, {})} | custom-call | tf_op jit(solution)/shard_map/last_other/pallas_call | solution.py:103
  (21 shorter events, 0.3 us)
Async XLA Ops:
  0.6 1.2 %copy-start.1 = (bf16[512,1024]{1,0:T(8,128)(2,1)S(1)}, bf16[512,1024]{1,0:T(8,128)(2,1)}, u32[]{:S(2)}) copy-start(bf16[512,1024]{1,0:T(8,128)(2,1)} %keys.15) | copy-start | bytes 3145732
  1.9 1.2 %copy-start.3 = (bf16[512,1024]{1,0:T(8,128)(2,1)S(1)}, bf16[512,1024]{1,0:T(8,128)(2,1)}, u32[]{:S(2)}) copy-start(bf16[512,1024]{1,0:T(8,128)(2,1)} %values.13) | copy-start | bytes 3145732
  3.1 24.3 %copy-start.2 = (bf16[512,1024]{1,0:T(8,128)(2,1)S(1)}, bf16[512,1024]{1,0:T(8,128)(2,1)}, u32[]{:S(2)}) copy-start(bf16[512,1024]{1,0:T(8,128)(2,1)} %keys.15) | copy-start | bytes 3145732
  4.1 23.3 %copy-start = (bf16[512,1024]{1,0:T(8,128)(2,1)S(1)}, bf16[512,1024]{1,0:T(8,128)(2,1)}, u32[]{:S(2)}) copy-start(bf16[512,1024]{1,0:T(8,128)(2,1)} %queries.17) | copy-start | bytes 3145732
  4.2 4.5 %collective-permute-start = (f32[4,128,128]{2,1,0:T(8,128)S(1)}, f32[4,128,128]{2,1,0:T(8,128)S(1)}, u32[]{:S(2)}, u32[]{:S(2)}) collective-permute-start(f32[4,128,128]{2,1,0:T(8,128)S(1)} %get-tuple-element.69), channel_id=1, source_target_pairs={{0,4},{4,0},{8,12},{12,8},{16,20},{20,16},{24,28},{28,24},{32,36},... | collective-permute-start | bytes 786440 | tf_op jit(solution)/shard_map/ppermute | solution.py:413
  26.0 2.9 %collective-permute-start.1 = (f32[64,128]{1,0:T(8,128)S(1)}, f32[64,128]{1,0:T(8,128)S(1)}, u32[]{:S(2)}, u32[]{:S(2)}) collective-permute-start(f32[64,128]{1,0:T(8,128)S(1)} %row_total.2.one), channel_id=1, source_target_pairs={{0,64},{4,68},{8,72},{12,76},{16,80},{20,84},{24,88},{28,92},{32,9... | collective-permute-start | bytes 98312 | tf_op jit(solution)/shard_map/ppermute | solution.py:420
  28.9 3.9 %copy-start.5 = (bf16[512,1024]{1,0:T(8,128)(2,1)S(1)}, bf16[512,1024]{1,0:T(8,128)(2,1)}, u32[]{:S(2)}) copy-start(bf16[512,1024]{1,0:T(8,128)(2,1)} %gate.5) | copy-start | bytes 3145732
  28.9 3.9 %copy-start.6 = (bf16[512,1024]{1,0:T(8,128)(2,1)S(1)}, bf16[512,1024]{1,0:T(8,128)(2,1)}, u32[]{:S(2)}) copy-start(bf16[512,1024]{1,0:T(8,128)(2,1)} %dout.1) | copy-start | bytes 3145732
  28.9 4.5 %collective-permute-start.2 = (f32[64,128]{1,0:T(8,128)S(1)}, f32[64,128]{1,0:T(8,128)S(1)}, u32[]{:S(2)}, u32[]{:S(2)}) collective-permute-start(f32[64,128]{1,0:T(8,128)S(1)} %pair_total.2.pair), channel_id=1, source_target_pairs={{0,192},{4,196},{8,200},{12,204},{16,208},{20,212},{24,216},{28,22... | collective-permute-start | bytes 98312 | tf_op jit(solution)/shard_map/ppermute | solution.py:423
  31.7 1.1 %copy-start.7 = (f32[1024]{0:T(1024)S(1)}, f32[1024]{0:T(1024)}, u32[]{:S(2)}) copy-start(f32[1024]{0:T(1024)} %param.10) | copy-start | bytes 12292
  45.4 5.8 %collective-permute-start.3 = (f32[4,128,128]{2,1,0:T(8,128)S(1)}, f32[4,128,128]{2,1,0:T(8,128)S(1)}, u32[]{:S(2)}, u32[]{:S(2)}) collective-permute-start(f32[4,128,128]{2,1,0:T(8,128)S(1)} %get-tuple-element.75), channel_id=1, source_target_pairs={{0,4},{4,0},{8,12},{12,8},{16,20},{20,16},{24,28},{28,24},{32,36},... | collective-permute-start | bytes 786440 | tf_op jit(solution)/shard_map/ppermute | solution.py:433
  51.8 2.5 %collective-permute-start.4 = (f32[8,128]{1,0:T(8,128)S(1)}, f32[8,128]{1,0:T(8,128)S(1)}, u32[]{:S(2)}, u32[]{:S(2)}) collective-permute-start(f32[8,128]{1,0:T(8,128)S(1)} %get-tuple-element.81.one), channel_id=1, source_target_pairs={{0,1},{1,0},{2,3},{3,2},{4,5},{5,4},{6,7},{7,6},{8,9},{9,8},{10,11... | collective-permute-start | bytes 12296 | tf_op jit(solution)/shard_map/ppermute | solution.py:505
  54.4 3.7 %collective-permute-start.5 = (f32[8,128]{1,0:T(8,128)S(1)}, f32[8,128]{1,0:T(8,128)S(1)}, u32[]{:S(2)}, u32[]{:S(2)}) collective-permute-start(f32[8,128]{1,0:T(8,128)S(1)} %pair_sums.1.pair), channel_id=1, source_target_pairs={{0,3},{1,2},{2,1},{3,0},{4,7},{5,6},{6,5},{7,4},{8,11},{9,10},{10,... | collective-permute-start | bytes 12296 | tf_op jit(solution)/shard_map/ppermute | solution.py:510
  58.9 4.3 %collective-permute-start.6 = (f32[4,136,128]{2,1,0:T(8,128)S(1)}, f32[4,136,128]{2,1,0:T(8,128)S(1)}, u32[]{:S(2)}, u32[]{:S(2)}) collective-permute-start(f32[4,136,128]{2,1,0:T(8,128)S(1)} %get-tuple-element.108), channel_id=1, source_target_pairs={{0,4},{4,0},{8,12},{12,8},{16,20},{20,16},{24,28},{28,24},{32,36},... | collective-permute-start | bytes 835592 | tf_op jit(solution)/shard_map/ppermute | solution.py:413
  63.2 15.2 %copy-start.4 = (bf16[512,1024]{1,0:T(8,128)(2,1)S(1)}, bf16[512,1024]{1,0:T(8,128)(2,1)}, u32[]{:S(2)}) copy-start(bf16[512,1024]{1,0:T(8,128)(2,1)} %values.13) | copy-start | bytes 3145732
  78.3 3.2 %collective-permute-start.7 = (f32[65,128]{1,0:T(8,128)S(1)}, f32[65,128]{1,0:T(8,128)S(1)}, u32[]{:S(2)}, u32[]{:S(2)}) collective-permute-start(f32[65,128]{1,0:T(8,128)S(1)} %row_total.3.one), channel_id=1, source_target_pairs={{0,64},{4,68},{8,72},{12,76},{16,80},{20,84},{24,88},{28,92},{32,9... | collective-permute-start | bytes 99848 | tf_op jit(solution)/shard_map/ppermute | solution.py:420
  81.5 4.8 %collective-permute-start.8 = (f32[65,128]{1,0:T(8,128)S(1)}, f32[65,128]{1,0:T(8,128)S(1)}, u32[]{:S(2)}, u32[]{:S(2)}) collective-permute-start(f32[65,128]{1,0:T(8,128)S(1)} %pair_total.3.pair), channel_id=1, source_target_pairs={{0,192},{4,196},{8,200},{12,204},{16,208},{20,212},{24,216},{28,22... | collective-permute-start | bytes 99848 | tf_op jit(solution)/shard_map/ppermute | solution.py:423
  98.4 5.9 %collective-permute-start.9 = (f32[4,136,128]{2,1,0:T(8,128)S(1)}, f32[4,136,128]{2,1,0:T(8,128)S(1)}, u32[]{:S(2)}, u32[]{:S(2)}) collective-permute-start(f32[4,136,128]{2,1,0:T(8,128)S(1)} %get-tuple-element.115), channel_id=1, source_target_pairs={{0,4},{4,0},{8,12},{12,8},{16,20},{20,16},{24,28},{28,24},{32,36},... | collective-permute-start | bytes 835592 | tf_op jit(solution)/shard_map/ppermute | solution.py:433

commit v4 on v3

--- a/solution.py
+++ b/solution.py
@@ -21,8 +21,6 @@
 F32 = jnp.float32
 BF16 = jnp.bfloat16
 MIB = 1024 * 1024
-FIRST_LIMIT = 8 * MIB
-PARTS = 4
 
 
 def dot_nn(a, b):
@@ -121,26 +119,17 @@
     return slice(index * DH, (index + 1) * DH)
 
 
-def states_kernel(core, column, keys, values, theirs, mine, key_buf, value_buf, sems):
-    copies = []
-    for part in range(PARTS):
-        rows = slice(part * BLOCK // PARTS, (part + 1) * BLOCK // PARTS)
-        pair = [
-            pltpu.make_async_copy(keys.at[rows], key_buf.at[rows], sems.at[0, part]),
-            pltpu.make_async_copy(values.at[rows], value_buf.at[rows], sems.at[1, part]),
-        ]
-        for copy in pair:
-            copy.start()
-        copies.append(pair)
-    for part in range(PARTS):
-        for copy in copies[part]:
-            copy.wait()
-        rows = slice(part * BLOCK // PARTS, (part + 1) * BLOCK // PARTS)
-        for owned, states in ((False, theirs), (True, mine)):
-            for index in range(OWNED):
-                columns = head_columns(core, owned, index)
-                state = dot_tn(key_buf[rows, columns], value_buf[rows, columns])
-                states[index] = state if part == 0 else states[index] + state
+def turn_keys_kernel(core, column, keys, turned):
+    for head in range(HEADS_HERE):
+        columns = local_columns(head)
+        turned[head] = keys[:, columns].T
+
+
+def states_kernel(core, turned, values, theirs, mine):
+    for owned, states in ((False, theirs), (True, mine)):
+        for index in range(OWNED):
+            head = OWNED * (core[0] if owned else 1 - core[0]) + index
+            states[index] = dot_nn(turned[head], values[:, head_columns(core, owned, index)])
 
 
 def intra_kernel(owned, core, queries, keys, values, intra, done):
@@ -288,13 +277,14 @@
 
 
 def value_kernel(core, grad_own, grad_other, top_own, top_other, bottom_own, bottom_other, query_here,
-                 value_own, value_other, grad_query, sem):
+                 value_own, value_other, grad_query, done, sem):
     copy = copy_out(query_here, grad_query, sem)
     for _, here, _, index, (grads, top, bottom, part) in each_head(
         core, (grad_own, grad_other), (top_own, top_other), (bottom_own, bottom_other), (value_own, value_other)
     ):
         part[:HALF, here] = dot_nn(top[index], grads[:, here])
         part[HALF:, here] = dot_nn(bottom[index], grads[HALF:, here])
+    done[...] = jnp.zeros_like(done)
     copy.wait()
 
 
@@ -343,9 +333,10 @@
             source = slice(part * PIECE, (part + 1) * PIECE)
             place = head * (DH // PIECE) + part
             pieces[piece_rows(place, rows)] = mine[head, source] + received[head, source]
-            if rows > PIECE:
-                last = place * rows + PIECE
-                pieces[last:last + 1] = mine[head, DH:DH + 1] + received[head, DH:DH + 1]
+    if rows > PIECE:
+        gains = [mine[head, DH:DH + 1] + received[head, DH:DH + 1] for head in range(OWNED)]
+        for place in range(ROW):
+            pieces[place * rows + PIECE:(place + 1) * rows] = jnp.concatenate(gains, axis=0)
 
 
 def row_total_kernel(rows, core, pieces, total):
@@ -355,34 +346,31 @@
     total[...] = whole
 
 
-def prefix_kernel(rows, reverse, column, pieces, neighbour, pair, other_pair, *done_and_sums):
-    sums = done_and_sums[-1]
+def prefix_kernel(rows, reverse, column, pieces, neighbour, pair, other_pair, *done_and_results):
+    *_, sums, gains = done_and_results
     odd, high = lax.rem(column[0], 2) == 1, column[0] >= 2
     take_one = jnp.logical_not(odd) if reverse else odd
     take_pair = jnp.logical_not(high) if reverse else high
     total = jnp.where(take_one, neighbour[:PIECE], 0.0) + jnp.where(take_pair, other_pair[:PIECE], 0.0)
     order = range(ROW - 1, -1, -1) if reverse else range(ROW)
     for chip in order:
-        sums[piece_rows(chip, rows)] = total
+        sums[piece_rows(chip, PIECE)] = total
         total = total + pieces[piece_rows(chip, rows)]
     if rows > PIECE:
-        whole = pair[PIECE:] + other_pair[PIECE:]
-        for chip in range(ROW):
-            sums[chip * rows + PIECE:(chip + 1) * rows] = whole
-
-
-def unpack_kernel(rows, reverse, core, back, kept, own, send):
+        gains[:OWNED] = pair[PIECE:] + other_pair[PIECE:]
+
+
+def unpack_kernel(rows, reverse, core, back, kept, gains, own, send):
     ahead = core[0] == (1 if reverse else 0)
     for head in range(OWNED):
         for part in range(DH // PIECE):
             target = slice(part * PIECE, (part + 1) * PIECE)
-            state = back[piece_rows(head * (DH // PIECE) + part, rows)]
+            state = back[piece_rows(head * (DH // PIECE) + part, PIECE)]
             both = state + kept[head, target]
             own[head, target] = jnp.where(ahead, state, both)
             send[head, target] = jnp.where(ahead, both, state)
         if rows > PIECE:
-            last = head * (DH // PIECE) * rows + PIECE
-            whole = jnp.broadcast_to(back[last:last + 1], (EXTRA, DH))
+            whole = jnp.broadcast_to(gains[head:head + 1], (EXTRA, DH))
             own[head, DH:] = whole
             send[head, DH:] = whole
 
@@ -403,16 +391,16 @@
 
 
 def sums_beyond(core, column, mine, theirs, reverse, beside_first, beside_second, before=()):
-    rows = PIECE + (1 if mine.shape[1] > DH else 0)
-    flat = (ROW * rows, DH)
+    rows = PIECE + (OWNED if mine.shape[1] > DH else 0)
 
     def exchange(pieces):
-        pieces = pieces.reshape(ROW, 1, rows * DH)
-        return lax.all_to_all(pieces, "seq", 0, 0, axis_index_groups=ROWS).reshape(flat)
+        high = pieces.shape[0]
+        pieces = pieces.reshape(ROW, 1, high // ROW * DH)
+        return lax.all_to_all(pieces, "seq", 0, 0, axis_index_groups=ROWS).reshape(high, DH)
 
     received = lax.ppermute(theirs, "seq", CORES)
     pieces, kept = call(
-        functools.partial(pack_kernel, rows, reverse), "pack", [shape(flat), shape((OWNED, DH, DH))],
+        functools.partial(pack_kernel, rows, reverse), "pack", [shape((ROW * rows, DH)), shape((OWNED, DH, DH))],
         core, mine, received, *before,
     )
     pieces = exchange(pieces)
@@ -422,13 +410,13 @@
     (pair,) = call(add_kernel, "pair_total", [shape((rows, DH))], core, total, neighbour, first)
     other_pair = lax.ppermute(pair, "seq", moved(lambda y: COLUMN - 1 - y))
     second = beside_second()
-    (sums,) = call(
-        functools.partial(prefix_kernel, rows, reverse), "prefix", [shape(flat)],
+    sums, gains = call(
+        functools.partial(prefix_kernel, rows, reverse), "prefix", [shape((ROW * PIECE, DH)), shape((8, DH))],
         column, pieces, neighbour, pair, other_pair, *second,
     )
     own, send = call(
         functools.partial(unpack_kernel, rows, reverse), "unpack", [shape(mine.shape)] * 2,
-        core, exchange(sums), kept,
+        core, exchange(sums), kept, gains,
     )
     return own, lax.ppermute(send, "seq", CORES)
 
@@ -446,13 +434,11 @@
     done = shape((8, DH))
 
     state = shape((OWNED, DH, DH))
-    whole = pltpu.VMEM((BLOCK, WIDE), BF16)
-    theirs, mine = call(
-        states_kernel, "states", [state, state], core, column, keys, values,
-        ins=[smem()] + [hbm()] * 2,
-        scratch=[whole, whole, pltpu.SemaphoreType.DMA((2, PARTS))],
-        limit=FIRST_LIMIT,
-    )
+    (turned_keys,) = call(
+        turn_keys_kernel, "turn_keys", [shape((HEADS_HERE, DH, BLOCK), BF16)], core, column, keys,
+        ins=[smem(), vmem()],
+    )
+    theirs, mine = call(states_kernel, "states", [state, state], core, turned_keys, values)
 
     intra = {}
 
@@ -542,20 +528,24 @@
             out_places=[vmem(), vmem(), hbm(), vmem()],
             scratch=one_copy,
         )
-        return (ended,)
+        return ended
+
+    def value_part():
+        *results["value"], ended = call(
+            value_kernel, "grad_value", [half, half, wide, done],
+            core, grad_own, grad_other, turned[True][0], turned[False][0], turned[True][1], turned[False][1],
+            results["query"][0],
+            out_places=[vmem(), vmem(), hbm(), vmem()],
+            scratch=one_copy,
+        )
+        return ended
 
     later_own, later_other = sums_beyond(
-        core, column, mine, theirs, True, query_part, key_part, (outputs_done,)
-    )
-    grad_query, output = results["query"]
+        core, column, mine, theirs, True, query_part, lambda: (key_part(), value_part()), (outputs_done,)
+    )
+    output = results["query"][1]
     key_own, key_other, dgate = results["key"]
-    value_own, value_other, grad_query = call(
-        value_kernel, "grad_value", [half, half, wide],
-        core, grad_own, grad_other, turned[True][0], turned[False][0], turned[True][1], turned[False][1],
-        grad_query,
-        out_places=[vmem(), vmem(), hbm()],
-        scratch=one_copy,
-    )
+    value_own, value_other, grad_query = results["value"]
     buffer = pltpu.VMEM((OWNED, BLOCK, DH), BF16)
     scratch = [buffer, buffer, pltpu.SemaphoreType.DMA((2, OWNED))]
     grad_key, grad_value = call(

time: 106 us -> 106 us (level)
    unnamed x16 -> x14, local copies, waits for them, and re-layouts: 2.47 us -> 2.14 us
    pallas_call x29 -> x30, Pallas kernels: 18.5 us -> 18.2 us  [call(): pl.pallas_call(kernel, in_specs=[smem()] + ins, out_specs=out_places, out...]
where the time goes in v4:
time: 106 us; the launch traced here: 105 us
  blocking collectives  56.4 us (53%)
  starting transfers between devices  25 us (24%)
  Pallas kernels  18.2 us (17%)
  waiting for transfers between devices  2.51 us (2%)
  local copies, waits for them, and re-layouts  2.14 us (2%)
  between operations  1.07 us (1%)
    all_to_all x4, blocking collectives, exchange(): lax.all_to_all(pieces, 'seq', 0, 0, axis_index_groups=ROWS)  56.4 us
    pallas_call x30, Pallas kernels, call(): pl.pallas_call(kernel, in_specs=[smem()] + ins, out_specs=out_places, out...  18.2 us
    ppermute x2, starting transfers between devices, sums_beyond(): return (own, lax.ppermute(send, 'seq', CORES))  7.8 us
    ppermute x2, starting transfers between devices, sums_beyond(): received = lax.ppermute(theirs, 'seq', CORES)  6.25 us
    ppermute x2, starting transfers between devices, sums_beyond(): other_pair = lax.ppermute(pair, 'seq', moved(lambda y: COLUMN - 1 - y))  5.58 us
    ppermute x1, starting transfers between devices, body(): lax.ppermute(pair, 'head', [(i, ring - 1 - i) for i in range(ring)])  2.48 us
    unnamed x14, local copies, waits for them, and re-layouts  2.14 us
  transfers between devices with their start and end apart: 10, of which 5 were waited for; matrix products, arithmetic and copies ran while one was open for 0% of the time, Pallas kernels for 13%

profile of v4, /device:TPU:1, one launch (start us, length us, event | category | flops | bytes accessed | tf_op | source)
XLA Modules:
  0.0 105.3 jit_solution(12572956560631753205)
XLA Ops:
  0.6 0.0 copy-start.1
  0.6 1.2 %copy-done.1 = bf16[512,1024]{1,0:T(8,128)(2,1)S(1)} copy-done((bf16[512,1024]{1,0:T(8,128)(2,1)S(1)}, bf16[512,1024]{1,0:T(8,128)(2,1)}, u32[]{:S(2)}) %copy-start.1) | copy-done | bytes 1048600
  1.9 0.3 turn_keys.1.turned
  2.2 0.9 copy-done.3
  3.1 0.5 states.1
  3.6 0.0 copy-start
  3.6 3.3 %collective-permute-start = (f32[4,128,128]{2,1,0:T(8,128)S(1)}, f32[4,128,128]{2,1,0:T(8,128)S(1)}, u32[]{:S(2)}, u32[]{:S(2)}) collective-permute-start(f32[4,128,128]{2,1,0:T(8,128)S(1)} %get-tuple-element.74), channel_id=1, source_target_pairs={{0,4},{4,0},{8,12},{12,8},{16,20},{20,16},{24,28},{28,24},{32,36},... | collective-permute-start | bytes 786440 | tf_op jit(solution)/shard_map/ppermute | solution.py:401
  6.9 1.2 %collective-permute-done.received = f32[4,128,128]{2,1,0:T(8,128)S(1)} collective-permute-done((f32[4,128,128]{2,1,0:T(8,128)S(1)}, f32[4,128,128]{2,1,0:T(8,128)S(1)}, u32[]{:S(2)}, u32[]{:S(2)}) %collective-permute-start) | collective-permute-done | bytes 262176 | tf_op jit(solution)/shard_map/ppermute | solution.py:401
  8.1 17.3 %all_to_all.20 = f32[8,1,8192]{2,1,0:T(1,128)S(1)} all-to-all(f32[8,1,8192]{2,1,0:T(1,128)S(1)} %bitcast.21), channel_id=1, replica_groups={{0,8,16,24,32,40,48,56},{4,12,20,28,36,44,52,60},{64,72,80,88,96,104,11..., dimensions={0} | all-to-all | bytes 524288 | tf_op jit(solution)/shard_map/all_to_all | solution.py:399
  25.5 1.4 %collective-permute-start.1 = (f32[64,128]{1,0:T(8,128)S(1)}, f32[64,128]{1,0:T(8,128)S(1)}, u32[]{:S(2)}, u32[]{:S(2)}) collective-permute-start(f32[64,128]{1,0:T(8,128)S(1)} %row_total.2.one), channel_id=1, source_target_pairs={{0,64},{4,68},{8,72},{12,76},{16,80},{20,84},{24,88},{28,92},{32,9... | collective-permute-start | bytes 98312 | tf_op jit(solution)/shard_map/ppermute | solution.py:408
  26.9 1.1 %intra_own.1 = (f32[512,512]{1,0:T(8,128)S(1)}, f32[8,128]{1,0:T(8,128)S(1)}) custom-call(s32[1]{0:T(128)} %bitcast.core, bf16[512,1024]{1,0:T(8,128)(2,1)S(1)} %copy-done, bf16[512,1024]{1,0:T(8,128)(2,1)S(1)} %copy-done.2, bf16[512,1024]{1,0:T(8,128)(2,1)S(1)} %copy-done.3), custom_call_target="tpu_custom_call" | custom-call | tf_op jit(solution)/shard_map/intra_own/pallas_call | solution.py:101
  28.0 0.4 collective-permute-done.1.other.neighbour
  28.3 0.0 copy-start.5
  28.4 2.8 %collective-permute-start.2 = (f32[64,128]{1,0:T(8,128)S(1)}, f32[64,128]{1,0:T(8,128)S(1)}, u32[]{:S(2)}, u32[]{:S(2)}) collective-permute-start(f32[64,128]{1,0:T(8,128)S(1)} %pair_total.2.pair), channel_id=1, source_target_pairs={{0,192},{4,196},{8,200},{12,204},{16,208},{20,212},{24,216},{28,22... | collective-permute-start | bytes 98312 | tf_op jit(solution)/shard_map/ppermute | solution.py:411
  31.2 1.1 %intra_other.1 = (f32[512,512]{1,0:T(8,128)S(1)}, f32[8,128]{1,0:T(8,128)S(1)}) custom-call(s32[1]{0:T(128)} %bitcast.core, bf16[512,1024]{1,0:T(8,128)(2,1)S(1)} %copy-done, bf16[512,1024]{1,0:T(8,128)(2,1)S(1)} %copy-done.2, bf16[512,1024]{1,0:T(8,128)(2,1)S(1)} %copy-done.3), custom_call_target="tpu_custom_call" | custom-call | tf_op jit(solution)/shard_map/intra_other/pallas_call | solution.py:101
  32.3 0.6 gates.1
  32.9 0.0 collective-permute-done.2.other_pair
  32.9 11.9 %all_to_all.21 = f32[8,1,8192]{2,1,0:T(1,128)S(1)} all-to-all(f32[8,1,8192]{2,1,0:T(1,128)S(1)} %bitcast.20), channel_id=1, replica_groups={{0,8,16,24,32,40,48,56},{4,12,20,28,36,44,52,60},{64,72,80,88,96,104,11..., dimensions={0} | all-to-all | bytes 524288 | tf_op jit(solution)/shard_map/all_to_all | solution.py:399
  44.8 4.7 %collective-permute-start.3 = (f32[4,128,128]{2,1,0:T(8,128)S(1)}, f32[4,128,128]{2,1,0:T(8,128)S(1)}, u32[]{:S(2)}, u32[]{:S(2)}) collective-permute-start(f32[4,128,128]{2,1,0:T(8,128)S(1)} %get-tuple-element.82), channel_id=1, source_target_pairs={{0,4},{4,0},{8,12},{12,8},{16,20},{20,16},{24,28},{28,24},{32,36},... | collective-permute-start | bytes 786440 | tf_op jit(solution)/shard_map/ppermute | solution.py:421
  49.5 0.5 attend_own.1
  50.0 0.7 collective-permute-done.3.state.other
  50.7 0.6 attend_other.1
  51.3 1.3 %collective-permute-start.4 = (f32[8,128]{1,0:T(8,128)S(1)}, f32[8,128]{1,0:T(8,128)S(1)}, u32[]{:S(2)}, u32[]{:S(2)}) collective-permute-start(f32[8,128]{1,0:T(8,128)S(1)} %get-tuple-element.88.one), channel_id=1, source_target_pairs={{0,1},{1,0},{2,3},{3,2},{4,5},{5,4},{6,7},{7,6},{8,9},{9,8},{10,11... | collective-permute-start | bytes 12296 | tf_op jit(solution)/shard_map/ppermute | solution.py:491
  52.6 0.6 turned_own.1
  53.2 0.5 early_own.1
  53.6 0.2 collective-permute-done.4.other
  53.8 2.5 %collective-permute-start.5 = (f32[8,128]{1,0:T(8,128)S(1)}, f32[8,128]{1,0:T(8,128)S(1)}, u32[]{:S(2)}, u32[]{:S(2)}) collective-permute-start(f32[8,128]{1,0:T(8,128)S(1)} %pair_sums.1.pair), channel_id=1, source_target_pairs={{0,3},{1,2},{2,1},{3,0},{4,7},{5,6},{6,5},{7,4},{8,11},{9,10},{10,... | collective-permute-start | bytes 12296 | tf_op jit(solution)/shard_map/ppermute | solution.py:496
  56.3 0.6 turned_other.1
  56.9 0.5 early_other.1
  57.4 0.1 collective-permute-done.5.other_pair
  57.5 0.8 grads_theirs.1
  58.3 2.9 %collective-permute-start.6 = (f32[4,136,128]{2,1,0:T(8,128)S(1)}, f32[4,136,128]{2,1,0:T(8,128)S(1)}, u32[]{:S(2)}, u32[]{:S(2)}) collective-permute-start(f32[4,136,128]{2,1,0:T(8,128)S(1)} %get-tuple-element.115), channel_id=1, source_target_pairs={{0,4},{4,0},{8,12},{12,8},{16,20},{20,16},{24,28},{28,24},{32,36},... | collective-permute-start | bytes 835592 | tf_op jit(solution)/shard_map/ppermute | solution.py:401
  61.3 0.7 grads_mine.1
  62.0 0.6 outputs.1
  62.6 0.0 collective-permute-done.6.received
  62.7 15.0 %all_to_all.22 = f32[8,1,8704]{2,1,0:T(1,128)S(1)} all-to-all(f32[8,1,8704]{2,1,0:T(1,128)S(1)} %bitcast.18), channel_id=1, replica_groups={{0,8,16,24,32,40,48,56},{4,12,20,28,36,44,52,60},{64,72,80,88,96,104,11..., dimensions={0} | all-to-all | bytes 557056 | tf_op jit(solution)/shard_map/all_to_all | solution.py:399
  77.8 0.2 collective-permute-start.7
  77.9 3.0 %grad_query.1 = (bf16[512,1024]{1,0:T(8,128)(2,1)S(1)}, bf16[512,1024]{1,0:T(8,128)(2,1)}, f32[8,128]{1,0:T(8,128)S(1)}) custom-call(s32[1]{0:T(128)} %bitcast.core, bf16[512,1024]{1,0:T(8,128)(2,1)S(1)} %copy-done.2, bf16[512,1024]{1,0:T(8,128)(2,1)S(1)} %copy-done.3, bf16[512,512]{1,0:T(8,128)(2,1)S(1)} %get-tuple-element.97.grad_own, ...), custom_call_target="tpu_custom_call" | custom-call | tf_op jit(solution)/shard_map/grad_query/pallas_call | solution.py:101
  80.9 0.0 collective-permute-done.7.other.neighbour
  81.0 2.8 %collective-permute-start.8 = (f32[68,128]{1,0:T(8,128)S(1)}, f32[68,128]{1,0:T(8,128)S(1)}, u32[]{:S(2)}, u32[]{:S(2)}) collective-permute-start(f32[68,128]{1,0:T(8,128)S(1)} %pair_total.3.pair), channel_id=1, source_target_pairs={{0,192},{4,196},{8,200},{12,204},{16,208},{20,212},{24,216},{28,22... | collective-permute-start | bytes 104456 | tf_op jit(solution)/shard_map/ppermute | solution.py:411
  83.7 2.0 %grad_key.1 = (f32[512,512]{1,0:T(8,128)S(1)}, f32[512,512]{1,0:T(8,128)S(1)}, bf16[512,1024]{1,0:T(8,128)(2,1)}, f32[8,128]{1,0:T(8,128)S(1)}) custom-call(s32[1]{0:T(128)} %bitcast.core, bf16[512,1024]{1,0:T(8,128)(2,1)S(1)} %copy-done, bf16[512,1024]{1,0:T(8,128)(2,1)S(1)} %copy-done.3, bf16[512,512]{1,0:T(8,128)(2,1)S(1)} %get-tuple-element.97.grad_own, ...), custom_call_target="tpu_custom_call" | custom-call | tf_op jit(solution)/shard_map/grad_key/pallas_call | solution.py:101
  85.7 1.0 grad_value.1
  86.7 0.0 collective-permute-done.8.other_pair
  86.8 12.2 %all_to_all.23 = f32[8,1,8192]{2,1,0:T(1,128)S(1)} all-to-all(f32[8,1,8192]{2,1,0:T(1,128)S(1)} %bitcast.19), channel_id=1, replica_groups={{0,8,16,24,32,40,48,56},{4,12,20,28,36,44,52,60},{64,72,80,88,96,104,11..., dimensions={0} | all-to-all | bytes 524288 | tf_op jit(solution)/shard_map/all_to_all | solution.py:399
  99.0 3.1 %collective-permute-start.9 = (f32[4,136,128]{2,1,0:T(8,128)S(1)}, f32[4,136,128]{2,1,0:T(8,128)S(1)}, u32[]{:S(2)}, u32[]{:S(2)}) collective-permute-start(f32[4,136,128]{2,1,0:T(8,128)S(1)} %get-tuple-element.125), channel_id=1, source_target_pairs={{0,4},{4,0},{8,12},{12,8},{16,20},{20,16},{24,28},{28,24},{32,36},... | collective-permute-start | bytes 835592 | tf_op jit(solution)/shard_map/ppermute | solution.py:421
  102.1 1.5 %last_own.1 = (bf16[512,1024]{1,0:T(8,128)(2,1)}, bf16[512,1024]{1,0:T(8,128)(2,1)}) custom-call(s32[1]{0:T(128)} %bitcast.core, bf16[512,1024]{1,0:T(8,128)(2,1)S(1)} %copy-done.2, bf16[512,1024]{1,0:T(8,128)(2,1)S(1)} %copy-done.3, f32[512,512]{1,0:T(8,128)S(1)} %get-tuple-element.126.part_key, f32[512,512]{1,0:T(8,128)S(1)} %get-tuple-element.127.part_value, ...), custom_call_target="tpu_custom_call" | custom-call | tf_op jit(solution)/shard_map/last_own/pallas_call | solution.py:101
  103.6 0.0 collective-permute-done.9.other
  103.6 1.5 %last_other.1 = (bf16[512,1024]{1,0:T(8,128)(2,1)}, bf16[512,1024]{1,0:T(8,128)(2,1)}, f32[8,128]{1,0:T(8,128)}) custom-call(s32[1]{0:T(128)} %bitcast.core, bf16[512,1024]{1,0:T(8,128)(2,1)S(1)} %copy-done.2, bf16[512,1024]{1,0:T(8,128)(2,1)S(1)} %copy-done.3, ...), custom_call_target="tpu_custom_call", output_to_operand_aliasing={{0}: (7, {}), {1}: (8, {})} | custom-call | tf_op jit(solution)/shard_map/last_other/pallas_call | solution.py:101
  (20 shorter events, 0.3 us)
Async XLA Ops:
  0.6 1.2 %copy-start.1 = (bf16[512,1024]{1,0:T(8,128)(2,1)S(1)}, bf16[512,1024]{1,0:T(8,128)(2,1)}, u32[]{:S(2)}) copy-start(bf16[512,1024]{1,0:T(8,128)(2,1)} %keys.15) | copy-start | bytes 3145732
  1.9 1.2 %copy-start.3 = (bf16[512,1024]{1,0:T(8,128)(2,1)S(1)}, bf16[512,1024]{1,0:T(8,128)(2,1)}, u32[]{:S(2)}) copy-start(bf16[512,1024]{1,0:T(8,128)(2,1)} %values.13) | copy-start | bytes 3145732
  3.1 23.8 %copy-start.2 = (bf16[512,1024]{1,0:T(8,128)(2,1)S(1)}, bf16[512,1024]{1,0:T(8,128)(2,1)}, u32[]{:S(2)}) copy-start(bf16[512,1024]{1,0:T(8,128)(2,1)} %keys.15) | copy-start | bytes 3145732
  3.6 23.3 %copy-start = (bf16[512,1024]{1,0:T(8,128)(2,1)S(1)}, bf16[512,1024]{1,0:T(8,128)(2,1)}, u32[]{:S(2)}) copy-start(bf16[512,1024]{1,0:T(8,128)(2,1)} %queries.17) | copy-start | bytes 3145732
  3.6 4.5 %collective-permute-start = (f32[4,128,128]{2,1,0:T(8,128)S(1)}, f32[4,128,128]{2,1,0:T(8,128)S(1)}, u32[]{:S(2)}, u32[]{:S(2)}) collective-permute-start(f32[4,128,128]{2,1,0:T(8,128)S(1)} %get-tuple-element.74), channel_id=1, source_target_pairs={{0,4},{4,0},{8,12},{12,8},{16,20},{20,16},{24,28},{28,24},{32,36},... | collective-permute-start | bytes 786440 | tf_op jit(solution)/shard_map/ppermute | solution.py:401
  25.5 2.9 %collective-permute-start.1 = (f32[64,128]{1,0:T(8,128)S(1)}, f32[64,128]{1,0:T(8,128)S(1)}, u32[]{:S(2)}, u32[]{:S(2)}) collective-permute-start(f32[64,128]{1,0:T(8,128)S(1)} %row_total.2.one), channel_id=1, source_target_pairs={{0,64},{4,68},{8,72},{12,76},{16,80},{20,84},{24,88},{28,92},{32,9... | collective-permute-start | bytes 98312 | tf_op jit(solution)/shard_map/ppermute | solution.py:408
  28.3 3.9 %copy-start.4 = (bf16[512,1024]{1,0:T(8,128)(2,1)S(1)}, bf16[512,1024]{1,0:T(8,128)(2,1)}, u32[]{:S(2)}) copy-start(bf16[512,1024]{1,0:T(8,128)(2,1)} %gate.5) | copy-start | bytes 3145732
  28.3 3.9 %copy-start.5 = (bf16[512,1024]{1,0:T(8,128)(2,1)S(1)}, bf16[512,1024]{1,0:T(8,128)(2,1)}, u32[]{:S(2)}) copy-start(bf16[512,1024]{1,0:T(8,128)(2,1)} %dout.1) | copy-start | bytes 3145732
  28.4 4.5 %collective-permute-start.2 = (f32[64,128]{1,0:T(8,128)S(1)}, f32[64,128]{1,0:T(8,128)S(1)}, u32[]{:S(2)}, u32[]{:S(2)}) collective-permute-start(f32[64,128]{1,0:T(8,128)S(1)} %pair_total.2.pair), channel_id=1, source_target_pairs={{0,192},{4,196},{8,200},{12,204},{16,208},{20,212},{24,216},{28,22... | collective-permute-start | bytes 98312 | tf_op jit(solution)/shard_map/ppermute | solution.py:411
  31.2 1.1 %copy-start.6 = (f32[1024]{0:T(1024)S(1)}, f32[1024]{0:T(1024)}, u32[]{:S(2)}) copy-start(f32[1024]{0:T(1024)} %param.10) | copy-start | bytes 12292
  44.8 5.8 %collective-permute-start.3 = (f32[4,128,128]{2,1,0:T(8,128)S(1)}, f32[4,128,128]{2,1,0:T(8,128)S(1)}, u32[]{:S(2)}, u32[]{:S(2)}) collective-permute-start(f32[4,128,128]{2,1,0:T(8,128)S(1)} %get-tuple-element.82), channel_id=1, source_target_pairs={{0,4},{4,0},{8,12},{12,8},{16,20},{20,16},{24,28},{28,24},{32,36},... | collective-permute-start | bytes 786440 | tf_op jit(solution)/shard_map/ppermute | solution.py:421
  51.3 2.5 %collective-permute-start.4 = (f32[8,128]{1,0:T(8,128)S(1)}, f32[8,128]{1,0:T(8,128)S(1)}, u32[]{:S(2)}, u32[]{:S(2)}) collective-permute-start(f32[8,128]{1,0:T(8,128)S(1)} %get-tuple-element.88.one), channel_id=1, source_target_pairs={{0,1},{1,0},{2,3},{3,2},{4,5},{5,4},{6,7},{7,6},{8,9},{9,8},{10,11... | collective-permute-start | bytes 12296 | tf_op jit(solution)/shard_map/ppermute | solution.py:491
  53.8 3.7 %collective-permute-start.5 = (f32[8,128]{1,0:T(8,128)S(1)}, f32[8,128]{1,0:T(8,128)S(1)}, u32[]{:S(2)}, u32[]{:S(2)}) collective-permute-start(f32[8,128]{1,0:T(8,128)S(1)} %pair_sums.1.pair), channel_id=1, source_target_pairs={{0,3},{1,2},{2,1},{3,0},{4,7},{5,6},{6,5},{7,4},{8,11},{9,10},{10,... | collective-permute-start | bytes 12296 | tf_op jit(solution)/shard_map/ppermute | solution.py:496
  58.3 4.3 %collective-permute-start.6 = (f32[4,136,128]{2,1,0:T(8,128)S(1)}, f32[4,136,128]{2,1,0:T(8,128)S(1)}, u32[]{:S(2)}, u32[]{:S(2)}) collective-permute-start(f32[4,136,128]{2,1,0:T(8,128)S(1)} %get-tuple-element.115), channel_id=1, source_target_pairs={{0,4},{4,0},{8,12},{12,8},{16,20},{20,16},{24,28},{28,24},{32,36},... | collective-permute-start | bytes 835592 | tf_op jit(solution)/shard_map/ppermute | solution.py:401
  77.8 3.2 %collective-permute-start.7 = (f32[68,128]{1,0:T(8,128)S(1)}, f32[68,128]{1,0:T(8,128)S(1)}, u32[]{:S(2)}, u32[]{:S(2)}) collective-permute-start(f32[68,128]{1,0:T(8,128)S(1)} %row_total.3.one), channel_id=1, source_target_pairs={{0,64},{4,68},{8,72},{12,76},{16,80},{20,84},{24,88},{28,92},{32,9... | collective-permute-start | bytes 104456 | tf_op jit(solution)/shard_map/ppermute | solution.py:408
  81.0 5.7 %collective-permute-start.8 = (f32[68,128]{1,0:T(8,128)S(1)}, f32[68,128]{1,0:T(8,128)S(1)}, u32[]{:S(2)}, u32[]{:S(2)}) collective-permute-start(f32[68,128]{1,0:T(8,128)S(1)} %pair_total.3.pair), channel_id=1, source_target_pairs={{0,192},{4,196},{8,200},{12,204},{16,208},{20,212},{24,216},{28,22... | collective-permute-start | bytes 104456 | tf_op jit(solution)/shard_map/ppermute | solution.py:411
  99.0 4.6 %collective-permute-start.9 = (f32[4,136,128]{2,1,0:T(8,128)S(1)}, f32[4,136,128]{2,1,0:T(8,128)S(1)}, u32[]{:S(2)}, u32[]{:S(2)}) collective-permute-start(f32[4,136,128]{2,1,0:T(8,128)S(1)} %get-tuple-element.125), channel_id=1, source_target_pairs={{0,4},{4,0},{8,12},{12,8},{16,20},{20,16},{24,28},{28,24},{32,36},... | collective-permute-start | bytes 835592 | tf_op jit(solution)/shard_map/ppermute | solution.py:421

commit v5 on v4

--- a/solution.py
+++ b/solution.py
@@ -132,31 +132,32 @@
             states[index] = dot_nn(turned[head], values[:, head_columns(core, owned, index)])
 
 
-def intra_kernel(owned, core, queries, keys, values, intra, done):
+def intra_kernel(owned, core, queries, keys, values, intra, *done):
     for index in range(OWNED):
         columns, here = head_columns(core, owned, index), local_columns(index)
         first, second = causal_product(queries[:, columns], keys[:, columns], values[:, columns])
         intra[:HALF, here] = first
         intra[HALF:, here] = second
-    done[...] = jnp.zeros_like(done)
-
-
-def gates_kernel(core, gate, dout, gain, normed_own, normed_other, gain_here, done):
+    for mark in done:
+        mark[...] = jnp.zeros_like(mark)
+
+
+def gates_kernel(core, gate, dout, gain, normed_own, normed_other, gain_here):
     for owned, normed in ((True, normed_own), (False, normed_other)):
         for index in range(OWNED):
             columns, here = head_columns(core, owned, index), local_columns(index)
             normed[:, here] = dout[:, columns].astype(F32) * jax.nn.sigmoid(gate[:, columns].astype(F32))
     gain_here[...] = gain[...]
-    done[...] = jnp.zeros_like(done)
-
-
-def turned_kernel(owned, core, queries, keys, top, bottom, done):
+
+
+def turned_kernel(owned, core, queries, keys, top, bottom, turned_query, done):
     for index in range(OWNED):
         columns = head_columns(core, owned, index)
         query, key = queries[:, columns], keys[:, columns]
         top[index, :, :HALF] = masked(dot_nt(key[:HALF], query[:HALF]), False)
         top[index, :, HALF:] = dot_nt(key[:HALF], query[HALF:]).astype(BF16)
         bottom[index] = masked(dot_nt(key[HALF:], query[HALF:]), False)
+        turned_query[index] = query.T
     done[...] = jnp.zeros_like(done)
 
 
@@ -187,13 +188,13 @@
             sums[place:place + 1, :] = jnp.sum(turned, axis=0, keepdims=True)
 
 
-def grads_half(core, owned, queries, attn_out, normed, gain, scale, cubes, grad, states):
+def grads_half(core, owned, turned_queries, attn_out, normed, gain, scale, cubes, grad, states):
     for index in range(OWNED):
         columns, here = head_columns(core, owned, index), local_columns(index)
         out, rate, one = attn_out[:, here], scale[...], normed[:, here]
         part = (rate * (one * gain[:, columns]) - out * cubes[...]).astype(BF16)
         grad[:, here] = part
-        states[index, :DH] = dot_tn(queries[:, columns], part)
+        states[index, :DH] = dot_nn(turned_queries[index], part)
         row = jnp.sum(one * out * rate, axis=0, keepdims=True)
         states[index, DH:] = jnp.broadcast_to(row, (EXTRA, DH))
 
@@ -202,7 +203,7 @@
     done_and_total[-1][...] = one[...] + other[...]
 
 
-def grads_theirs_kernel(core, pair, other_pair, turned_done, early_done, queries, attn_out, normed, gain,
+def grads_theirs_kernel(core, pair, other_pair, turned_done, early_done, turned_queries, attn_out, normed, gain,
                         grad, scale, cubes, theirs):
     whole = pair[...] + other_pair[...]
     for part in range(BLOCK // DH):
@@ -212,11 +213,11 @@
         one = lax.rsqrt(mean_square + EPSILON)
         scale[rows, :] = jnp.broadcast_to(one, (DH, DH)).T
         cubes[rows, :] = jnp.broadcast_to(one * one * one * mean_prod, (DH, DH)).T
-    grads_half(core, False, queries, attn_out, normed, gain, scale, cubes, grad, theirs)
-
-
-def grads_mine_kernel(core, scale, cubes, queries, attn_out, normed, gain, grad, mine):
-    grads_half(core, True, queries, attn_out, normed, gain, scale, cubes, grad, mine)
+    grads_half(core, False, turned_queries, attn_out, normed, gain, scale, cubes, grad, theirs)
+
+
+def grads_mine_kernel(core, scale, cubes, turned_queries, attn_out, normed, gain, grad, mine):
+    grads_half(core, True, turned_queries, attn_out, normed, gain, scale, cubes, grad, mine)
 
 
 def each_head(core, *halves):
@@ -254,24 +255,36 @@
 
 
 def query_kernel(core, keys, values, grad_own, grad_other, own, other, output_here,
-                 grad_query, output, done, sem):
+                 grad_query, left_own, left_other, right_own, right_other, output, done, sem):
     copy = copy_out(output_here, output, sem)
-    for columns, here, _, index, (grads, states) in each_head(core, (grad_own, grad_other), (own, other)):
-        grad = grads[:, here]
+    for columns, here, _, index, (grads, states, left, right) in each_head(
+        core, (grad_own, grad_other), (own, other), (left_own, left_other), (right_own, right_other)
+    ):
+        grad, value, key = grads[:, here], values[:, columns], keys[:, columns]
         inter = times_state_t(grad, states[index, :DH])
-        first, second = causal_product(grad, values[:, columns], keys[:, columns])
+        top = masked(dot_nt(grad[:HALF], value[:HALF]), True)
+        low = dot_nt(grad[HALF:], value[:HALF]).astype(BF16)
+        corner = masked(dot_nt(grad[HALF:], value[HALF:]), True)
+        left[index, :HALF] = top
+        left[index, HALF:] = low
+        right[index] = corner
+        first = dot_nn(top, key[:HALF])
+        second = dot_nn(jnp.concatenate([low, corner], axis=1), key)
         grad_query[:HALF, columns] = (first + inter[:HALF]).astype(BF16)
         grad_query[HALF:, columns] = (second + inter[HALF:]).astype(BF16)
     done[...] = jnp.zeros_like(done)
     copy.wait()
 
 
-def key_kernel(core, queries, values, grad_own, grad_other, dgate_here, key_own, key_other, dgate, done, sem):
+def key_kernel(core, queries, left_own, left_other, right_own, right_other, dgate_here,
+               key_own, key_other, dgate, done, sem):
     copy = copy_out(dgate_here, dgate, sem)
-    for columns, here, _, _, (grads, part) in each_head(core, (grad_own, grad_other), (key_own, key_other)):
-        first, second = anticausal_product(values[:, columns], grads[:, here], queries[:, columns])
-        part[:HALF, here] = first
-        part[HALF:, here] = second
+    for columns, here, _, index, (left, right, part) in each_head(
+        core, (left_own, left_other), (right_own, right_other), (key_own, key_other)
+    ):
+        query = queries[:, columns]
+        part[:HALF, here] = dot_tn(left[index], query)
+        part[HALF:, here] = dot_tn(right[index], query[HALF:])
     done[...] = jnp.zeros_like(done)
     copy.wait()
 
@@ -360,6 +373,16 @@
         gains[:OWNED] = pair[PIECE:] + other_pair[PIECE:]
 
 
+def chips_prefix_kernel(core, pieces, sums):
+    chips = COLUMN * ROW
+    height = OWNED * DH // chips
+    total = jnp.zeros((height, DH), F32)
+    for chip in range(chips):
+        rows = slice(chip * height, (chip + 1) * height)
+        sums[rows] = total
+        total = total + pieces[rows]
+
+
 def unpack_kernel(rows, reverse, core, back, kept, gains, own, send):
     ahead = core[0] == (1 if reverse else 0)
     for head in range(OWNED):
@@ -421,6 +444,28 @@
     return own, lax.ppermute(send, "seq", CORES)
 
 
+def sums_before(core, mine, theirs, before):
+    chips = COLUMN * ROW
+    groups = [[2 * i + one for i in range(chips)] for one in range(2)]
+    flat = (OWNED * DH, DH)
+
+    def exchange(pieces):
+        pieces = pieces.reshape(chips, 1, OWNED * DH // chips * DH)
+        return lax.all_to_all(pieces, "seq", 0, 0, axis_index_groups=groups).reshape(flat)
+
+    received = lax.ppermute(theirs, "seq", CORES)
+    pieces, kept = call(
+        functools.partial(pack_kernel, PIECE, False), "pack", [shape(flat), shape((OWNED, DH, DH))],
+        core, mine, received, before,
+    )
+    (sums,) = call(chips_prefix_kernel, "prefix", [shape(flat)], core, exchange(pieces))
+    own, send = call(
+        functools.partial(unpack_kernel, PIECE, False), "unpack", [shape(mine.shape)] * 2,
+        core, exchange(sums), kept, before,
+    )
+    return own, lax.ppermute(send, "seq", CORES)
+
+
 def body(queries, keys, values, gate, gain, dout):
     index = lax.axis_index("seq").astype(jnp.int32)
     core = lax.rem(index, 2).reshape(1)
@@ -440,23 +485,16 @@
     )
     theirs, mine = call(states_kernel, "states", [state, state], core, turned_keys, values)
 
-    intra = {}
-
-    def intra_part(owned):
-        name = "intra_own" if owned else "intra_other"
-        intra[owned], ended = call(
-            functools.partial(intra_kernel, owned), name, [half, done], core, queries, keys, values,
-        )
-        return ended
-
-    normed_own, normed_other, gain_row, gates_done = call(
-        gates_kernel, "gates", [half, half, shape((1, WIDE)), done], core, gate, dout, gain_row,
-    )
-    own, other = sums_beyond(
-        core, column, mine, theirs, False,
-        lambda: intra_part(True), lambda: (intra_part(False), gates_done),
-    )
-    intra_own, intra_other = intra[True], intra[False]
+    normed_own, normed_other, gain_row = call(
+        gates_kernel, "gates", [half, half, shape((1, WIDE))], core, gate, dout, gain_row,
+    )
+    intra_own, intra_done = call(
+        functools.partial(intra_kernel, True), "intra_own", [half, done], core, queries, keys, values,
+    )
+    own, other = sums_before(core, mine, theirs, intra_done)
+    (intra_other,) = call(
+        functools.partial(intra_kernel, False), "intra_other", [half], core, queries, keys, values,
+    )
     out_own, squares, products = call(
         attend_own_kernel, "attend_own", [half, tokens, tokens],
         core, queries, intra_own, normed_own, gain_row, own,
@@ -472,7 +510,8 @@
         name = "turned_own" if owned else "turned_other"
         *turned[owned], ended = call(
             functools.partial(turned_kernel, owned), name,
-            [shape((OWNED, HALF, BLOCK), BF16), shape((OWNED, HALF, HALF), BF16), done],
+            [shape((OWNED, HALF, BLOCK), BF16), shape((OWNED, HALF, HALF), BF16),
+             shape((OWNED, DH, BLOCK), BF16), done],
             core, queries, keys,
         )
         return ended
@@ -497,11 +536,11 @@
     grad_other, scale, cubes, theirs = call(
         grads_theirs_kernel, "grads_theirs", [half_low, tokens, tokens, with_gain],
         core, pair, other_pair, turned_part(False), early_part(False, out_other, normed_other),
-        queries, out_other, normed_other, gain_row,
+        turned[False][2], out_other, normed_other, gain_row,
     )
     grad_own, mine = call(
         grads_mine_kernel, "grads_mine", [half_low, with_gain],
-        core, scale, cubes, queries, out_own, normed_own, gain_row,
+        core, scale, cubes, turned[True][2], out_own, normed_own, gain_row,
     )
     output, dgate, outputs_done = call(
         outputs_kernel, "outputs", [wide, wide, done],
@@ -512,11 +551,13 @@
 
     one_copy = [pltpu.SemaphoreType.DMA]
 
+    left, right = shape((OWNED, BLOCK, HALF), BF16), shape((OWNED, HALF, HALF), BF16)
+
     def query_part():
         *results["query"], ended = call(
-            query_kernel, "grad_query", [wide, wide, done],
+            query_kernel, "grad_query", [wide, left, left, right, right, wide, done],
             core, keys, values, grad_own, grad_other, own, other, output,
-            out_places=[vmem(), hbm(), vmem()],
+            out_places=[vmem()] * 5 + [hbm(), vmem()],
             scratch=one_copy,
         )
         return ended
@@ -524,7 +565,7 @@
     def key_part():
         *results["key"], ended = call(
             key_kernel, "grad_key", [half, half, wide, done],
-            core, queries, values, grad_own, grad_other, dgate,
+            core, queries, *results["query"][1:5], dgate,
             out_places=[vmem(), vmem(), hbm(), vmem()],
             scratch=one_copy,
         )
@@ -543,7 +584,7 @@
     later_own, later_other = sums_beyond(
         core, column, mine, theirs, True, query_part, lambda: (key_part(), value_part()), (outputs_done,)
     )
-    output = results["query"][1]
+    output = results["query"][5]
     key_own, key_other, dgate = results["key"]
     value_own, value_other, grad_query = results["value"]
     buffer = pltpu.VMEM((OWNED, BLOCK, DH), BF16)

time: 106 us -> 103 us (0.972)
  starting transfers between devices: 25 us -> 19 us
  blocking collectives: 56.4 us -> 62.1 us
  waiting for transfers between devices: 2.51 us -> 1 us
    all_to_all x0 -> x2, blocking collectives: none -> 34.9 us  [exchange(): lax.all_to_all(pieces, 'seq', 0, 0, axis_index_groups=groups).reshape(flat)]
    all_to_all x4 -> x2, blocking collectives: 56.4 us -> 27.2 us  [exchange(): lax.all_to_all(pieces, 'seq', 0, 0, axis_index_groups=ROWS)]
    ppermute x0 -> x2, starting transfers between devices: none -> 7.01 us  [the longest x1 3.69 us: sums_before(): return (own, lax.ppermute(send, 'seq', CORES))]
    ppermute x2 -> x1, starting transfers between devices: 5.58 us -> 1.09 us  [sums_beyond(): other_pair = lax.ppermute(pair, 'seq', moved(lambda y: COLUMN - 1 - y))]
    ppermute x2 -> x1, starting transfers between devices: 7.8 us -> 3.78 us  [sums_beyond(): return (own, lax.ppermute(send, 'seq', CORES))]
    ppermute x2 -> x1, starting transfers between devices: 6.25 us -> 2.88 us  [sums_beyond(): received = lax.ppermute(theirs, 'seq', CORES)]
    ppermute x2 -> x1, waiting for transfers between devices: 1.16 us -> 0.01 us  [sums_beyond(): received = lax.ppermute(theirs, 'seq', CORES)]
    ppermute x2 -> x1, starting transfers between devices: 1.56 us -> 0.44 us  [sums_beyond(): neighbour = lax.ppermute(total, 'seq', moved(lambda y: y ^ 1))]
  transfers between devices with their start and end apart: 10 -> 8, of which waited for: 5 -> 4; matrix products, arithmetic and copies ran while one was open for 0% -> 0% of each run, Pallas kernels for 13% -> 13%
where the time goes in v5:
time: 103 us; the launch traced here: 102 us
  blocking collectives  62.1 us (60%)
  starting transfers between devices  19 us (18%)
  Pallas kernels  17.2 us (17%)
  local copies, waits for them, and re-layouts  2.14 us (2%)
  between operations  1.03 us (1%)
    all_to_all x2, blocking collectives, exchange(): lax.all_to_all(pieces, 'seq', 0, 0, axis_index_groups=groups).reshape(flat)  34.9 us
    all_to_all x2, blocking collectives, exchange(): lax.all_to_all(pieces, 'seq', 0, 0, axis_index_groups=ROWS)  27.2 us
    pallas_call x28, Pallas kernels, call(): pl.pallas_call(kernel, in_specs=[smem()] + ins, out_specs=out_places, out...  17.2 us
    ppermute x1, starting transfers between devices, sums_beyond(): return (own, lax.ppermute(send, 'seq', CORES))  3.78 us
    ppermute x1, starting transfers between devices, sums_before(): return (own, lax.ppermute(send, 'seq', CORES))  3.69 us
    ppermute x1, starting transfers between devices, sums_before(): received = lax.ppermute(theirs, 'seq', CORES)  3.33 us
    ppermute x1, starting transfers between devices, sums_beyond(): received = lax.ppermute(theirs, 'seq', CORES)  2.88 us
    ppermute x1, starting transfers between devices, body(): lax.ppermute(pair, 'head', [(i, ring - 1 - i) for i in range(ring)])  2.48 us
  transfers between devices with their start and end apart: 8, of which 4 were waited for; matrix products, arithmetic and copies ran while one was open for 0% of the time, Pallas kernels for 13%

profile of v5, /device:TPU:1, one launch (start us, length us, event | category | flops | bytes accessed | tf_op | source)
XLA Modules:
  0.0 102.5 jit_solution(1363090019987117122)
XLA Ops:
  0.6 0.0 copy-start
  0.6 1.2 %copy-done = bf16[512,1024]{1,0:T(8,128)(2,1)S(1)} copy-done((bf16[512,1024]{1,0:T(8,128)(2,1)S(1)}, bf16[512,1024]{1,0:T(8,128)(2,1)}, u32[]{:S(2)}) %copy-start) | copy-done | bytes 1048600
  1.9 0.3 turn_keys.1.turned
  2.2 0.9 copy-done.3
  3.1 0.5 states.1
  3.6 3.3 %collective-permute-start = (f32[4,128,128]{2,1,0:T(8,128)S(1)}, f32[4,128,128]{2,1,0:T(8,128)S(1)}, u32[]{:S(2)}, u32[]{:S(2)}) collective-permute-start(f32[4,128,128]{2,1,0:T(8,128)S(1)} %get-tuple-element.74), channel_id=1, source_target_pairs={{0,4},{4,0},{8,12},{12,8},{16,20},{20,16},{24,28},{28,24},{32,36},... | collective-permute-start | bytes 786440 | tf_op jit(solution)/shard_map/ppermute | solution.py:456
  6.9 0.0 copy-done.1
  6.9 0.0 copy-done.2
  6.9 1.1 %intra_own.1 = (f32[512,512]{1,0:T(8,128)S(1)}, f32[8,128]{1,0:T(8,128)S(1)}) custom-call(s32[1]{0:T(128)} %bitcast.core, bf16[512,1024]{1,0:T(8,128)(2,1)S(1)} %copy-done.2, bf16[512,1024]{1,0:T(8,128)(2,1)S(1)} %copy-done.1, bf16[512,1024]{1,0:T(8,128)(2,1)S(1)} %copy-done.3), custom_call_target="tpu_custom_call" | custom-call | tf_op jit(solution)/shard_map/intra_own/pallas_call | solution.py:101
  8.0 0.1 collective-permute-done.received
  8.1 0.1 pack.2
  8.1 19.2 %all_to_all.20 = f32[32,1,2048]{2,1,0:T(1,128)S(1)} all-to-all(f32[32,1,2048]{2,1,0:T(1,128)S(1)} %bitcast.20), channel_id=1, replica_groups={{0,8,16,24,32,40,48,56,64,72,80,88,96,104,112,120,128,136,144,152,160,1..., dimensions={0} | all-to-all | bytes 524288 | tf_op jit(solution)/shard_map/all_to_all | solution.py:454
  27.4 15.7 %all_to_all.21 = f32[32,1,2048]{2,1,0:T(1,128)S(1)} all-to-all(f32[32,1,2048]{2,1,0:T(1,128)S(1)} %bitcast.17), channel_id=1, replica_groups={{0,8,16,24,32,40,48,56,64,72,80,88,96,104,112,120,128,136,144,152,160,1..., dimensions={0} | all-to-all | bytes 524288 | tf_op jit(solution)/shard_map/all_to_all | solution.py:454
  43.1 0.0 copy-start.4
  43.2 0.0 copy-start.5
  43.2 3.7 %collective-permute-start.1 = (f32[4,128,128]{2,1,0:T(8,128)S(1)}, f32[4,128,128]{2,1,0:T(8,128)S(1)}, u32[]{:S(2)}, u32[]{:S(2)}) collective-permute-start(f32[4,128,128]{2,1,0:T(8,128)S(1)} %get-tuple-element.78), channel_id=1, source_target_pairs={{0,4},{4,0},{8,12},{12,8},{16,20},{20,16},{24,28},{28,24},{32,36},... | collective-permute-start | bytes 786440 | tf_op jit(solution)/shard_map/ppermute | solution.py:466
  46.9 1.1 %intra_other.1.intra = f32[512,512]{1,0:T(8,128)S(1)} custom-call(s32[1]{0:T(128)} %bitcast.core, bf16[512,1024]{1,0:T(8,128)(2,1)S(1)} %copy-done.2, bf16[512,1024]{1,0:T(8,128)(2,1)S(1)} %copy-done.1, bf16[512,1024]{1,0:T(8,128)(2,1)S(1)} %copy-done.3), custom_call_target="tpu_custom_call" | custom-call | tf_op jit(solution)/shard_map/intra_other/pallas_call | solution.py:101
  47.9 0.0 copy-done.4
  48.0 0.6 gates.1
  48.5 0.5 attend_own.1
  49.0 0.0 collective-permute-done.1.state.other
  49.0 0.6 attend_other.1
  49.6 1.3 %collective-permute-start.2 = (f32[8,128]{1,0:T(8,128)S(1)}, f32[8,128]{1,0:T(8,128)S(1)}, u32[]{:S(2)}, u32[]{:S(2)}) collective-permute-start(f32[8,128]{1,0:T(8,128)S(1)} %get-tuple-element.84.one), channel_id=1, source_target_pairs={{0,1},{1,0},{2,3},{3,2},{4,5},{5,4},{6,7},{7,6},{8,9},{9,8},{10,11... | collective-permute-start | bytes 12296 | tf_op jit(solution)/shard_map/ppermute | solution.py:530
  50.9 0.6 turned_own.1
  51.5 0.5 early_own.1
  52.0 0.2 collective-permute-done.2.other
  52.2 2.5 %collective-permute-start.3 = (f32[8,128]{1,0:T(8,128)S(1)}, f32[8,128]{1,0:T(8,128)S(1)}, u32[]{:S(2)}, u32[]{:S(2)}) collective-permute-start(f32[8,128]{1,0:T(8,128)S(1)} %pair_sums.1.pair), channel_id=1, source_target_pairs={{0,3},{1,2},{2,1},{3,0},{4,7},{5,6},{6,5},{7,4},{8,11},{9,10},{10,... | collective-permute-start | bytes 12296 | tf_op jit(solution)/shard_map/ppermute | solution.py:535
  54.7 0.6 turned_other.1
  55.2 0.5 early_other.1
  55.7 0.1 collective-permute-done.3.other_pair
  55.8 0.7 grads_theirs.1
  56.6 2.9 %collective-permute-start.4 = (f32[4,136,128]{2,1,0:T(8,128)S(1)}, f32[4,136,128]{2,1,0:T(8,128)S(1)}, u32[]{:S(2)}, u32[]{:S(2)}) collective-permute-start(f32[4,136,128]{2,1,0:T(8,128)S(1)} %get-tuple-element.117), channel_id=1, source_target_pairs={{0,4},{4,0},{8,12},{12,8},{16,20},{20,16},{24,28},{28,24},{32,36},... | collective-permute-start | bytes 835592 | tf_op jit(solution)/shard_map/ppermute | solution.py:424
  59.5 0.7 grads_mine.1
  60.1 0.7 outputs.1
  60.8 0.0 collective-permute-done.4.received
  60.9 15.4 %all_to_all.22 = f32[8,1,8704]{2,1,0:T(1,128)S(1)} all-to-all(f32[8,1,8704]{2,1,0:T(1,128)S(1)} %bitcast.18), channel_id=1, replica_groups={{0,8,16,24,32,40,48,56},{4,12,20,28,36,44,52,60},{64,72,80,88,96,104,11..., dimensions={0} | all-to-all | bytes 557056 | tf_op jit(solution)/shard_map/all_to_all | solution.py:422
  76.3 0.4 collective-permute-start.5
  76.7 2.7 %grad_query.1 = (bf16[512,1024]{1,0:T(8,128)(2,1)S(1)}, bf16[4,512,256]{2,1,0:T(8,128)(2,1)S(1)}, bf16[4,512,256]{2,1,0:T(8,128)(2,1)S(1)}, bf16[4,256,256]{2,1,...) custom-call(s32[1]{0:T(128)} %bitcast.core, ...), custom_call_target="tpu_custom_call" | custom-call | tf_op jit(solution)/shard_map/grad_query/pallas_call | solution.py:101
  79.4 0.0 collective-permute-done.5.other.neighbour
  79.5 1.1 %collective-permute-start.6 = (f32[68,128]{1,0:T(8,128)S(1)}, f32[68,128]{1,0:T(8,128)S(1)}, u32[]{:S(2)}, u32[]{:S(2)}) collective-permute-start(f32[68,128]{1,0:T(8,128)S(1)} %pair_total.1.pair), channel_id=1, source_target_pairs={{0,192},{4,196},{8,200},{12,204},{16,208},{20,212},{24,216},{28,22... | collective-permute-start | bytes 104456 | tf_op jit(solution)/shard_map/ppermute | solution.py:434
  80.6 1.0 grad_value.1
  81.5 1.4 %grad_key.1 = (f32[512,512]{1,0:T(8,128)S(1)}, f32[512,512]{1,0:T(8,128)S(1)}, bf16[512,1024]{1,0:T(8,128)(2,1)}, f32[8,128]{1,0:T(8,128)S(1)}) custom-call(s32[1]{0:T(128)} %bitcast.core, bf16[512,1024]{1,0:T(8,128)(2,1)S(1)} %copy-done.2, bf16[4,512,256]{2,1,0:T(8,128)(2,1)S(1)} %get-tuple-element.109.left_own, ...), custom_call_target="tpu_custom_call" | custom-call | tf_op jit(solution)/shard_map/grad_key/pallas_call | solution.py:101
  83.0 0.6 collective-permute-done.6.other_pair
  83.6 11.8 %all_to_all.23 = f32[8,1,8192]{2,1,0:T(1,128)S(1)} all-to-all(f32[8,1,8192]{2,1,0:T(1,128)S(1)} %bitcast.19), channel_id=1, replica_groups={{0,8,16,24,32,40,48,56},{4,12,20,28,36,44,52,60},{64,72,80,88,96,104,11..., dimensions={0} | all-to-all | bytes 524288 | tf_op jit(solution)/shard_map/all_to_all | solution.py:422
  95.5 3.8 %collective-permute-start.7 = (f32[4,136,128]{2,1,0:T(8,128)S(1)}, f32[4,136,128]{2,1,0:T(8,128)S(1)}, u32[]{:S(2)}, u32[]{:S(2)}) collective-permute-start(f32[4,136,128]{2,1,0:T(8,128)S(1)} %get-tuple-element.127), channel_id=1, source_target_pairs={{0,4},{4,0},{8,12},{12,8},{16,20},{20,16},{24,28},{28,24},{32,36},... | collective-permute-start | bytes 835592 | tf_op jit(solution)/shard_map/ppermute | solution.py:444
  99.2 1.5 %last_own.1 = (bf16[512,1024]{1,0:T(8,128)(2,1)}, bf16[512,1024]{1,0:T(8,128)(2,1)}) custom-call(s32[1]{0:T(128)} %bitcast.core, bf16[512,1024]{1,0:T(8,128)(2,1)S(1)} %copy-done.1, bf16[512,1024]{1,0:T(8,128)(2,1)S(1)} %copy-done.3, f32[512,512]{1,0:T(8,128)S(1)} %get-tuple-element.128.part_key, f32[512,512]{1,0:T(8,128)S(1)} %get-tuple-element.129.part_value, ...), custom_call_target="tpu_custom_call" | custom-call | tf_op jit(solution)/shard_map/last_own/pallas_call | solution.py:101
  100.7 0.0 collective-permute-done.7.other
  100.7 1.5 %last_other.1 = (bf16[512,1024]{1,0:T(8,128)(2,1)}, bf16[512,1024]{1,0:T(8,128)(2,1)}, f32[8,128]{1,0:T(8,128)}) custom-call(s32[1]{0:T(128)} %bitcast.core, bf16[512,1024]{1,0:T(8,128)(2,1)S(1)} %copy-done.1, bf16[512,1024]{1,0:T(8,128)(2,1)S(1)} %copy-done.3, ...), custom_call_target="tpu_custom_call", output_to_operand_aliasing={{0}: (7, {}), {1}: (8, {})} | custom-call | tf_op jit(solution)/shard_map/last_other/pallas_call | solution.py:101
  (14 shorter events, 0.2 us)
Async XLA Ops:
  0.6 1.2 %copy-start = (bf16[512,1024]{1,0:T(8,128)(2,1)S(1)}, bf16[512,1024]{1,0:T(8,128)(2,1)}, u32[]{:S(2)}) copy-start(bf16[512,1024]{1,0:T(8,128)(2,1)} %keys.15) | copy-start | bytes 3145732
  1.9 1.2 %copy-start.3 = (bf16[512,1024]{1,0:T(8,128)(2,1)S(1)}, bf16[512,1024]{1,0:T(8,128)(2,1)}, u32[]{:S(2)}) copy-start(bf16[512,1024]{1,0:T(8,128)(2,1)} %values.11) | copy-start | bytes 3145732
  3.1 3.8 %copy-start.1 = (bf16[512,1024]{1,0:T(8,128)(2,1)S(1)}, bf16[512,1024]{1,0:T(8,128)(2,1)}, u32[]{:S(2)}) copy-start(bf16[512,1024]{1,0:T(8,128)(2,1)} %keys.15) | copy-start | bytes 3145732
  3.1 3.8 %copy-start.2 = (bf16[512,1024]{1,0:T(8,128)(2,1)S(1)}, bf16[512,1024]{1,0:T(8,128)(2,1)}, u32[]{:S(2)}) copy-start(bf16[512,1024]{1,0:T(8,128)(2,1)} %queries.13) | copy-start | bytes 3145732
  3.6 4.5 %collective-permute-start = (f32[4,128,128]{2,1,0:T(8,128)S(1)}, f32[4,128,128]{2,1,0:T(8,128)S(1)}, u32[]{:S(2)}, u32[]{:S(2)}) collective-permute-start(f32[4,128,128]{2,1,0:T(8,128)S(1)} %get-tuple-element.74), channel_id=1, source_target_pairs={{0,4},{4,0},{8,12},{12,8},{16,20},{20,16},{24,28},{28,24},{32,36},... | collective-permute-start | bytes 786440 | tf_op jit(solution)/shard_map/ppermute | solution.py:456
  43.1 4.8 %copy-start.4 = (bf16[512,1024]{1,0:T(8,128)(2,1)S(1)}, bf16[512,1024]{1,0:T(8,128)(2,1)}, u32[]{:S(2)}) copy-start(bf16[512,1024]{1,0:T(8,128)(2,1)} %gate.5) | copy-start | bytes 3145732
  43.2 4.8 %copy-start.5 = (bf16[512,1024]{1,0:T(8,128)(2,1)S(1)}, bf16[512,1024]{1,0:T(8,128)(2,1)}, u32[]{:S(2)}) copy-start(bf16[512,1024]{1,0:T(8,128)(2,1)} %dout.1) | copy-start | bytes 3145732
  43.2 5.9 %collective-permute-start.1 = (f32[4,128,128]{2,1,0:T(8,128)S(1)}, f32[4,128,128]{2,1,0:T(8,128)S(1)}, u32[]{:S(2)}, u32[]{:S(2)}) collective-permute-start(f32[4,128,128]{2,1,0:T(8,128)S(1)} %get-tuple-element.78), channel_id=1, source_target_pairs={{0,4},{4,0},{8,12},{12,8},{16,20},{20,16},{24,28},{28,24},{32,36},... | collective-permute-start | bytes 786440 | tf_op jit(solution)/shard_map/ppermute | solution.py:466
  46.9 1.1 %copy-start.6 = (f32[1024]{0:T(1024)S(1)}, f32[1024]{0:T(1024)}, u32[]{:S(2)}) copy-start(f32[1024]{0:T(1024)} %param.10) | copy-start | bytes 12292
  49.6 2.5 %collective-permute-start.2 = (f32[8,128]{1,0:T(8,128)S(1)}, f32[8,128]{1,0:T(8,128)S(1)}, u32[]{:S(2)}, u32[]{:S(2)}) collective-permute-start(f32[8,128]{1,0:T(8,128)S(1)} %get-tuple-element.84.one), channel_id=1, source_target_pairs={{0,1},{1,0},{2,3},{3,2},{4,5},{5,4},{6,7},{7,6},{8,9},{9,8},{10,11... | collective-permute-start | bytes 12296 | tf_op jit(solution)/shard_map/ppermute | solution.py:530
  52.2 3.7 %collective-permute-start.3 = (f32[8,128]{1,0:T(8,128)S(1)}, f32[8,128]{1,0:T(8,128)S(1)}, u32[]{:S(2)}, u32[]{:S(2)}) collective-permute-start(f32[8,128]{1,0:T(8,128)S(1)} %pair_sums.1.pair), channel_id=1, source_target_pairs={{0,3},{1,2},{2,1},{3,0},{4,7},{5,6},{6,5},{7,4},{8,11},{9,10},{10,... | collective-permute-start | bytes 12296 | tf_op jit(solution)/shard_map/ppermute | solution.py:535
  56.6 4.2 %collective-permute-start.4 = (f32[4,136,128]{2,1,0:T(8,128)S(1)}, f32[4,136,128]{2,1,0:T(8,128)S(1)}, u32[]{:S(2)}, u32[]{:S(2)}) collective-permute-start(f32[4,136,128]{2,1,0:T(8,128)S(1)} %get-tuple-element.117), channel_id=1, source_target_pairs={{0,4},{4,0},{8,12},{12,8},{16,20},{20,16},{24,28},{28,24},{32,36},... | collective-permute-start | bytes 835592 | tf_op jit(solution)/shard_map/ppermute | solution.py:424
  76.3 3.1 %collective-permute-start.5 = (f32[68,128]{1,0:T(8,128)S(1)}, f32[68,128]{1,0:T(8,128)S(1)}, u32[]{:S(2)}, u32[]{:S(2)}) collective-permute-start(f32[68,128]{1,0:T(8,128)S(1)} %row_total.1.one), channel_id=1, source_target_pairs={{0,64},{4,68},{8,72},{12,76},{16,80},{20,84},{24,88},{28,92},{32,9... | collective-permute-start | bytes 104456 | tf_op jit(solution)/shard_map/ppermute | solution.py:431
  79.5 4.1 %collective-permute-start.6 = (f32[68,128]{1,0:T(8,128)S(1)}, f32[68,128]{1,0:T(8,128)S(1)}, u32[]{:S(2)}, u32[]{:S(2)}) collective-permute-start(f32[68,128]{1,0:T(8,128)S(1)} %pair_total.1.pair), channel_id=1, source_target_pairs={{0,192},{4,196},{8,200},{12,204},{16,208},{20,212},{24,216},{28,22... | collective-permute-start | bytes 104456 | tf_op jit(solution)/shard_map/ppermute | solution.py:434
  95.5 5.3 %collective-permute-start.7 = (f32[4,136,128]{2,1,0:T(8,128)S(1)}, f32[4,136,128]{2,1,0:T(8,128)S(1)}, u32[]{:S(2)}, u32[]{:S(2)}) collective-permute-start(f32[4,136,128]{2,1,0:T(8,128)S(1)} %get-tuple-element.127), channel_id=1, source_target_pairs={{0,4},{4,0},{8,12},{12,8},{16,20},{20,16},{24,28},{28,24},{32,36},... | collective-permute-start | bytes 835592 | tf_op jit(solution)/shard_map/ppermute | solution.py:444

commit v6 on v5

--- a/solution.py
+++ b/solution.py
@@ -57,10 +57,10 @@
     return jnp.where(keep, scores, 0.0).astype(BF16)
 
 
-def causal_product(a, b, values):
-    top = masked(dot_nt(a[:HALF], b[:HALF]), True)
-    left = dot_nt(a[HALF:], b[:HALF]).astype(BF16)
-    right = masked(dot_nt(a[HALF:], b[HALF:]), True)
+def causal_product(a, turned, values):
+    top = masked(dot_nn(a[:HALF], turned[:, :HALF]), True)
+    left = dot_nn(a[HALF:], turned[:, :HALF]).astype(BF16)
+    right = masked(dot_nn(a[HALF:], turned[:, HALF:]), True)
     first = dot_nn(top, values[:HALF])
     second = dot_nn(jnp.concatenate([left, right], axis=1), values)
     return first, second
@@ -95,7 +95,7 @@
     return pl.BlockSpec(memory_space=pltpu.HBM)
 
 
-def call(kernel, name, outs, core, *args, ins=None, out_places=None, scratch=(), limit=8 * MIB, aliases={}):
+def call(kernel, name, outs, core, *args, ins=None, out_places=None, scratch=(), limit=8 * MIB):
     ins = [vmem()] * len(args) if ins is None else ins
     out_places = [vmem()] * len(outs) if out_places is None else out_places
     return pl.pallas_call(
@@ -104,7 +104,6 @@
         out_specs=out_places,
         out_shape=outs,
         scratch_shapes=list(scratch),
-        input_output_aliases=aliases,
         compiler_params=pltpu.CompilerParams(vmem_limit_bytes=limit),
         name=name,
     )(core, *args)
@@ -132,10 +131,11 @@
             states[index] = dot_nn(turned[head], values[:, head_columns(core, owned, index)])
 
 
-def intra_kernel(owned, core, queries, keys, values, intra, *done):
-    for index in range(OWNED):
+def intra_kernel(owned, core, queries, turned_keys, values, intra, *done):
+    for index in range(OWNED):
+        head = OWNED * (core[0] if owned else 1 - core[0]) + index
         columns, here = head_columns(core, owned, index), local_columns(index)
-        first, second = causal_product(queries[:, columns], keys[:, columns], values[:, columns])
+        first, second = causal_product(queries[:, columns], turned_keys[head], values[:, columns])
         intra[:HALF, here] = first
         intra[HALF:, here] = second
     for mark in done:
@@ -276,9 +276,9 @@
     copy.wait()
 
 
-def key_kernel(core, queries, left_own, left_other, right_own, right_other, dgate_here,
-               key_own, key_other, dgate, done, sem):
-    copy = copy_out(dgate_here, dgate, sem)
+def key_kernel(core, queries, left_own, left_other, right_own, right_other, dgate_here, query_here,
+               key_own, key_other, dgate, grad_query, done, sems):
+    copies = [copy_out(dgate_here, dgate, sems.at[0]), copy_out(query_here, grad_query, sems.at[1])]
     for columns, here, _, index, (left, right, part) in each_head(
         core, (left_own, left_other), (right_own, right_other), (key_own, key_other)
     ):
@@ -286,50 +286,48 @@
         part[:HALF, here] = dot_tn(left[index], query)
         part[HALF:, here] = dot_tn(right[index], query[HALF:])
     done[...] = jnp.zeros_like(done)
-    copy.wait()
-
-
-def value_kernel(core, grad_own, grad_other, top_own, top_other, bottom_own, bottom_other, query_here,
-                 value_own, value_other, grad_query, done, sem):
-    copy = copy_out(query_here, grad_query, sem)
-    for _, here, _, index, (grads, top, bottom, part) in each_head(
-        core, (grad_own, grad_other), (top_own, top_other), (bottom_own, bottom_other), (value_own, value_other)
-    ):
-        part[:HALF, here] = dot_nn(top[index], grads[:, here])
-        part[HALF:, here] = dot_nn(bottom[index], grads[HALF:, here])
-    done[...] = jnp.zeros_like(done)
-    copy.wait()
-
-
-def last_half(owned, core, keys, values, part_key, part_value, states, grad_key, grad_value, key_buf, value_buf, sems):
-    copies = []
-    for index in range(OWNED):
-        columns, here = head_columns(core, owned, index), local_columns(index)
-        state = states[index, :DH]
-        key_buf[index] = (part_key[:, here] + times_state_t(values[:, columns], state)).astype(BF16)
-        value_buf[index] = (part_value[:, here] + times_state(keys[:, columns], state)).astype(BF16)
-        for which, (buffer, target) in enumerate(((key_buf, grad_key), (value_buf, grad_value))):
-            copy = pltpu.make_async_copy(buffer.at[index], target.at[:, columns], sems.at[which, index])
-            copy.start()
-            copies.append(copy)
     for copy in copies:
         copy.wait()
 
 
-def last_own_kernel(core, keys, values, part_key, part_value, states, grad_key, grad_value, *scratch):
-    last_half(True, core, keys, values, part_key, part_value, states, grad_key, grad_value, *scratch)
+def value_kernel(core, grad, top, bottom, part_value, *done):
+    for index in range(OWNED):
+        here = local_columns(index)
+        part_value[:HALF, here] = dot_nn(top[index], grad[:, here])
+        part_value[HALF:, here] = dot_nn(bottom[index], grad[HALF:, here])
+    for mark in done:
+        mark[...] = jnp.zeros_like(mark)
+
+
+def last_own_kernel(core, keys, values, part_key, part_value, states, grad_key, grad_value):
+    for index in range(OWNED):
+        columns, here = head_columns(core, True, index), local_columns(index)
+        state = states[index, :DH]
+        grad_key[:, here] = (part_key[:, here] + times_state_t(values[:, columns], state)).astype(BF16)
+        grad_value[:, here] = (part_value[:, here] + times_state(keys[:, columns], state)).astype(BF16)
 
 
 def last_other_kernel(core, keys, values, part_key, part_value, own, other, key_before, value_before,
-                      grad_key, grad_value, dgain, dgain_buf, dgain_sem, *scratch):
+                      grad_key, grad_value, dgain, key_buf, value_buf, dgain_buf, sems, own_sems, dgain_sem):
+    first = pl.ds(pl.multiple_of(core[0] * HALF_WIDE, HALF_WIDE), HALF_WIDE)
+    copies = [
+        copy_out(key_before, grad_key.at[:, first], own_sems.at[0]),
+        copy_out(value_before, grad_value.at[:, first], own_sems.at[1]),
+    ]
     for owned, states in ((True, own), (False, other)):
         for index in range(OWNED):
             row = OWNED * (core[0] if owned else 1 - core[0]) + index
             dgain_buf[pl.ds(row, 1), :] = states[index, DH:DH + 1]
-    copy = pltpu.make_async_copy(dgain_buf, dgain, dgain_sem)
-    copy.start()
-    last_half(False, core, keys, values, part_key, part_value, other, grad_key, grad_value, *scratch)
-    copy.wait()
+    copies.append(copy_out(dgain_buf, dgain, dgain_sem))
+    for index in range(OWNED):
+        columns, here = head_columns(core, False, index), local_columns(index)
+        state = other[index, :DH]
+        key_buf[index] = (part_key[:, here] + times_state_t(values[:, columns], state)).astype(BF16)
+        copies.append(copy_out(key_buf.at[index], grad_key.at[:, columns], sems.at[0, index]))
+        value_buf[index] = (part_value[:, here] + times_state(keys[:, columns], state)).astype(BF16)
+        copies.append(copy_out(value_buf.at[index], grad_value.at[:, columns], sems.at[1, index]))
+    for copy in copies:
+        copy.wait()
 
 
 def piece_rows(place, rows):
@@ -489,11 +487,11 @@
         gates_kernel, "gates", [half, half, shape((1, WIDE))], core, gate, dout, gain_row,
     )
     intra_own, intra_done = call(
-        functools.partial(intra_kernel, True), "intra_own", [half, done], core, queries, keys, values,
+        functools.partial(intra_kernel, True), "intra_own", [half, done], core, queries, turned_keys, values,
     )
     own, other = sums_before(core, mine, theirs, intra_done)
     (intra_other,) = call(
-        functools.partial(intra_kernel, False), "intra_other", [half], core, queries, keys, values,
+        functools.partial(intra_kernel, False), "intra_other", [half], core, queries, turned_keys, values,
     )
     out_own, squares, products = call(
         attend_own_kernel, "attend_own", [half, tokens, tokens],
@@ -564,20 +562,16 @@
 
     def key_part():
         *results["key"], ended = call(
-            key_kernel, "grad_key", [half, half, wide, done],
-            core, queries, *results["query"][1:5], dgate,
-            out_places=[vmem(), vmem(), hbm(), vmem()],
-            scratch=one_copy,
+            key_kernel, "grad_key", [half, half, wide, wide, done],
+            core, queries, *results["query"][1:5], dgate, results["query"][0],
+            out_places=[vmem(), vmem(), hbm(), hbm(), vmem()],
+            scratch=[pltpu.SemaphoreType.DMA((2,))],
         )
         return ended
 
     def value_part():
-        *results["value"], ended = call(
-            value_kernel, "grad_value", [half, half, wide, done],
-            core, grad_own, grad_other, turned[True][0], turned[False][0], turned[True][1], turned[False][1],
-            results["query"][0],
-            out_places=[vmem(), vmem(), hbm(), vmem()],
-            scratch=one_copy,
+        results["value"], ended = call(
+            value_kernel, "value_own", [half, done], core, grad_own, *turned[True][:2],
         )
         return ended
 
@@ -585,22 +579,21 @@
         core, column, mine, theirs, True, query_part, lambda: (key_part(), value_part()), (outputs_done,)
     )
     output = results["query"][5]
-    key_own, key_other, dgate = results["key"]
-    value_own, value_other, grad_query = results["value"]
+    key_own, key_other, dgate, grad_query = results["key"]
+    value_own = results["value"]
+    (value_other,) = call(value_kernel, "value_other", [half], core, grad_other, *turned[False][:2])
+    key_before, value_before = call(
+        last_own_kernel, "last_own", [half_low, half_low], core, keys, values, key_own, value_own, later_own,
+    )
     buffer = pltpu.VMEM((OWNED, BLOCK, DH), BF16)
-    scratch = [buffer, buffer, pltpu.SemaphoreType.DMA((2, OWNED))]
-    grad_key, grad_value = call(
-        last_own_kernel, "last_own", [wide, wide], core, keys, values, key_own, value_own, later_own,
-        out_places=[hbm(), hbm()],
-        scratch=scratch,
-    )
     grad_key, grad_value, dgain = call(
         last_other_kernel, "last_other", [wide, wide, shape((HEADS_HERE, DH))],
-        core, keys, values, key_other, value_other, later_own, later_other, grad_key, grad_value,
-        ins=[vmem()] * 6 + [hbm()] * 2,
+        core, keys, values, key_other, value_other, later_own, later_other, key_before, value_before,
         out_places=[hbm()] * 3,
-        scratch=[pltpu.VMEM((HEADS_HERE, DH), F32), pltpu.SemaphoreType.DMA] + scratch,
-        aliases={7: 0, 8: 1},
+        scratch=[
+            buffer, buffer, pltpu.VMEM((HEADS_HERE, DH), F32),
+            pltpu.SemaphoreType.DMA((2, OWNED)), pltpu.SemaphoreType.DMA((2,)), pltpu.SemaphoreType.DMA,
+        ],
     )
     return output, grad_query, grad_key, grad_value, dgate, dgain.reshape(WIDE)
 

time: 103 us -> 103 us (level)
    pallas_call x28 -> x29, Pallas kernels: 17.2 us -> 16.7 us  [call(): pl.pallas_call(kernel, in_specs=[smem()] + ins, out_specs=out_places, out...]
  transfers between devices with their start and end apart: 8 -> 8, of which waited for: 4 -> 4; matrix products, arithmetic and copies ran while one was open for 0% -> 0% of each run, Pallas kernels for 13% -> 12%
where the time goes in v6:
time: 103 us; the launch traced here: 102 us
  blocking collectives  62.2 us (60%)
  starting transfers between devices  18.8 us (18%)
  Pallas kernels  16.7 us (16%)
  local copies, waits for them, and re-layouts  2.14 us (2%)
  waiting for transfers between devices  1.35 us (1%)
  between operations  1.04 us (1%)
    all_to_all x2, blocking collectives, exchange(): lax.all_to_all(pieces, 'seq', 0, 0, axis_index_groups=groups).reshape(flat)  34.7 us
    all_to_all x2, blocking collectives, exchange(): lax.all_to_all(pieces, 'seq', 0, 0, axis_index_groups=ROWS)  27.4 us
    pallas_call x29, Pallas kernels, call(): pl.pallas_call(kernel, in_specs=[smem()] + ins, out_specs=out_places, out...  16.7 us
    ppermute x1, starting transfers between devices, sums_beyond(): return (own, lax.ppermute(send, 'seq', CORES))  3.72 us
    ppermute x1, starting transfers between devices, sums_before(): return (own, lax.ppermute(send, 'seq', CORES))  3.69 us
    ppermute x1, starting transfers between devices, sums_before(): received = lax.ppermute(theirs, 'seq', CORES)  3.33 us
    ppermute x1, starting transfers between devices, sums_beyond(): received = lax.ppermute(theirs, 'seq', CORES)  2.72 us
    ppermute x1, starting transfers between devices, body(): lax.ppermute(pair, 'head', [(i, ring - 1 - i) for i in range(ring)])  2.48 us
  transfers between devices with their start and end apart: 8, of which 4 were waited for; matrix products, arithmetic and copies ran while one was open for 0% of the time, Pallas kernels for 12%

profile of v6, /device:TPU:1, one launch (start us, length us, event | category | flops | bytes accessed | tf_op | source)
XLA Modules:
  0.0 102.2 jit_solution(9137962716198724474)
XLA Ops:
  0.6 0.0 copy-start.1
  0.6 1.2 %copy-done.1 = bf16[512,1024]{1,0:T(8,128)(2,1)S(1)} copy-done((bf16[512,1024]{1,0:T(8,128)(2,1)S(1)}, bf16[512,1024]{1,0:T(8,128)(2,1)}, u32[]{:S(2)}) %copy-start.1) | copy-done | bytes 1048600
  1.9 0.3 turn_keys.1.turned_keys.turned
  2.2 0.9 copy-done.3
  3.1 0.5 states.1
  3.6 3.3 %collective-permute-start = (f32[4,128,128]{2,1,0:T(8,128)S(1)}, f32[4,128,128]{2,1,0:T(8,128)S(1)}, u32[]{:S(2)}, u32[]{:S(2)}) collective-permute-start(f32[4,128,128]{2,1,0:T(8,128)S(1)} %get-tuple-element.73), channel_id=1, source_target_pairs={{0,4},{4,0},{8,12},{12,8},{16,20},{20,16},{24,28},{28,24},{32,36},... | collective-permute-start | bytes 786440 | tf_op jit(solution)/shard_map/ppermute | solution.py:454
  6.9 1.1 %intra_own.1 = (f32[512,512]{1,0:T(8,128)S(1)}, f32[8,128]{1,0:T(8,128)S(1)}) custom-call(s32[1]{0:T(128)} %bitcast.core, bf16[512,1024]{1,0:T(8,128)(2,1)S(1)} %copy-done, bf16[8,128,512]{2,1,0:T(8,128)(2,1)S(1)} %turn_keys.1.turned_keys.turned, bf16[512,1024]{1,0:T(8,128)(2,1)S(1)} %copy-done.3), custom_call_target="tpu_custom_call" | custom-call | tf_op jit(solution)/shard_map/intra_own/pallas_call | solution.py:101
  8.0 0.1 collective-permute-done.received
  8.1 0.1 pack.2
  8.1 18.9 %all_to_all.20 = f32[32,1,2048]{2,1,0:T(1,128)S(1)} all-to-all(f32[32,1,2048]{2,1,0:T(1,128)S(1)} %bitcast.20), channel_id=1, replica_groups={{0,8,16,24,32,40,48,56,64,72,80,88,96,104,112,120,128,136,144,152,160,1..., dimensions={0} | all-to-all | bytes 524288 | tf_op jit(solution)/shard_map/all_to_all | solution.py:452
  27.1 15.8 %all_to_all.21 = f32[32,1,2048]{2,1,0:T(1,128)S(1)} all-to-all(f32[32,1,2048]{2,1,0:T(1,128)S(1)} %bitcast.17), channel_id=1, replica_groups={{0,8,16,24,32,40,48,56,64,72,80,88,96,104,112,120,128,136,144,152,160,1..., dimensions={0} | all-to-all | bytes 524288 | tf_op jit(solution)/shard_map/all_to_all | solution.py:452
  43.0 0.0 copy-start.4
  43.0 0.0 copy-start.5
  43.0 3.7 %collective-permute-start.1 = (f32[4,128,128]{2,1,0:T(8,128)S(1)}, f32[4,128,128]{2,1,0:T(8,128)S(1)}, u32[]{:S(2)}, u32[]{:S(2)}) collective-permute-start(f32[4,128,128]{2,1,0:T(8,128)S(1)} %get-tuple-element.77), channel_id=1, source_target_pairs={{0,4},{4,0},{8,12},{12,8},{16,20},{20,16},{24,28},{28,24},{32,36},... | collective-permute-start | bytes 786440 | tf_op jit(solution)/shard_map/ppermute | solution.py:464
  46.7 1.1 %intra_other.1.intra = f32[512,512]{1,0:T(8,128)S(1)} custom-call(s32[1]{0:T(128)} %bitcast.core, bf16[512,1024]{1,0:T(8,128)(2,1)S(1)} %copy-done, bf16[8,128,512]{2,1,0:T(8,128)(2,1)S(1)} %turn_keys.1.turned_keys.turned, bf16[512,1024]{1,0:T(8,128)(2,1)S(1)} %copy-done.3), custom_call_target="tpu_custom_call" | custom-call | tf_op jit(solution)/shard_map/intra_other/pallas_call | solution.py:101
  47.8 0.6 gates.1
  48.3 0.5 attend_own.1
  48.8 0.0 collective-permute-done.1.state.other
  48.8 0.0 copy-start.2
  48.8 0.6 attend_other.1
  49.4 1.3 %collective-permute-start.2 = (f32[8,128]{1,0:T(8,128)S(1)}, f32[8,128]{1,0:T(8,128)S(1)}, u32[]{:S(2)}, u32[]{:S(2)}) collective-permute-start(f32[8,128]{1,0:T(8,128)S(1)} %get-tuple-element.83.one), channel_id=1, source_target_pairs={{0,1},{1,0},{2,3},{3,2},{4,5},{5,4},{6,7},{7,6},{8,9},{9,8},{10,11... | collective-permute-start | bytes 12296 | tf_op jit(solution)/shard_map/ppermute | solution.py:528
  50.7 0.6 turned_own.1
  51.3 0.5 early_own.1
  51.8 0.2 collective-permute-done.2.other
  52.0 2.5 %collective-permute-start.3 = (f32[8,128]{1,0:T(8,128)S(1)}, f32[8,128]{1,0:T(8,128)S(1)}, u32[]{:S(2)}, u32[]{:S(2)}) collective-permute-start(f32[8,128]{1,0:T(8,128)S(1)} %pair_sums.1.pair), channel_id=1, source_target_pairs={{0,3},{1,2},{2,1},{3,0},{4,7},{5,6},{6,5},{7,4},{8,11},{9,10},{10,... | collective-permute-start | bytes 12296 | tf_op jit(solution)/shard_map/ppermute | solution.py:533
  54.5 0.6 turned_other.1
  55.1 0.5 early_other.1
  55.5 0.1 collective-permute-done.3.other_pair
  55.6 0.7 grads_theirs.1
  56.4 2.7 %collective-permute-start.4 = (f32[4,136,128]{2,1,0:T(8,128)S(1)}, f32[4,136,128]{2,1,0:T(8,128)S(1)}, u32[]{:S(2)}, u32[]{:S(2)}) collective-permute-start(f32[4,136,128]{2,1,0:T(8,128)S(1)} %get-tuple-element.113), channel_id=1, source_target_pairs={{0,4},{4,0},{8,12},{12,8},{16,20},{20,16},{24,28},{28,24},{32,36},... | collective-permute-start | bytes 835592 | tf_op jit(solution)/shard_map/ppermute | solution.py:422
  59.1 0.7 grads_mine.1
  59.8 0.7 outputs.1
  60.5 0.0 collective-permute-done.4.received
  60.5 0.1 pack.3
  60.6 15.6 %all_to_all.22 = f32[8,1,8704]{2,1,0:T(1,128)S(1)} all-to-all(f32[8,1,8704]{2,1,0:T(1,128)S(1)} %bitcast.18), channel_id=1, replica_groups={{0,8,16,24,32,40,48,56},{4,12,20,28,36,44,52,60},{64,72,80,88,96,104,11..., dimensions={0} | all-to-all | bytes 557056 | tf_op jit(solution)/shard_map/all_to_all | solution.py:420
  76.2 0.4 collective-permute-start.5
  76.7 2.7 %grad_query.1 = (bf16[512,1024]{1,0:T(8,128)(2,1)S(1)}, bf16[4,512,256]{2,1,0:T(8,128)(2,1)S(1)}, bf16[4,512,256]{2,1,0:T(8,128)(2,1)S(1)}, bf16[4,256,256]{2,1,...) custom-call(s32[1]{0:T(128)} %bitcast.core, ...), custom_call_target="tpu_custom_call" | custom-call | tf_op jit(solution)/shard_map/grad_query/pallas_call | solution.py:101
  79.4 0.0 collective-permute-done.5.other.neighbour
  79.4 1.1 %collective-permute-start.6 = (f32[68,128]{1,0:T(8,128)S(1)}, f32[68,128]{1,0:T(8,128)S(1)}, u32[]{:S(2)}, u32[]{:S(2)}) collective-permute-start(f32[68,128]{1,0:T(8,128)S(1)} %pair_total.1.pair), channel_id=1, source_target_pairs={{0,192},{4,196},{8,200},{12,204},{16,208},{20,212},{24,216},{28,22... | collective-permute-start | bytes 104456 | tf_op jit(solution)/shard_map/ppermute | solution.py:432
  80.5 0.6 value_own.1
  81.1 1.5 %grad_key.1 = (f32[512,512]{1,0:T(8,128)S(1)}, f32[512,512]{1,0:T(8,128)S(1)}, bf16[512,1024]{1,0:T(8,128)(2,1)}, bf16[512,1024]{1,0:T(8,128)(2,1)}, f32[8,128]{1,0:T(8,128)S(1)}) custom-call(s32[1]{0:T(128)} %bitcast.core, bf16[512,1024]{1,0:T(8,128)(2,1)S(1)} %copy-done, bf16[4,512,256]{2,1,0:T(8,128)(2,1)S(1)} %get-tuple-element.102.left_own, ...), custom_call_target="tpu_custom_call" | custom-call | tf_op jit(solution)/shard_map/grad_key/pallas_call | solution.py:101
  82.6 1.0 collective-permute-done.6.other_pair
  83.5 11.8 %all_to_all.23 = f32[8,1,8192]{2,1,0:T(1,128)S(1)} all-to-all(f32[8,1,8192]{2,1,0:T(1,128)S(1)} %bitcast.19), channel_id=1, replica_groups={{0,8,16,24,32,40,48,56},{4,12,20,28,36,44,52,60},{64,72,80,88,96,104,11..., dimensions={0} | all-to-all | bytes 524288 | tf_op jit(solution)/shard_map/all_to_all | solution.py:420
  95.4 3.7 %collective-permute-start.7 = (f32[4,136,128]{2,1,0:T(8,128)S(1)}, f32[4,136,128]{2,1,0:T(8,128)S(1)}, u32[]{:S(2)}, u32[]{:S(2)}) collective-permute-start(f32[4,136,128]{2,1,0:T(8,128)S(1)} %get-tuple-element.125), channel_id=1, source_target_pairs={{0,4},{4,0},{8,12},{12,8},{16,20},{20,16},{24,28},{28,24},{32,36},... | collective-permute-start | bytes 835592 | tf_op jit(solution)/shard_map/ppermute | solution.py:442
  99.1 0.6 value_other.1.part_value
  99.7 0.7 last_own.1
  100.4 0.0 collective-permute-done.7.other
  100.4 1.6 %last_other.1 = (bf16[512,1024]{1,0:T(8,128)(2,1)}, bf16[512,1024]{1,0:T(8,128)(2,1)}, f32[8,128]{1,0:T(8,128)}) custom-call(s32[1]{0:T(128)} %bitcast.core, bf16[512,1024]{1,0:T(8,128)(2,1)S(1)} %copy-done.2, bf16[512,1024]{1,0:T(8,128)(2,1)S(1)} %copy-done.3, f32[512,512]{1,0:T(8,128)S(1)} %get-tuple-element.109.part_key, ...), custom_call_target="tpu_custom_call" | custom-call | tf_op jit(solution)/shard_map/last_other/pallas_call | solution.py:101
  (15 shorter events, 0.2 us)
Async XLA Ops:
  0.6 1.2 %copy-start.1 = (bf16[512,1024]{1,0:T(8,128)(2,1)S(1)}, bf16[512,1024]{1,0:T(8,128)(2,1)}, u32[]{:S(2)}) copy-start(bf16[512,1024]{1,0:T(8,128)(2,1)} %keys.11) | copy-start | bytes 3145732
  1.9 1.2 %copy-start.3 = (bf16[512,1024]{1,0:T(8,128)(2,1)S(1)}, bf16[512,1024]{1,0:T(8,128)(2,1)}, u32[]{:S(2)}) copy-start(bf16[512,1024]{1,0:T(8,128)(2,1)} %values.11) | copy-start | bytes 3145732
  3.1 3.8 %copy-start = (bf16[512,1024]{1,0:T(8,128)(2,1)S(1)}, bf16[512,1024]{1,0:T(8,128)(2,1)}, u32[]{:S(2)}) copy-start(bf16[512,1024]{1,0:T(8,128)(2,1)} %queries.13) | copy-start | bytes 3145732
  3.6 4.5 %collective-permute-start = (f32[4,128,128]{2,1,0:T(8,128)S(1)}, f32[4,128,128]{2,1,0:T(8,128)S(1)}, u32[]{:S(2)}, u32[]{:S(2)}) collective-permute-start(f32[4,128,128]{2,1,0:T(8,128)S(1)} %get-tuple-element.73), channel_id=1, source_target_pairs={{0,4},{4,0},{8,12},{12,8},{16,20},{20,16},{24,28},{28,24},{32,36},... | collective-permute-start | bytes 786440 | tf_op jit(solution)/shard_map/ppermute | solution.py:454
  43.0 4.8 %copy-start.4 = (bf16[512,1024]{1,0:T(8,128)(2,1)S(1)}, bf16[512,1024]{1,0:T(8,128)(2,1)}, u32[]{:S(2)}) copy-start(bf16[512,1024]{1,0:T(8,128)(2,1)} %gate.5) | copy-start | bytes 3145732
  43.0 4.8 %copy-start.5 = (bf16[512,1024]{1,0:T(8,128)(2,1)S(1)}, bf16[512,1024]{1,0:T(8,128)(2,1)}, u32[]{:S(2)}) copy-start(bf16[512,1024]{1,0:T(8,128)(2,1)} %dout.1) | copy-start | bytes 3145732
  43.0 5.8 %collective-permute-start.1 = (f32[4,128,128]{2,1,0:T(8,128)S(1)}, f32[4,128,128]{2,1,0:T(8,128)S(1)}, u32[]{:S(2)}, u32[]{:S(2)}) collective-permute-start(f32[4,128,128]{2,1,0:T(8,128)S(1)} %get-tuple-element.77), channel_id=1, source_target_pairs={{0,4},{4,0},{8,12},{12,8},{16,20},{20,16},{24,28},{28,24},{32,36},... | collective-permute-start | bytes 786440 | tf_op jit(solution)/shard_map/ppermute | solution.py:464
  46.7 1.1 %copy-start.6 = (f32[1024]{0:T(1024)S(1)}, f32[1024]{0:T(1024)}, u32[]{:S(2)}) copy-start(f32[1024]{0:T(1024)} %param.10) | copy-start | bytes 12292
  48.8 1.9 %copy-start.2 = (bf16[512,1024]{1,0:T(8,128)(2,1)S(1)}, bf16[512,1024]{1,0:T(8,128)(2,1)}, u32[]{:S(2)}) copy-start(bf16[512,1024]{1,0:T(8,128)(2,1)} %keys.11) | copy-start | bytes 3145732
  49.4 2.5 %collective-permute-start.2 = (f32[8,128]{1,0:T(8,128)S(1)}, f32[8,128]{1,0:T(8,128)S(1)}, u32[]{:S(2)}, u32[]{:S(2)}) collective-permute-start(f32[8,128]{1,0:T(8,128)S(1)} %get-tuple-element.83.one), channel_id=1, source_target_pairs={{0,1},{1,0},{2,3},{3,2},{4,5},{5,4},{6,7},{7,6},{8,9},{9,8},{10,11... | collective-permute-start | bytes 12296 | tf_op jit(solution)/shard_map/ppermute | solution.py:528
  52.0 3.7 %collective-permute-start.3 = (f32[8,128]{1,0:T(8,128)S(1)}, f32[8,128]{1,0:T(8,128)S(1)}, u32[]{:S(2)}, u32[]{:S(2)}) collective-permute-start(f32[8,128]{1,0:T(8,128)S(1)} %pair_sums.1.pair), channel_id=1, source_target_pairs={{0,3},{1,2},{2,1},{3,0},{4,7},{5,6},{6,5},{7,4},{8,11},{9,10},{10,... | collective-permute-start | bytes 12296 | tf_op jit(solution)/shard_map/ppermute | solution.py:533
  56.4 4.1 %collective-permute-start.4 = (f32[4,136,128]{2,1,0:T(8,128)S(1)}, f32[4,136,128]{2,1,0:T(8,128)S(1)}, u32[]{:S(2)}, u32[]{:S(2)}) collective-permute-start(f32[4,136,128]{2,1,0:T(8,128)S(1)} %get-tuple-element.113), channel_id=1, source_target_pairs={{0,4},{4,0},{8,12},{12,8},{16,20},{20,16},{24,28},{28,24},{32,36},... | collective-permute-start | bytes 835592 | tf_op jit(solution)/shard_map/ppermute | solution.py:422
  76.2 3.1 %collective-permute-start.5 = (f32[68,128]{1,0:T(8,128)S(1)}, f32[68,128]{1,0:T(8,128)S(1)}, u32[]{:S(2)}, u32[]{:S(2)}) collective-permute-start(f32[68,128]{1,0:T(8,128)S(1)} %row_total.1.one), channel_id=1, source_target_pairs={{0,64},{4,68},{8,72},{12,76},{16,80},{20,84},{24,88},{28,92},{32,9... | collective-permute-start | bytes 104456 | tf_op jit(solution)/shard_map/ppermute | solution.py:429
  79.4 4.1 %collective-permute-start.6 = (f32[68,128]{1,0:T(8,128)S(1)}, f32[68,128]{1,0:T(8,128)S(1)}, u32[]{:S(2)}, u32[]{:S(2)}) collective-permute-start(f32[68,128]{1,0:T(8,128)S(1)} %pair_total.1.pair), channel_id=1, source_target_pairs={{0,192},{4,196},{8,200},{12,204},{16,208},{20,212},{24,216},{28,22... | collective-permute-start | bytes 104456 | tf_op jit(solution)/shard_map/ppermute | solution.py:432
  95.4 5.0 %collective-permute-start.7 = (f32[4,136,128]{2,1,0:T(8,128)S(1)}, f32[4,136,128]{2,1,0:T(8,128)S(1)}, u32[]{:S(2)}, u32[]{:S(2)}) collective-permute-start(f32[4,136,128]{2,1,0:T(8,128)S(1)} %get-tuple-element.125), channel_id=1, source_target_pairs={{0,4},{4,0},{8,12},{12,8},{16,20},{20,16},{24,28},{28,24},{32,36},... | collective-permute-start | bytes 835592 | tf_op jit(solution)/shard_map/ppermute | solution.py:442

commit v7 on v6

--- a/solution.py
+++ b/solution.py
@@ -254,9 +254,8 @@
     return copy
 
 
-def query_kernel(core, keys, values, grad_own, grad_other, own, other, output_here,
-                 grad_query, left_own, left_other, right_own, right_other, output, done, sem):
-    copy = copy_out(output_here, output, sem)
+def query_kernel(core, keys, values, grad_own, grad_other, own, other,
+                 grad_query, left_own, left_other, right_own, right_other, done):
     for columns, here, _, index, (grads, states, left, right) in each_head(
         core, (grad_own, grad_other), (own, other), (left_own, left_other), (right_own, right_other)
     ):
@@ -273,7 +272,6 @@
         grad_query[:HALF, columns] = (first + inter[:HALF]).astype(BF16)
         grad_query[HALF:, columns] = (second + inter[HALF:]).astype(BF16)
     done[...] = jnp.zeros_like(done)
-    copy.wait()
 
 
 def key_kernel(core, queries, left_own, left_other, right_own, right_other, dgate_here, query_here,
@@ -297,6 +295,12 @@
         part_value[HALF:, here] = dot_nn(bottom[index], grad[HALF:, here])
     for mark in done:
         mark[...] = jnp.zeros_like(mark)
+
+
+def value_own_kernel(core, grad, top, bottom, output_here, part_value, output, done, sem):
+    copy = copy_out(output_here, output, sem)
+    value_kernel(core, grad, top, bottom, part_value, done)
+    copy.wait()
 
 
 def last_own_kernel(core, keys, values, part_key, part_value, states, grad_key, grad_value):
@@ -553,10 +557,8 @@
 
     def query_part():
         *results["query"], ended = call(
-            query_kernel, "grad_query", [wide, left, left, right, right, wide, done],
-            core, keys, values, grad_own, grad_other, own, other, output,
-            out_places=[vmem()] * 5 + [hbm(), vmem()],
-            scratch=one_copy,
+            query_kernel, "grad_query", [wide, left, left, right, right, done],
+            core, keys, values, grad_own, grad_other, own, other,
         )
         return ended
 
@@ -570,17 +572,18 @@
         return ended
 
     def value_part():
-        results["value"], ended = call(
-            value_kernel, "value_own", [half, done], core, grad_own, *turned[True][:2],
+        *results["value"], ended = call(
+            value_own_kernel, "value_own", [half, wide, done], core, grad_own, *turned[True][:2], output,
+            out_places=[vmem(), hbm(), vmem()],
+            scratch=one_copy,
         )
         return ended
 
     later_own, later_other = sums_beyond(
         core, column, mine, theirs, True, query_part, lambda: (key_part(), value_part()), (outputs_done,)
     )
-    output = results["query"][5]
     key_own, key_other, dgate, grad_query = results["key"]
-    value_own = results["value"]
+    value_own, output_out = results["value"]
     (value_other,) = call(value_kernel, "value_other", [half], core, grad_other, *turned[False][:2])
     key_before, value_before = call(
         last_own_kernel, "last_own", [half_low, half_low], core, keys, values, key_own, value_own, later_own,
@@ -595,7 +598,7 @@
             pltpu.SemaphoreType.DMA((2, OWNED)), pltpu.SemaphoreType.DMA((2,)), pltpu.SemaphoreType.DMA,
         ],
     )
-    return output, grad_query, grad_key, grad_value, dgate, dgain.reshape(WIDE)
+    return output_out, grad_query, grad_key, grad_value, dgate, dgain.reshape(WIDE)
 
 
 def solution(mesh):

time: 103 us -> 103 us (level)
  transfers between devices with their start and end apart: 8 -> 8, of which waited for: 4 -> 4; matrix products, arithmetic and copies ran while one was open for 0% -> 0% of each run, Pallas kernels for 12% -> 13%
where the time goes in v7:
time: 103 us; the launch traced here: 102 us
  blocking collectives  62.1 us (60%)
  starting transfers between devices  19 us (18%)
  Pallas kernels  16.9 us (16%)
  local copies, waits for them, and re-layouts  2.14 us (2%)
  between operations  1.04 us (1%)
    all_to_all x2, blocking collectives, exchange(): lax.all_to_all(pieces, 'seq', 0, 0, axis_index_groups=groups).reshape(flat)  34.7 us
    all_to_all x2, blocking collectives, exchange(): lax.all_to_all(pieces, 'seq', 0, 0, axis_index_groups=ROWS)  27.4 us
    pallas_call x29, Pallas kernels, call(): pl.pallas_call(kernel, in_specs=[smem()] + ins, out_specs=out_places, out...  16.9 us
    ppermute x1, starting transfers between devices, sums_beyond(): return (own, lax.ppermute(send, 'seq', CORES))  3.97 us
    ppermute x1, starting transfers between devices, sums_before(): return (own, lax.ppermute(send, 'seq', CORES))  3.69 us
    ppermute x1, starting transfers between devices, sums_before(): received = lax.ppermute(theirs, 'seq', CORES)  3.33 us
    ppermute x1, starting transfers between devices, sums_beyond(): received = lax.ppermute(theirs, 'seq', CORES)  2.73 us
    ppermute x1, starting transfers between devices, body(): lax.ppermute(pair, 'head', [(i, ring - 1 - i) for i in range(ring)])  2.48 us
  transfers between devices with their start and end apart: 8, of which 4 were waited for; matrix products, arithmetic and copies ran while one was open for 0% of the time, Pallas kernels for 13%

profile of v7, /device:TPU:1, one launch (start us, length us, event | category | flops | bytes accessed | tf_op | source)
XLA Modules:
  0.0 102.1 jit_solution(18333269846344192233)
XLA Ops:
  0.6 0.0 copy-start.1
  0.6 1.2 %copy-done.1 = bf16[512,1024]{1,0:T(8,128)(2,1)S(1)} copy-done((bf16[512,1024]{1,0:T(8,128)(2,1)S(1)}, bf16[512,1024]{1,0:T(8,128)(2,1)}, u32[]{:S(2)}) %copy-start.1) | copy-done | bytes 1048600
  1.9 0.3 turn_keys.1.turned_keys.turned
  2.2 0.9 copy-done.3
  3.1 0.5 states.1
  3.6 3.3 %collective-permute-start = (f32[4,128,128]{2,1,0:T(8,128)S(1)}, f32[4,128,128]{2,1,0:T(8,128)S(1)}, u32[]{:S(2)}, u32[]{:S(2)}) collective-permute-start(f32[4,128,128]{2,1,0:T(8,128)S(1)} %get-tuple-element.73), channel_id=1, source_target_pairs={{0,4},{4,0},{8,12},{12,8},{16,20},{20,16},{24,28},{28,24},{32,36},... | collective-permute-start | bytes 786440 | tf_op jit(solution)/shard_map/ppermute | solution.py:458
  6.9 0.0 copy-done
  6.9 1.1 %intra_own.1 = (f32[512,512]{1,0:T(8,128)S(1)}, f32[8,128]{1,0:T(8,128)S(1)}) custom-call(s32[1]{0:T(128)} %bitcast.core, bf16[512,1024]{1,0:T(8,128)(2,1)S(1)} %copy-done, bf16[8,128,512]{2,1,0:T(8,128)(2,1)S(1)} %turn_keys.1.turned_keys.turned, bf16[512,1024]{1,0:T(8,128)(2,1)S(1)} %copy-done.3), custom_call_target="tpu_custom_call" | custom-call | tf_op jit(solution)/shard_map/intra_own/pallas_call | solution.py:101
  8.0 0.1 collective-permute-done.received
  8.1 0.1 pack.2
  8.1 18.9 %all_to_all.20 = f32[32,1,2048]{2,1,0:T(1,128)S(1)} all-to-all(f32[32,1,2048]{2,1,0:T(1,128)S(1)} %bitcast.20), channel_id=1, replica_groups={{0,8,16,24,32,40,48,56,64,72,80,88,96,104,112,120,128,136,144,152,160,1..., dimensions={0} | all-to-all | bytes 524288 | tf_op jit(solution)/shard_map/all_to_all | solution.py:456
  27.1 15.8 %all_to_all.21 = f32[32,1,2048]{2,1,0:T(1,128)S(1)} all-to-all(f32[32,1,2048]{2,1,0:T(1,128)S(1)} %bitcast.17), channel_id=1, replica_groups={{0,8,16,24,32,40,48,56,64,72,80,88,96,104,112,120,128,136,144,152,160,1..., dimensions={0} | all-to-all | bytes 524288 | tf_op jit(solution)/shard_map/all_to_all | solution.py:456
  43.0 0.0 copy-start.4
  43.0 0.0 copy-start.5
  43.0 3.7 %collective-permute-start.1 = (f32[4,128,128]{2,1,0:T(8,128)S(1)}, f32[4,128,128]{2,1,0:T(8,128)S(1)}, u32[]{:S(2)}, u32[]{:S(2)}) collective-permute-start(f32[4,128,128]{2,1,0:T(8,128)S(1)} %get-tuple-element.77), channel_id=1, source_target_pairs={{0,4},{4,0},{8,12},{12,8},{16,20},{20,16},{24,28},{28,24},{32,36},... | collective-permute-start | bytes 786440 | tf_op jit(solution)/shard_map/ppermute | solution.py:468
  46.7 1.1 %intra_other.1.intra = f32[512,512]{1,0:T(8,128)S(1)} custom-call(s32[1]{0:T(128)} %bitcast.core, bf16[512,1024]{1,0:T(8,128)(2,1)S(1)} %copy-done, bf16[8,128,512]{2,1,0:T(8,128)(2,1)S(1)} %turn_keys.1.turned_keys.turned, bf16[512,1024]{1,0:T(8,128)(2,1)S(1)} %copy-done.3), custom_call_target="tpu_custom_call" | custom-call | tf_op jit(solution)/shard_map/intra_other/pallas_call | solution.py:101
  47.8 0.6 gates.1
  48.3 0.5 attend_own.1
  48.8 0.0 collective-permute-done.1.state.other
  48.8 0.0 copy-start.2
  48.8 0.6 attend_other.1
  49.4 1.3 %collective-permute-start.2 = (f32[8,128]{1,0:T(8,128)S(1)}, f32[8,128]{1,0:T(8,128)S(1)}, u32[]{:S(2)}, u32[]{:S(2)}) collective-permute-start(f32[8,128]{1,0:T(8,128)S(1)} %get-tuple-element.83.one), channel_id=1, source_target_pairs={{0,1},{1,0},{2,3},{3,2},{4,5},{5,4},{6,7},{7,6},{8,9},{9,8},{10,11... | collective-permute-start | bytes 12296 | tf_op jit(solution)/shard_map/ppermute | solution.py:532
  50.7 0.6 turned_own.1
  51.3 0.5 early_own.1
  51.8 0.2 collective-permute-done.2.other
  52.0 2.5 %collective-permute-start.3 = (f32[8,128]{1,0:T(8,128)S(1)}, f32[8,128]{1,0:T(8,128)S(1)}, u32[]{:S(2)}, u32[]{:S(2)}) collective-permute-start(f32[8,128]{1,0:T(8,128)S(1)} %pair_sums.1.pair), channel_id=1, source_target_pairs={{0,3},{1,2},{2,1},{3,0},{4,7},{5,6},{6,5},{7,4},{8,11},{9,10},{10,... | collective-permute-start | bytes 12296 | tf_op jit(solution)/shard_map/ppermute | solution.py:537
  54.4 0.6 turned_other.1
  55.0 0.5 early_other.1
  55.5 0.1 collective-permute-done.3.other_pair
  55.6 0.7 grads_theirs.1
  56.4 2.7 %collective-permute-start.4 = (f32[4,136,128]{2,1,0:T(8,128)S(1)}, f32[4,136,128]{2,1,0:T(8,128)S(1)}, u32[]{:S(2)}, u32[]{:S(2)}) collective-permute-start(f32[4,136,128]{2,1,0:T(8,128)S(1)} %get-tuple-element.115), channel_id=1, source_target_pairs={{0,4},{4,0},{8,12},{12,8},{16,20},{20,16},{24,28},{28,24},{32,36},... | collective-permute-start | bytes 835592 | tf_op jit(solution)/shard_map/ppermute | solution.py:426
  59.1 0.6 grads_mine.1
  59.7 0.7 outputs.1
  60.4 0.0 collective-permute-done.4.received
  60.5 15.5 %all_to_all.22 = f32[8,1,8704]{2,1,0:T(1,128)S(1)} all-to-all(f32[8,1,8704]{2,1,0:T(1,128)S(1)} %bitcast.18), channel_id=1, replica_groups={{0,8,16,24,32,40,48,56},{4,12,20,28,36,44,52,60},{64,72,80,88,96,104,11..., dimensions={0} | all-to-all | bytes 557056 | tf_op jit(solution)/shard_map/all_to_all | solution.py:424
  76.1 0.4 collective-permute-start.5
  76.5 2.5 %grad_query.1 = (bf16[512,1024]{1,0:T(8,128)(2,1)S(1)}, bf16[4,512,256]{2,1,0:T(8,128)(2,1)S(1)}, bf16[4,512,256]{2,1,0:T(8,128)(2,1)S(1)}, bf16[4,256,256]{2,1,...) custom-call(s32[1]{0:T(128)} %bitcast.core, bf16[512,1024]{1,0:T(8,128)(2,1)S(1)} %copy-done.2, ...), custom_call_target="tpu_custom_call" | custom-call | tf_op jit(solution)/shard_map/grad_query/pallas_call | solution.py:101
  79.1 0.0 collective-permute-done.5.other.neighbour
  79.1 1.1 %collective-permute-start.6 = (f32[68,128]{1,0:T(8,128)S(1)}, f32[68,128]{1,0:T(8,128)S(1)}, u32[]{:S(2)}, u32[]{:S(2)}) collective-permute-start(f32[68,128]{1,0:T(8,128)S(1)} %pair_total.1.pair), channel_id=1, source_target_pairs={{0,192},{4,196},{8,200},{12,204},{16,208},{20,212},{24,216},{28,22... | collective-permute-start | bytes 104456 | tf_op jit(solution)/shard_map/ppermute | solution.py:436
  80.2 1.0 value_own.1
  81.2 1.5 %grad_key.1 = (f32[512,512]{1,0:T(8,128)S(1)}, f32[512,512]{1,0:T(8,128)S(1)}, bf16[512,1024]{1,0:T(8,128)(2,1)}, bf16[512,1024]{1,0:T(8,128)(2,1)}, f32[8,128]{1,0:T(8,128)S(1)}) custom-call(s32[1]{0:T(128)} %bitcast.core, bf16[512,1024]{1,0:T(8,128)(2,1)S(1)} %copy-done, bf16[4,512,256]{2,1,0:T(8,128)(2,1)S(1)} %get-tuple-element.104.left_own, ...), custom_call_target="tpu_custom_call" | custom-call | tf_op jit(solution)/shard_map/grad_key/pallas_call | solution.py:101
  82.7 0.5 collective-permute-done.6.other_pair
  83.2 11.8 %all_to_all.23 = f32[8,1,8192]{2,1,0:T(1,128)S(1)} all-to-all(f32[8,1,8192]{2,1,0:T(1,128)S(1)} %bitcast.19), channel_id=1, replica_groups={{0,8,16,24,32,40,48,56},{4,12,20,28,36,44,52,60},{64,72,80,88,96,104,11..., dimensions={0} | all-to-all | bytes 524288 | tf_op jit(solution)/shard_map/all_to_all | solution.py:424
  95.1 4.0 %collective-permute-start.7 = (f32[4,136,128]{2,1,0:T(8,128)S(1)}, f32[4,136,128]{2,1,0:T(8,128)S(1)}, u32[]{:S(2)}, u32[]{:S(2)}) collective-permute-start(f32[4,136,128]{2,1,0:T(8,128)S(1)} %get-tuple-element.125), channel_id=1, source_target_pairs={{0,4},{4,0},{8,12},{12,8},{16,20},{20,16},{24,28},{28,24},{32,36},... | collective-permute-start | bytes 835592 | tf_op jit(solution)/shard_map/ppermute | solution.py:446
  99.0 0.6 value_other.1.part_value
  99.6 0.7 last_own.1
  100.3 0.0 collective-permute-done.7.other
  100.4 1.6 %last_other.1 = (bf16[512,1024]{1,0:T(8,128)(2,1)}, bf16[512,1024]{1,0:T(8,128)(2,1)}, f32[8,128]{1,0:T(8,128)}) custom-call(s32[1]{0:T(128)} %bitcast.core, bf16[512,1024]{1,0:T(8,128)(2,1)S(1)} %copy-done.2, bf16[512,1024]{1,0:T(8,128)(2,1)S(1)} %copy-done.3, f32[512,512]{1,0:T(8,128)S(1)} %get-tuple-element.111.part_key, ...), custom_call_target="tpu_custom_call" | custom-call | tf_op jit(solution)/shard_map/last_other/pallas_call | solution.py:101
  (15 shorter events, 0.2 us)
Async XLA Ops:
  0.6 1.2 %copy-start.1 = (bf16[512,1024]{1,0:T(8,128)(2,1)S(1)}, bf16[512,1024]{1,0:T(8,128)(2,1)}, u32[]{:S(2)}) copy-start(bf16[512,1024]{1,0:T(8,128)(2,1)} %keys.11) | copy-start | bytes 3145732
  1.9 1.2 %copy-start.3 = (bf16[512,1024]{1,0:T(8,128)(2,1)S(1)}, bf16[512,1024]{1,0:T(8,128)(2,1)}, u32[]{:S(2)}) copy-start(bf16[512,1024]{1,0:T(8,128)(2,1)} %values.11) | copy-start | bytes 3145732
  3.1 3.8 %copy-start = (bf16[512,1024]{1,0:T(8,128)(2,1)S(1)}, bf16[512,1024]{1,0:T(8,128)(2,1)}, u32[]{:S(2)}) copy-start(bf16[512,1024]{1,0:T(8,128)(2,1)} %queries.13) | copy-start | bytes 3145732
  3.6 4.5 %collective-permute-start = (f32[4,128,128]{2,1,0:T(8,128)S(1)}, f32[4,128,128]{2,1,0:T(8,128)S(1)}, u32[]{:S(2)}, u32[]{:S(2)}) collective-permute-start(f32[4,128,128]{2,1,0:T(8,128)S(1)} %get-tuple-element.73), channel_id=1, source_target_pairs={{0,4},{4,0},{8,12},{12,8},{16,20},{20,16},{24,28},{28,24},{32,36},... | collective-permute-start | bytes 786440 | tf_op jit(solution)/shard_map/ppermute | solution.py:458
  43.0 4.8 %copy-start.4 = (bf16[512,1024]{1,0:T(8,128)(2,1)S(1)}, bf16[512,1024]{1,0:T(8,128)(2,1)}, u32[]{:S(2)}) copy-start(bf16[512,1024]{1,0:T(8,128)(2,1)} %gate.5) | copy-start | bytes 3145732
  43.0 4.8 %copy-start.5 = (bf16[512,1024]{1,0:T(8,128)(2,1)S(1)}, bf16[512,1024]{1,0:T(8,128)(2,1)}, u32[]{:S(2)}) copy-start(bf16[512,1024]{1,0:T(8,128)(2,1)} %dout.1) | copy-start | bytes 3145732
  43.0 5.8 %collective-permute-start.1 = (f32[4,128,128]{2,1,0:T(8,128)S(1)}, f32[4,128,128]{2,1,0:T(8,128)S(1)}, u32[]{:S(2)}, u32[]{:S(2)}) collective-permute-start(f32[4,128,128]{2,1,0:T(8,128)S(1)} %get-tuple-element.77), channel_id=1, source_target_pairs={{0,4},{4,0},{8,12},{12,8},{16,20},{20,16},{24,28},{28,24},{32,36},... | collective-permute-start | bytes 786440 | tf_op jit(solution)/shard_map/ppermute | solution.py:468
  46.7 1.1 %copy-start.6 = (f32[1024]{0:T(1024)S(1)}, f32[1024]{0:T(1024)}, u32[]{:S(2)}) copy-start(f32[1024]{0:T(1024)} %param.10) | copy-start | bytes 12292
  48.8 1.9 %copy-start.2 = (bf16[512,1024]{1,0:T(8,128)(2,1)S(1)}, bf16[512,1024]{1,0:T(8,128)(2,1)}, u32[]{:S(2)}) copy-start(bf16[512,1024]{1,0:T(8,128)(2,1)} %keys.11) | copy-start | bytes 3145732
  49.4 2.5 %collective-permute-start.2 = (f32[8,128]{1,0:T(8,128)S(1)}, f32[8,128]{1,0:T(8,128)S(1)}, u32[]{:S(2)}, u32[]{:S(2)}) collective-permute-start(f32[8,128]{1,0:T(8,128)S(1)} %get-tuple-element.83.one), channel_id=1, source_target_pairs={{0,1},{1,0},{2,3},{3,2},{4,5},{5,4},{6,7},{7,6},{8,9},{9,8},{10,11... | collective-permute-start | bytes 12296 | tf_op jit(solution)/shard_map/ppermute | solution.py:532
  52.0 3.7 %collective-permute-start.3 = (f32[8,128]{1,0:T(8,128)S(1)}, f32[8,128]{1,0:T(8,128)S(1)}, u32[]{:S(2)}, u32[]{:S(2)}) collective-permute-start(f32[8,128]{1,0:T(8,128)S(1)} %pair_sums.1.pair), channel_id=1, source_target_pairs={{0,3},{1,2},{2,1},{3,0},{4,7},{5,6},{6,5},{7,4},{8,11},{9,10},{10,... | collective-permute-start | bytes 12296 | tf_op jit(solution)/shard_map/ppermute | solution.py:537
  56.4 4.1 %collective-permute-start.4 = (f32[4,136,128]{2,1,0:T(8,128)S(1)}, f32[4,136,128]{2,1,0:T(8,128)S(1)}, u32[]{:S(2)}, u32[]{:S(2)}) collective-permute-start(f32[4,136,128]{2,1,0:T(8,128)S(1)} %get-tuple-element.115), channel_id=1, source_target_pairs={{0,4},{4,0},{8,12},{12,8},{16,20},{20,16},{24,28},{28,24},{32,36},... | collective-permute-start | bytes 835592 | tf_op jit(solution)/shard_map/ppermute | solution.py:426
  76.1 3.0 %collective-permute-start.5 = (f32[68,128]{1,0:T(8,128)S(1)}, f32[68,128]{1,0:T(8,128)S(1)}, u32[]{:S(2)}, u32[]{:S(2)}) collective-permute-start(f32[68,128]{1,0:T(8,128)S(1)} %row_total.1.one), channel_id=1, source_target_pairs={{0,64},{4,68},{8,72},{12,76},{16,80},{20,84},{24,88},{28,92},{32,9... | collective-permute-start | bytes 104456 | tf_op jit(solution)/shard_map/ppermute | solution.py:433
  79.1 4.1 %collective-permute-start.6 = (f32[68,128]{1,0:T(8,128)S(1)}, f32[68,128]{1,0:T(8,128)S(1)}, u32[]{:S(2)}, u32[]{:S(2)}) collective-permute-start(f32[68,128]{1,0:T(8,128)S(1)} %pair_total.1.pair), channel_id=1, source_target_pairs={{0,192},{4,196},{8,200},{12,204},{16,208},{20,212},{24,216},{28,22... | collective-permute-start | bytes 104456 | tf_op jit(solution)/shard_map/ppermute | solution.py:436
  95.1 5.3 %collective-permute-start.7 = (f32[4,136,128]{2,1,0:T(8,128)S(1)}, f32[4,136,128]{2,1,0:T(8,128)S(1)}, u32[]{:S(2)}, u32[]{:S(2)}) collective-permute-start(f32[4,136,128]{2,1,0:T(8,128)S(1)} %get-tuple-element.125), channel_id=1, source_target_pairs={{0,4},{4,0},{8,12},{12,8},{16,20},{20,16},{24,28},{28,24},{32,36},... | collective-permute-start | bytes 835592 | tf_op jit(solution)/shard_map/ppermute | solution.py:446
